TPU v7x, 128 devices: a whole 4x4x4 slice. The times are simulated.
128 devices in a mesh: head: 8 (over y, x_hi), ctx: 16 (over z, x_lo, core).
Axes of the slice: x: 4 (x_hi: 2, x_lo: 2; x = x_hi * 2 + x_lo), y: 4, z: 4, core: 2. Of those that a mesh axis runs over, the one named last changes fastest.
Arguments:
- queries: bfloat16 [2048, 36864], P('ctx', 'head'), may hold values from -12 to 12
- latent_rows: bfloat16 [2048, 576], P('ctx'), may hold values from -4 to 4
- output_grad: bfloat16 [2048, 8192], P('ctx', 'head'), may hold values from -12 to 12
- up_query: bfloat16 [1536, 12288], P(None, 'head'), may hold values from -0.15625 to 0.15625
- up_key: bfloat16 [64, 128, 512], P('head'), may hold values from -0.5 to 0.5
- up_value: bfloat16 [64, 512, 128], P('head'), may hold values from -0.25 to 0.25
- block_order: int32 [32], replicated, may hold values from 0 to 31, each once
Outputs:
- compressed_grad: bfloat16 [2048, 1536], P('ctx', 'head')
- latent_grad: bfloat16 [2048, 576], P('ctx')
Inputs may be any that keep to these rules, and one draw needn't show every extreme that they name: `block_order`: every sequence block number appears exactly once.
All inputs are finite; a program needn't handle non-finite values.
Results may differ from a plain program's by a relative error of at most 0.025.
Values may be sent and summed in bfloat16 or wider, within the bound.
No kernel may reach another device: no remote copies, remote signals or barrier semaphores. Data moves between devices by JAX's collectives and lax.ppermute only.
A program may use at most 64 MiB of HBM per device.

v0:
```python
import jax
import jax.numpy as jnp
from jax import lax
from jax.sharding import PartitionSpec as P

D_LAT = 512
D_ROPE = 64
D_NOPE = 128
D_V = 128
BLOCK = 64


lowest_score = -1e30


def per_device(queries, latent_rows, output_grad, up_query, up_key, up_value, block_order):
    tok_rows = queries.shape[0]
    row_width = latent_rows.shape[1]
    heads_local = up_key.shape[0]
    ctx_size = lax.axis_size("ctx")
    rows_all = tok_rows * ctx_size
    softmax_scale = (D_NOPE + D_ROPE) ** (-0.5)
    half_rope = D_ROPE // 2
    first_row = lax.axis_index("ctx") * tok_rows
    local_rows = first_row + jnp.arange(tok_rows, dtype=jnp.int32)
    query_pos = block_order[local_rows // BLOCK] * BLOCK + local_rows % BLOCK
    last_query = jnp.max(query_pos)
    query_heads = queries.reshape(tok_rows, heads_local, row_width)
    grad_heads = output_grad.reshape(tok_rows, heads_local, D_V)
    value_grad = jnp.einsum(
        "thv,hlv->thl", grad_heads, up_value, preferred_element_type=jnp.float32
    ).astype(jnp.bfloat16)

    def key_positions(key_count):
        rows = jnp.arange(key_count, dtype=jnp.int32)
        return block_order[rows // BLOCK] * BLOCK + rows % BLOCK

    def block_scores(key_block):
        return (
            jnp.einsum("thw,kw->htk", query_heads, key_block, preferred_element_type=jnp.float32)
            * softmax_scale
        )

    def block_prob_grad(key_block):
        return jnp.einsum(
            "thl,kl->htk", value_grad, key_block[:, :D_LAT], preferred_element_type=jnp.float32
        )

    def make_grad_step(row_max, row_sum, row_delta):

        def grad_step(running, key_block, offset):
            key_count = key_block.shape[0]
            key_pos = key_positions(key_count)

            def grad_compute(current):
                visible = (key_pos[None, :] <= query_pos[:, None])[None]
                scores = block_scores(key_block)
                prob = (
                    jnp.where(visible, jnp.exp(scores - row_max[..., None]), 0.0)
                    / row_sum[..., None]
                )
                prob_grad = block_prob_grad(key_block)
                score_grad = (prob * (prob_grad - row_delta[..., None]) * softmax_scale).astype(
                    jnp.bfloat16
                )
                prob_low = prob.astype(jnp.bfloat16)
                query_acc = jnp.einsum(
                    "htk,kw->thw", score_grad, key_block, preferred_element_type=jnp.float32
                )
                block_grad = jnp.einsum(
                    "htk,thw->kw", score_grad, query_heads, preferred_element_type=jnp.float32
                )
                value_part = jnp.einsum(
                    "htk,thl->kl", prob_low, value_grad, preferred_element_type=jnp.float32
                )
                block_grad = block_grad + jnp.pad(value_part, ((0, 0), (0, D_ROPE)))
                return (query_acc, block_grad)

            return lax.cond(
                jnp.min(key_pos) <= last_query, grad_compute, lambda current: current, running
            )

        return grad_step

    stats_init = (
        jnp.full((heads_local, tok_rows), lowest_score, jnp.float32),
        jnp.zeros((heads_local, tok_rows), jnp.float32),
        jnp.zeros((heads_local, tok_rows), jnp.float32),
    )
    grad_init = (
        jnp.zeros((tok_rows, heads_local, row_width), jnp.float32),
        jnp.zeros((rows_all, row_width), jnp.float32),
    )
    key_block = lax.all_gather(latent_rows, "ctx", axis=0, tiled=True)
    key_pos = key_positions(key_block.shape[0])

    def stats_compute(current):
        row_max, row_sum, weighted = current
        visible = (key_pos[None, :] <= query_pos[:, None])[None]
        scores = block_scores(key_block)
        masked = jnp.where(visible, scores, lowest_score)
        new_max = jnp.maximum(row_max, jnp.max(masked, axis=2))
        exponent = jnp.where(visible, jnp.exp(scores - new_max[..., None]), 0.0)
        prob_grad = block_prob_grad(key_block)
        return (new_max, jnp.sum(exponent, axis=2), jnp.sum(exponent * prob_grad, axis=2))

    row_max, row_sum, weighted = lax.cond(
        jnp.min(key_pos) <= last_query, stats_compute, lambda current: current, stats_init
    )
    grad_step = make_grad_step(row_max, row_sum, weighted / row_sum)
    query_acc, key_buffer = grad_step(
        grad_init, lax.all_gather(latent_rows, "ctx", axis=0, tiled=True), jnp.int32(0)
    )
    query_back = query_acc.astype(jnp.bfloat16)
    nope_grad = jnp.einsum(
        "thl,hnl->thn", query_back[..., :D_LAT], up_key, preferred_element_type=jnp.float32
    )
    frequency = 10000.0 ** (-(2.0 * jnp.arange(half_rope, dtype=jnp.float32)) / D_ROPE)
    angles = query_pos.astype(jnp.float32)[:, None] * frequency[None, :]
    cosine_table = jnp.cos(angles)[:, None, :]
    sine_table = jnp.sin(angles)[:, None, :]
    rope_grad = query_back[..., D_LAT:].astype(jnp.float32)
    low_half = rope_grad[..., :half_rope]
    high_half = rope_grad[..., half_rope:]
    rope_back = jnp.concatenate(
        [
            low_half * cosine_table + high_half * sine_table,
            high_half * cosine_table - low_half * sine_table,
        ],
        axis=2,
    )
    full_grad = jnp.concatenate([nope_grad, rope_back], axis=2).astype(jnp.bfloat16)
    full_grad = full_grad.reshape(tok_rows, heads_local * (D_NOPE + D_ROPE))
    partial_value = lax.dot_general(
        full_grad, up_query, (((1,), (1,)), ((), ())), preferred_element_type=jnp.float32
    )
    compressed_grad = lax.psum_scatter(
        partial_value.astype(jnp.bfloat16), "head", scatter_dimension=1, tiled=True
    )
    owned_sum = lax.psum_scatter(
        key_buffer.astype(jnp.bfloat16), "ctx", scatter_dimension=0, tiled=True
    )
    latent_grad = lax.psum(owned_sum, "head")
    return (compressed_grad, latent_grad)


def solution(mesh):
    in_specs = (
        P("ctx", "head"),
        P("ctx", None),
        P("ctx", "head"),
        P(None, "head"),
        P("head", None, None),
        P("head", None, None),
        P(),
    )
    out_specs = (P("ctx", "head"), P("ctx", None))
    return jax.shard_map(
        per_device, mesh=mesh, in_specs=in_specs, out_specs=out_specs, check_vma=False
    )
```

profile of v0, /device:TPU:0, one launch (start us, length us, event | category | flops | bytes accessed | tf_op | source)
XLA Modules:
  0.0 313.5 jit_solution(5247029609861998133)
XLA Ops:
  7.2 1.8 copy.44
  9.1 1.8 copy.45
  10.9 1.6 gather_fusion
  12.5 0.7 reduce_max.18
  14.4 1.8 fusion.45
  16.2 2.1 fusion.44
  18.3 4.3 %compare_select_fusion.1 = s32[2048,1]{0,1:T(1,128)S(1)} fusion(s32[]{:T(128)} %bitcast.37, s32[]{:T(128)} %bitcast.38, s32[]{:T(128)} %bitcast.39, s32[]{:T(128)} %bitcast.40, s32[]{:T(128)} %bitcast.41, s32[]{:T(128)} %bitcast.43, s32[]{:T(128)} %bitcast.42), kind=kLoop, calls=%fused_computation.74 | loop fusion | flops 47104 | bytes 8220 | tf_op jit(solution)/shard_map/gather | solution.py:36
  22.6 16.1 %fusion.42 = (s32[]{:T(128)}, s32[2048]{0:T(1024)S(1)}) fusion(pred[2048]{0:T(1024)(128)(4,1)S(1)} %compare_reduce_fusion, pred[2048]{0:T(1024)(128)(4,1)S(1)} %compare_reduce_fusion.1, pred[2048]{0:T(1024)(128)(4,1)S(1)} %compare_reduce_fusion.2, pred[2048]{0:T(1024)(128)(4,1)S(1)} %compare_reduce_fusion.3, pred[2048]{0:T(1024)(128)(4,1)S(1)} %compare_reduce_fusion.4, ...), kind=kLoop, calls=%fused_computation.105 | loop fusion | flops 69631 | bytes 67688 | tf_op jit(solution)/shard_map/reduce_min | solution.py:80
  40.1 1.4 fusion.28
  41.5 5.8 %all-gather.2.cloned.1.call-done = bf16[2048,576]{1,0:T(8,128)(2,1)} async-done(((bf16[128,576]{1,0:T(8,128)(2,1)}), bf16[2048,576]{1,0:T(8,128)(2,1)}) %all-gather.2.cloned.1.call-update) | async-done | bytes 2359312 | tf_op jit(solution)/shard_map/all_gather | solution.py:112
  47.2 13.0 %conditional.2 = (f32[8,128]{1,0:T(8,128)}, f32[8,128]{1,0:T(8,128)S(1)}, f32[8,128]{1,0:T(8,128)S(1)}) conditional(s32[]{:T(128)} %convert_element_type.44, () %tuple.27, (s32[2048]{0:T(1024)S(1)}, s32[128]{0:T(128)S(1)}, bf16[2048,576]{1,0:T(8,128)(2,1)}, bf16[128,8,576]{0,2,1:T(8,128)(2,1)S(1)}, bf16[128,8,512]{0,2,1:T(8,128)(2,1)S(1)}) %tuple.82), branch_computations={%region_2.3_spmd, %region_3.7_spmd} | conditional | flops 4588828672 | bytes 42373684 | solution.py:107
  47.2 0.3 broadcast_compare_fusion
  47.6 5.7 %fusion.1 = (f32[8,128]{1,0:T(8,128)S(1)}, f32[2048,128,8]{1,0,2:T(8,128)S(1)}) fusion(pred[128,2048]{0,1:T(8,128)(4,1)S(1)} %broadcast_compare_fusion, bf16[128,8,576]{0,2,1:T(8,128)(2,1)S(1)} %get-tuple-element.48, bf16[2048,576]{1,0:T(8,128)(2,1)} %get-tuple-element.47), kind=kOutput, calls=%fused_computation.5 | convolution fusion | flops 2422209536 | bytes 12193792 | tf_op jit(solution)/shard_map/cond/branch_1_fun/thw,kw->htk/dot_general | solution.py:40
  53.3 0.6 broadcast_maximum_fusion
  53.9 3.9 %fusion = f32[8,128]{1,0:T(8,128)S(1)} fusion(f32[2048,128,8]{1,0,2:T(8,128)S(1)} %get-tuple-element.90, bf16[128,8,512]{0,2,1:T(8,128)(2,1)S(1)} %get-tuple-element.84, f32[8,128]{1,0:T(8,128)} %broadcast_maximum_fusion, pred[128,2048]{0,1:T(8,128)(4,1)S(1)} %broadcast_compare_fusion, bf16[2048,576]{1,0:T(8,128)(2,1)S(1)} %copy-done.3), kind=kOutput, calls=%fused_computation.2 | convolution fusion | flops 2157968384 | bytes 11804672 | tf_op jit(solution)/shard_map/cond/branch_1_fun/thl,kl->htk/dot_general | solution.py:45
  57.8 2.4 fusion.4
  60.2 18.9 %conditional.3 = (bf16[128,8,576]{0,2,1:T(8,128)(2,1)}, bf16[2048,576]{0,1:T(8,128)(2,1)S(1)}) conditional(s32[]{:T(128)} %convert_element_type.44, () %tuple.26, (s32[2048]{0:T(1024)S(1)}, s32[128]{0:T(128)S(1)}, bf16[2048,576]{1,0:T(8,128)(2,1)}, bf16[128,8,576]{0,2,1:T(8,128)(2,1)S(1)}, f32[8,128]{1,0:T(8,128)}, /*index=5*/f32[8,128]{1,0:T(8,128)S(1)}, ...), branch_computations={%region_7.8_spmd, %region_8.9_spmd} | conditional | flops 11564221440 | bytes 80380520 | solution.py:79
  60.4 0.3 broadcast_compare_fusion.1
  60.8 6.4 %fusion.14 = f32[8,128,2048]{1,2,0:T(8,128)S(1)} fusion(f32[8,128]{1,0:T(8,128)S(1)} %get-tuple-element.55, f32[8,128]{1,0:T(8,128)} %get-tuple-element.54, pred[128,2048]{0,1:T(8,128)(4,1)S(1)} %broadcast_compare_fusion.1, bf16[128,8,576]{0,2,1:T(8,128)(2,1)S(1)} %get-tuple-element.53, bf16[2048,576]{1,0:T(8,128)(2,1)} %get-tuple-element.52), kind=kOutput, calls=%fused_computation.22 | convolution fusion | flops 2424307712 | bytes 12197888 | tf_op jit(solution)/shard_map/cond/branch_1_fun/thw,kw->htk/dot_general | solution.py:40
  67.2 2.8 fusion.11
  70.1 2.4 fusion.17
  72.5 2.9 bitcast_add_fusion
  75.4 3.7 %fusion.25 = bf16[128,8,576]{0,2,1:T(8,128)(2,1)} fusion(bf16[8,128,2048]{1,2,0:T(8,128)(2,1)S(1)} %fusion.11, bf16[2048,576]{1,0:T(8,128)(2,1)S(1)} %copy-done.4), kind=kOutput, calls=%fused_computation.32 | convolution fusion | flops 2415919104 | bytes 7733248 | tf_op jit(solution)/shard_map/cond/branch_1_fun/htk,kw->thw/dot_general | solution.py:67
  79.1 2.6 copy.62
  82.3 1.7 copy.48
  84.5 1.7 fusion.29
  86.2 4.5 %convolution_convert_fusion = bf16[128,1536]{0,1:T(8,128)(2,1)} fusion(bf16[1536,1536]{1,0:T(8,128)(2,1)} %param.14, bf16[128,1536]{0,1:T(8,128)(2,1)S(1)} %bitcast.121), kind=kOutput, calls=%fused_computation.34 | convolution fusion | flops 604176384 | bytes 5505024 | tf_op jit(solution)/shard_map/dot_general | solution.py:134
  90.8 56.7 %reduce-scatter.7.cloned.1.call-done = bf16[128,576]{1,0:T(8,128)(2,1)} async-done(((bf16[2048,576]{1,0:T(8,128)(2,1)}), bf16[128,576]{1,0:T(8,128)(2,1)}) %reduce-scatter.7.cloned.1.call-update) | async-done | bytes 147472
  147.5 1.7 copy.63
  149.3 71.3 %reduce-scatter.5.cloned.1.call-done = bf16[128,192]{0,1:T(8,128)(2,1)} async-done(((bf16[128,1536]{0,1:T(8,128)(2,1)}), bf16[128,192]{0,1:T(8,128)(2,1)}) %reduce-scatter.5.cloned.1.call-update) | async-done | bytes 49168 | tf_op jit(solution)/shard_map/reduce_scatter | solution.py:137
  220.5 84.8 %all-reduce.3.cloned.1.call-done = bf16[128,576]{0,1:T(8,128)(2,1)} async-done(((bf16[128,576]{0,1:T(8,128)(2,1)}), bf16[128,576]{0,1:T(8,128)(2,1)}) %all-reduce.3.cloned.1.call-update) | async-done | bytes 147472 | tf_op jit(solution)/shard_map/psum | solution.py:143
  305.4 1.6 copy.80
  (54 shorter events, 2.5 us)
Async XLA Ops:
  7.2 32.9 %copy-start = (bf16[8,512,128]{2,1,0:T(8,128)(2,1)S(1)}, bf16[8,512,128]{2,1,0:T(8,128)(2,1)}, u32[]{:S(2)}) copy-start(bf16[8,512,128]{2,1,0:T(8,128)(2,1)} %param.16) | copy-start | bytes 3145732
  7.2 40.0 %all-gather.2.cloned.1.call-start = ((), (), s32[]{:S(2)}) async-start(), calls=%async_computation.2 | async-start | bytes 2785280 | tf_op jit(solution)/shard_map/all_gather | solution.py:112
  9.0 138.5 %reduce-scatter.7.cloned.1.call-start = ((), (), s32[]{:S(2)}) async-start(), calls=%async_computation.5 | async-start | bytes 2785280
  47.6 6.3 %copy-start.3 = (bf16[2048,576]{1,0:T(8,128)(2,1)S(1)}, bf16[2048,576]{1,0:T(8,128)(2,1)}, u32[]{:S(2)}) copy-start(bf16[2048,576]{1,0:T(8,128)(2,1)} %get-tuple-element.47) | copy-start | bytes 7077892 | tf_op jit(solution)/shard_map/cond
  60.4 6.8 %copy-start.1 = (bf16[128,8,576]{0,2,1:T(8,128)(2,1)}, bf16[128,8,576]{0,2,1:T(8,128)(2,1)S(1)}, u32[]{:S(2)}) copy-start(bf16[128,8,576]{0,2,1:T(8,128)(2,1)S(1)} %get-tuple-element.53) | copy-start | bytes 3538948 | tf_op jit(solution)/shard_map/cond
  60.8 6.4 %copy-start.4 = (bf16[2048,576]{1,0:T(8,128)(2,1)S(1)}, bf16[2048,576]{1,0:T(8,128)(2,1)}, u32[]{:S(2)}) copy-start(bf16[2048,576]{1,0:T(8,128)(2,1)} %get-tuple-element.52) | copy-start | bytes 7077892 | tf_op jit(solution)/shard_map/cond
  70.1 2.4 copy-start.2
  81.7 138.9 %reduce-scatter.5.cloned.1.call-start = ((), (), s32[]{:S(2)}) async-start(), calls=%async_computation.3 | async-start | bytes 442368 | tf_op jit(solution)/shard_map/reduce_scatter | solution.py:137
  90.8 214.6 %all-reduce.3.cloned.1.call-start = ((), (), s32[]{:S(2)}) async-start(), calls=%async_computation.4 | async-start | bytes 294912 | tf_op jit(solution)/shard_map/psum | solution.py:143
Sparse Core Ops, SparseCore 0:
  9.7 37.4 all-gather.1
  81.8 65.6 reduce-scatter.6
  151.7 68.8 reduce-scatter.4
  223.4 81.8 all-reduce.2
where the time goes:
time: 314 us; the launch traced here: 313 us
  waiting for transfers between devices  219 us (70%)
  matrix products  35.4 us (11%)
  other arithmetic  26.6 us (8%)
  local copies, waits for them, and re-layouts  16.9 us (5%)
  between operations  15.3 us (5%)
    psum x1, waiting for transfers between devices, per_device(): latent_grad = lax.psum(owned_sum, 'head')  84.8 us
    reduce_scatter x1, waiting for transfers between devices, per_device(): lax.psum_scatter(partial_value.astype(jnp.bfloat16), 'head', scatter_dime...  71.3 us
    unnamed x5, waiting for transfers between devices  56.8 us
    reduce_min x1, other arithmetic, grad_step(): jnp.min(key_pos) <= last_query  16.1 us
    dot_general x2, matrix products, block_scores(): jnp.einsum('thw,kw->htk', query_heads, key_block, preferred_element_type=...  12.1 us
    unnamed x7, local copies, waits for them, and re-layouts  9.4 us
    dot_general x2, matrix products, block_prob_grad(): jnp.einsum('thl,kl->htk', value_grad, key_block[:, :D_LAT], preferred_ele...  6.78 us
  transfers between devices with their start and end apart: 4, of which 4 were waited for; matrix products, arithmetic and copies ran while one was open for 13% of the time, Pallas kernels for 0%

commit v1 on v0

v1 whole, which is shorter than its diff:
```python
import functools

import jax
import jax.numpy as jnp
from jax import lax
from jax.experimental import pallas as pl
from jax.experimental.pallas import tpu as pltpu
from jax.sharding import Mesh
from jax.sharding import PartitionSpec as P

D_LAT = 512
D_ROPE = 64
D_NOPE = 128
D_V = 128
BLOCK = 64
ROW = D_LAT + D_ROPE
HALF = D_ROPE // 2
N_Y, N_XH, N_Z, N_XL = 4, 2, 4, 2
TOK = 128
HEADS_L = 8
SHARDS = N_Z * N_XL
KEYS = SHARDS * TOK
ROWS = 2 * HEADS_L * TOK
HROWS = HEADS_L * TOK
F_ROWS = HEADS_L * (D_NOPE + D_ROPE)
C_COLS = 192
SCALE = (D_NOPE + D_ROPE) ** -0.5
LOG2E = 1.4426950408889634
MASKED = -1e30
AXES = ("y", "xh", "z", "xl", "core")
VMEM_LIMIT = 56 * 1024 * 1024
TN = 256

SHIFTS = ((0, 1, 0), (0, 3, 0), (0, 0, 1), (0, 2, 0), (1, 1, 1), (0, 3, 1), (1, 2, 1))

NT = (((1,), (1,)), ((), ()))
NN = (((1,), (0,)), ((), ()))
bf16 = jnp.bfloat16
f32 = jnp.float32


def dot(a, b, dims=NN):
    return lax.dot_general(a, b, dims, preferred_element_type=f32)


def shift(x, dy=0, dxh=0, dz=0, dxl=0, dcore=0):
    pairs = []
    dims = (N_Y, N_XH, N_Z, N_XL, 2)
    deltas = (dy, dxh, dz, dxl, dcore)
    for source in range(N_Y * N_XH * N_Z * N_XL * 2):
        rest, coords = source, []
        for n in reversed(dims):
            coords.append(rest % n)
            rest //= n
        coords.reverse()
        target = 0
        for n, c, d in zip(dims, coords, deltas):
            target = target * n + (c + d) % n
        pairs.append((source, target))
    return lax.ppermute(x, AXES, pairs)


def params(**kw):
    return pltpu.CompilerParams(vmem_limit_bytes=VMEM_LIMIT, **kw)


def vmem():
    return pl.BlockSpec(memory_space=pltpu.VMEM)


def smem():
    return pl.BlockSpec(memory_space=pltpu.SMEM)


def prologue_kernel(q0, q1, do0, do1, uv, qt, gt):
    for s, (q, do) in enumerate(((q0, do0), (q1, do1))):
        for j in range(HEADS_L * ROW // 128):
            t = q[:, j * 128 : (j + 1) * 128].T
            for k in range(2):
                r = j * 128 + k * 64
                h, d = r // ROW, r % ROW
                col = (s * HEADS_L + h) * TOK
                qt[d : d + 64, col : col + TOK] = t[k * 64 : (k + 1) * 64, :]
        for h in range(HEADS_L):
            col = (s * HEADS_L + h) * TOK
            g = dot(uv[h], do[:, h * D_V : (h + 1) * D_V], NT)
            gt[:, col : col + TOK] = g.astype(bf16)


def prologue(q0, q1, do0, do1, uv):
    return pl.pallas_call(
        prologue_kernel,
        out_shape=(
            jax.ShapeDtypeStruct((ROW, ROWS), bf16),
            jax.ShapeDtypeStruct((D_LAT, ROWS), bf16),
        ),
        in_specs=[vmem()] * 5,
        out_specs=(vmem(), vmem()),
        compiler_params=params(),
        cost_estimate=pl.CostEstimate(
            flops=2 * ROWS * D_V * D_LAT, bytes_accessed=9 * 1024 * 1024, transcendentals=0
        ),
        name="prologue",
    )(q0, q1, do0, do1, uv)


def scores_kernel(kblk, qblk, *refs):
    kts = refs[:SHARDS]
    qt, gt, e_out, dp_out, m_out, merged, k_nat, bias = refs[SHARDS:]

    @pl.when(pl.program_id(0) == 0)
    def _():
        for s in range(SHARDS):
            for j in range(4):
                k_nat[s * TOK : (s + 1) * TOK, j * 128 : (j + 1) * 128] = kts[s][
                    j * 128 : (j + 1) * 128, :
                ].T
            k_nat[s * TOK : (s + 1) * TOK, D_LAT:ROW] = kts[s][D_LAT:ROW, :].T
        lane = lax.broadcasted_iota(jnp.int32, (BLOCK, TOK), 1)
        sub = lax.broadcasted_iota(jnp.int32, (BLOCK, TOK), 0)
        for t in range(2):
            q_pos = jnp.where(
                lane < BLOCK, qblk[2 * t] * BLOCK + lane, qblk[2 * t + 1] * BLOCK + lane - BLOCK
            )
            for b in range(2 * SHARDS):
                k_pos = kblk[b] * BLOCK + sub
                bias[t, b * BLOCK : (b + 1) * BLOCK, :] = jnp.where(k_pos <= q_pos, 0.0, MASKED)

    token_set = pl.program_id(0) // (HROWS // TN)
    k_scale = SCALE * LOG2E
    ms, ls, ws = [], [], []
    for s in range(SHARDS):
        rows = slice(s * TOK, (s + 1) * TOK)
        sc = dot(k_nat[rows, :], qt[...])
        dp = dot(k_nat[rows, :D_LAT], gt[...])
        b = bias[token_set, rows, :]
        for j in range(TN // TOK):
            cols = slice(j * TOK, (j + 1) * TOK)
            x = sc[:, cols] * k_scale + b
            m = jnp.max(x, axis=0, keepdims=True)
            e = jnp.exp2(x - m)
            d = dp[:, cols]
            l = jnp.sum(e, axis=0, keepdims=True)
            w = jnp.sum(e * d, axis=0, keepdims=True)
            e_out[rows, cols] = e.astype(bf16)
            dp_out[rows, cols] = d.astype(bf16)
            m_out[s : s + 1, cols] = m
            ms.append(m)
            ls.append(l)
            ws.append(w)
    n = TN // TOK
    for j in range(n):
        cols = slice(j * TOK, (j + 1) * TOK)
        mj, lj, wj = ms[j::n], ls[j::n], ws[j::n]
        top = functools.reduce(jnp.maximum, mj)
        f = [jnp.exp2(m - top) for m in mj]
        merged[0:1, cols] = top
        merged[1:2, cols] = sum(a * b for a, b in zip(f, lj))
        merged[2:3, cols] = sum(a * b for a, b in zip(f, wj))


def scores(kblk, qblk, kts, qt, gt):
    return pl.pallas_call(
        scores_kernel,
        grid=(ROWS // TN,),
        out_shape=(
            jax.ShapeDtypeStruct((KEYS, ROWS), bf16),
            jax.ShapeDtypeStruct((KEYS, ROWS), bf16),
            jax.ShapeDtypeStruct((SHARDS, ROWS), f32),
            jax.ShapeDtypeStruct((8, ROWS), f32),
        ),
        in_specs=[smem(), smem()]
        + [pl.BlockSpec((ROW, TOK), lambda i: (0, 0))] * SHARDS
        + [pl.BlockSpec((ROW, TN), lambda i: (0, i)), pl.BlockSpec((D_LAT, TN), lambda i: (0, i))],
        out_specs=(
            pl.BlockSpec((KEYS, TN), lambda i: (0, i)),
            pl.BlockSpec((KEYS, TN), lambda i: (0, i)),
            pl.BlockSpec((SHARDS, TN), lambda i: (0, i)),
            pl.BlockSpec((8, TN), lambda i: (0, i)),
        ),
        scratch_shapes=[pltpu.VMEM((KEYS, ROW), bf16), pltpu.VMEM((2, KEYS, TOK), f32)],
        compiler_params=params(),
        cost_estimate=pl.CostEstimate(
            flops=2 * ROWS * KEYS * (ROW + D_LAT),
            bytes_accessed=14 * 1024 * 1024,
            transcendentals=ROWS * KEYS,
        ),
        name="scores",
    )(kblk, qblk, *kts, qt, gt)


def grads_kernel(e, dp, m, mine, theirs, qt, gt, *refs):
    outs = refs[:2]
    ds_out, r_s, rc_s, delta_s, p_s = refs[2:]

    @pl.when(pl.program_id(0) == 0)
    def _():
        for j in range(2):
            a = slice(j * HROWS, (j + 1) * HROWS)
            b = slice((1 - j) * HROWS, (2 - j) * HROWS)
            m0, m1 = mine[0:1, a], theirs[0:1, b]
            top = jnp.maximum(m0, m1)
            f0, f1 = jnp.exp2(m0 - top), jnp.exp2(m1 - top)
            inv = 1.0 / (f0 * mine[1:2, a] + f1 * theirs[1:2, b])
            delta_s[0:1, a] = (f0 * mine[2:3, a] + f1 * theirs[2:3, b]) * inv
            r = jnp.exp2(m[:, a] - top) * inv
            r_s[:, a] = r
            rc_s[:, a] = r * SCALE

    step = pl.program_id(0)
    for k in range(2):
        rows = slice(k * TOK, (k + 1) * TOK)
        for j in range(ROWS // TN):
            cols = slice(j * TN, (j + 1) * TN)
            ef = e[rows, cols].astype(f32)
            r = r_s[pl.ds(step * 2 + k, 1), cols]
            rc = rc_s[pl.ds(step * 2 + k, 1), cols]
            p_s[rows, cols] = (ef * r).astype(bf16)
            ds_out[rows, cols] = (
                ef * rc * (dp[rows, cols].astype(f32) - delta_s[0:1, cols])
            ).astype(bf16)
    dk = dot(qt[...], ds_out[...], NT)
    dv = dot(gt[...], p_s[...], NT)
    for k in range(2):
        cols = slice(k * TOK, (k + 1) * TOK)
        outs[k][0, :D_LAT, :] = (dk[:D_LAT, cols] + dv[:, cols]).astype(bf16)
        outs[k][0, D_LAT:, :] = dk[D_LAT:, cols].astype(bf16)


def grads(e, dp, m, mine, theirs, qt, gt):
    full = lambda shape: pl.BlockSpec(shape, lambda i: (0,) * len(shape))
    steps = SHARDS // 2
    return pl.pallas_call(
        grads_kernel,
        grid=(steps,),
        out_shape=(
            jax.ShapeDtypeStruct((steps, ROW, TOK), bf16),
            jax.ShapeDtypeStruct((steps, ROW, TOK), bf16),
            jax.ShapeDtypeStruct((KEYS, ROWS), bf16),
        ),
        in_specs=[
            pl.BlockSpec((2 * TOK, ROWS), lambda i: (i, 0)),
            pl.BlockSpec((2 * TOK, ROWS), lambda i: (i, 0)),
            full((SHARDS, ROWS)),
            full((8, ROWS)),
            full((8, ROWS)),
            full((ROW, ROWS)),
            full((D_LAT, ROWS)),
        ],
        out_specs=(
            pl.BlockSpec((1, ROW, TOK), lambda i: (i, 0, 0)),
            pl.BlockSpec((1, ROW, TOK), lambda i: (i, 0, 0)),
            pl.BlockSpec((2 * TOK, ROWS), lambda i: (i, 0)),
        ),
        scratch_shapes=[
            pltpu.VMEM((SHARDS, ROWS), f32),
            pltpu.VMEM((SHARDS, ROWS), f32),
            pltpu.VMEM((8, ROWS), f32),
            pltpu.VMEM((2 * TOK, ROWS), bf16),
        ],
        compiler_params=params(),
        cost_estimate=pl.CostEstimate(
            flops=2 * ROWS * KEYS * (ROW + D_LAT),
            bytes_accessed=18 * 1024 * 1024,
            transcendentals=0,
        ),
        name="grads",
    )(e, dp, m, mine, theirs, qt, gt)


def query_kernel(*refs):
    kts = refs[:SHARDS]
    ds, out, kt = refs[SHARDS:]

    @pl.when(pl.program_id(0) == 0)
    def _():
        for s in range(SHARDS):
            kt[:, s * TOK : (s + 1) * TOK] = kts[s][...]

    out[...] = dot(kt[...], ds[...]).astype(bf16)


def query_grad(kts, ds, token_set):
    steps = HROWS // TN
    return pl.pallas_call(
        query_kernel,
        grid=(steps,),
        out_shape=jax.ShapeDtypeStruct((ROW, HROWS), bf16),
        in_specs=[pl.BlockSpec((ROW, TOK), lambda i: (0, 0))] * SHARDS
        + [pl.BlockSpec((KEYS, TN), lambda i: (0, i + token_set * steps))],
        out_specs=pl.BlockSpec((ROW, TN), lambda i: (0, i)),
        scratch_shapes=[pltpu.VMEM((ROW, KEYS), bf16)],
        compiler_params=params(),
        cost_estimate=pl.CostEstimate(
            flops=2 * HROWS * KEYS * ROW, bytes_accessed=4 * 1024 * 1024, transcendentals=0
        ),
        name="query_grad",
    )(*kts, ds)


def project_kernel(place, own, got, cos, sin, uk, uq_hbm, send, keep, uq, ft, cg, sem):
    copy = pltpu.make_async_copy(uq_hbm, uq, sem)
    copy.start()
    for h in range(HEADS_L):
        cols = slice(h * TOK, (h + 1) * TOK)
        d = (own[:, cols].astype(f32) + got[:, cols].astype(f32)).astype(bf16)
        base = h * (D_NOPE + D_ROPE)
        ft[base : base + D_NOPE, :] = dot(uk[h], d[:D_LAT]).astype(bf16)
        a = d[D_LAT : D_LAT + HALF].astype(f32)
        b = d[D_LAT + HALF :].astype(f32)
        base += D_NOPE
        ft[base : base + HALF, :] = (a * cos[...] + b * sin[...]).astype(bf16)
        ft[base + HALF : base + D_ROPE, :] = (b * cos[...] - a * sin[...]).astype(bf16)
    copy.wait()
    cg[...] = dot(uq[...], ft[...]).astype(bf16)
    y, xh = place[0], place[1]
    for d in range(N_Y):
        yd = lax.rem(y + d, N_Y)
        send[d] = cg[pl.ds(pl.multiple_of((yd * 2 + 1 - xh) * C_COLS, 64), C_COLS), :]
        keep[d] = cg[pl.ds(pl.multiple_of((yd * 2 + xh) * C_COLS, 64), C_COLS), :]


def project(place, own, got, cos, sin, uk, uq):
    q_rank = uq.shape[0]
    return pl.pallas_call(
        project_kernel,
        out_shape=(
            jax.ShapeDtypeStruct((N_Y, C_COLS, TOK), bf16),
            jax.ShapeDtypeStruct((N_Y, C_COLS, TOK), bf16),
        ),
        in_specs=[smem()] + [vmem()] * 5 + [pl.BlockSpec(memory_space=pl.ANY)],
        out_specs=(vmem(), vmem()),
        scratch_shapes=[
            pltpu.VMEM((q_rank, F_ROWS), bf16),
            pltpu.VMEM((F_ROWS, TOK), bf16),
            pltpu.VMEM((q_rank, TOK), bf16),
            pltpu.SemaphoreType.DMA,
        ],
        compiler_params=params(),
        cost_estimate=pl.CostEstimate(
            flops=2 * TOK * F_ROWS * q_rank + 2 * HROWS * D_LAT * D_NOPE,
            bytes_accessed=9 * 1024 * 1024,
            transcendentals=0,
        ),
        name="project",
    )(place, own, got, cos, sin, uk, uq)


def per_device(queries, latent_rows, output_grad, up_query, up_key, up_value, block_order):
    y, xh = lax.axis_index("y"), lax.axis_index("xh")
    z, xl, core = lax.axis_index("z"), lax.axis_index("xl"), lax.axis_index("core")

    def place(z, xl, c):
        return (z * N_XL + xl) * 2 + c

    own_kt = latent_rows.T
    q_other = shift(queries, dcore=1)
    do_other = shift(output_grad, dcore=1)
    kts = [own_kt] + [shift(own_kt, dxh=a, dz=b, dxl=c) for a, b, c in SHIFTS]
    owners = [place(z, xl, core)] + [
        place((z - b) % N_Z, (xl - c) % N_XL, core) for _, b, c in SHIFTS
    ]
    order2 = block_order.reshape(-1, 2)
    kblk = order2[jnp.stack(owners)].reshape(-1)
    qblk = order2[jnp.stack([place(z, xl, core), place(z, xl, 1 - core)])].reshape(-1)
    token = jnp.arange(TOK, dtype=jnp.int32)
    pos = jnp.where(token < BLOCK, qblk[0] * BLOCK + token, qblk[1] * BLOCK + token - BLOCK)
    frequency = 10000.0 ** (-(2.0 * jnp.arange(HALF, dtype=f32)) / D_ROPE)
    angles = pos.astype(f32)[None, :] * frequency[:, None]
    cos, sin = jnp.cos(angles), jnp.sin(angles)

    qt, gt = prologue(queries, q_other, output_grad, do_other, up_value)
    e, dp, m, mine = scores(kblk, qblk, kts, qt, gt)
    theirs = shift(mine, dcore=1)
    dk_even, dk_odd, ds = grads(e, dp, m, mine, theirs, qt, gt)

    total = dk_even[0].astype(f32)
    for i, (a, b, c) in enumerate(SHIFTS, 1):
        part = (dk_even, dk_odd)[i % 2][i // 2]
        total = total + shift(part, dxh=-a, dz=-b, dxl=-c).astype(f32)
    total = total.astype(bf16)

    dq_other = shift(query_grad(kts, ds, 1), dcore=1)
    dq_own = query_grad(kts, ds, 0)
    send, keep = project(jnp.stack([y, xh]), dq_own, dq_other, cos, sin, up_key, up_query)
    cg = (keep.astype(f32) + shift(send, dxh=1).astype(f32)).astype(bf16)
    part = [cg[0]] + [shift(cg[d], dy=d) for d in range(1, N_Y)]
    cg = sum(p.astype(f32) for p in part).astype(bf16)

    total = (total.astype(f32) + shift(total, dxh=1).astype(f32)).astype(bf16)
    s1, s2, s3 = (shift(total, dy=d).astype(f32) for d in range(1, N_Y))
    total = ((total.astype(f32) + s2) + (s1 + s3)).astype(bf16)
    return cg.T, total.T


def solution(mesh):
    fine = Mesh(mesh.devices.reshape(N_Y, N_XH, N_Z, N_XL, 2), AXES)
    head, ctx = ("y", "xh"), ("z", "xl", "core")
    in_specs = (
        P(ctx, head),
        P(ctx, None),
        P(ctx, head),
        P(None, head),
        P(head, None, None),
        P(head, None, None),
        P(),
    )
    out_specs = (P(ctx, head), P(ctx, None))
    return jax.shard_map(
        per_device, mesh=fine, in_specs=in_specs, out_specs=out_specs, check_vma=False
    )
```

time: 314 us -> 116 us (0.37)
  waiting for transfers between devices: 219 us -> 13.4 us
  starting transfers between devices: 0.38 us -> 45.7 us
  Pallas kernels: 0 us -> 44.7 us
  matrix products: 35.4 us -> 0 us
  other arithmetic: 26.6 us -> 4.06 us
  between operations: 15.3 us -> 2.18 us
  local copies, waits for them, and re-layouts: 16.9 us -> 5.82 us
    psum x1 -> x0, waiting for transfers between devices: 84.8 us -> none  [per_device(): latent_grad = lax.psum(owned_sum, 'head')]
    reduce_scatter x1 -> x0, waiting for transfers between devices: 71.3 us -> none  [per_device(): lax.psum_scatter(partial_value.astype(jnp.bfloat16), 'head', scatter_dime...]
    unnamed x5 -> x0, waiting for transfers between devices: 56.8 us -> none
    ppermute x0 -> x26, starting transfers between devices: none -> 45.7 us  [shift(): return lax.ppermute(x, AXES, pairs)]
    pallas_call x0 -> x6, Pallas kernels: none -> 44.7 us  [the longest x1 11.9 us: scores(): pl.pallas_call(scores_kernel, grid=(ROWS // TN,), out_shape=(jax.ShapeDty...]
    dot_general x10 -> x0, matrix products: 35.4 us -> none  [the longest x2 12.1 us: block_scores(): jnp.einsum('thw,kw->htk', query_heads, key_block, preferred_element_type=...]
    reduce_min x1 -> x0, other arithmetic: 16.1 us -> none  [grad_step(): jnp.min(key_pos) <= last_query]
    ppermute x0 -> x26, waiting for transfers between devices: none -> 13.4 us  [shift(): return lax.ppermute(x, AXES, pairs)]
  transfers between devices with their start and end apart: 4 -> 26, of which waited for: 4 -> 7; matrix products, arithmetic and copies ran while one was open for 13% -> 6% of each run, Pallas kernels for 0% -> 15%
where the time goes in v1:
time: 116 us
  starting transfers between devices  45.7 us (39%)
  Pallas kernels  44.7 us (39%)
  waiting for transfers between devices  13.4 us (12%)
  local copies, waits for them, and re-layouts  5.82 us (5%)
  other arithmetic  4.06 us (3%)
  between operations  2.18 us (2%)
    ppermute x26, starting transfers between devices, shift(): return lax.ppermute(x, AXES, pairs)  45.7 us
    ppermute x26, waiting for transfers between devices, shift(): return lax.ppermute(x, AXES, pairs)  13.4 us
    pallas_call x1, Pallas kernels, scores(): pl.pallas_call(scores_kernel, grid=(ROWS // TN,), out_shape=(jax.ShapeDty...  11.9 us
    pallas_call x2, Pallas kernels, query_grad(): pl.pallas_call(query_kernel, grid=(steps,), out_shape=jax.ShapeDtypeStruc...  10.6 us
    pallas_call x1, Pallas kernels, grads(): pl.pallas_call(grads_kernel, grid=(steps,), out_shape=(jax.ShapeDtypeStru...  10.6 us
    pallas_call x1, Pallas kernels, project(): pl.pallas_call(project_kernel, out_shape=(jax.ShapeDtypeStruct((N_Y, C_CO...  6.51 us
    pallas_call x1, Pallas kernels, prologue(): pl.pallas_call(prologue_kernel, out_shape=(jax.ShapeDtypeStruct((ROW, ROW...  5.1 us
    unnamed x28, local copies, waits for them, and re-layouts  2.46 us
  transfers between devices with their start and end apart: 26, of which 7 were waited for; matrix products, arithmetic and copies ran while one was open for 6% of the time, Pallas kernels for 15%

profile of v1, /device:TPU:0, one launch (start us, length us, event | category | flops | bytes accessed | tf_op | source)
XLA Modules:
  0.0 115.8 jit_solution(7388059183034709557)
XLA Ops:
  0.7 2.1 %collective-permute-start = (bf16[576,128]{1,0:T(8,128)(2,1)}, bf16[576,128]{1,0:T(8,128)(2,1)S(1)}, u32[]{:S(2)}, u32[]{:S(2)}) collective-permute-start(bf16[576,128]{1,0:T(8,128)(2,1)} %bitcast.50), channel_id=1, source_target_pairs={{0,4},{1,5},{2,6},{3,7},{4,8},{5,9},{6,10},{7,11},{8,12},{9,13},{1... | collective-permute-start | bytes 442376 | tf_op jit(solution)/shard_map/ppermute | solution.py:60
  2.8 2.2 %collective-permute-start.1 = (bf16[576,128]{1,0:T(8,128)(2,1)}, bf16[576,128]{1,0:T(8,128)(2,1)S(1)}, u32[]{:S(2)}, u32[]{:S(2)}) collective-permute-start(bf16[576,128]{1,0:T(8,128)(2,1)} %bitcast.51), channel_id=1, source_target_pairs={{0,12},{1,13},{2,14},{3,15},{4,0},{5,1},{6,2},{7,3},{8,4},{9,5},{1... | collective-permute-start | bytes 442376 | tf_op jit(solution)/shard_map/ppermute | solution.py:60
  5.0 1.5 %collective-permute-start.2 = (bf16[576,128]{1,0:T(8,128)(2,1)}, bf16[576,128]{1,0:T(8,128)(2,1)S(1)}, u32[]{:S(2)}, u32[]{:S(2)}) collective-permute-start(bf16[576,128]{1,0:T(8,128)(2,1)} %bitcast.52), channel_id=1, source_target_pairs={{0,2},{1,3},{2,0},{3,1},{4,6},{5,7},{6,4},{7,5},{8,10},{9,11},{10,... | collective-permute-start | bytes 442376 | tf_op jit(solution)/shard_map/ppermute | solution.py:60
  8.7 0.8 collective-permute-done.refs_1_
  9.6 1.6 %collective-permute-start.3 = (bf16[576,128]{1,0:T(8,128)(2,1)}, bf16[576,128]{1,0:T(8,128)(2,1)S(1)}, u32[]{:S(2)}, u32[]{:S(2)}) collective-permute-start(bf16[576,128]{1,0:T(8,128)(2,1)} %bitcast.53), channel_id=1, source_target_pairs={{0,8},{1,9},{2,10},{3,11},{4,12},{5,13},{6,14},{7,15},{8,0},{9,1},... | collective-permute-start | bytes 442376 | tf_op jit(solution)/shard_map/ppermute | solution.py:60
  11.2 3.2 %collective-permute-start.4 = (bf16[576,128]{1,0:T(8,128)(2,1)}, bf16[576,128]{1,0:T(8,128)(2,1)S(1)}, u32[]{:S(2)}, u32[]{:S(2)}) collective-permute-start(bf16[576,128]{1,0:T(8,128)(2,1)} %bitcast.54), channel_id=1, source_target_pairs={{0,22},{1,23},{2,20},{3,21},{4,26},{5,27},{6,24},{7,25},{8,30},{9,... | collective-permute-start | bytes 442376 | tf_op jit(solution)/shard_map/ppermute | solution.py:60
  14.4 1.9 %collective-permute-start.5 = (bf16[576,128]{1,0:T(8,128)(2,1)}, bf16[576,128]{1,0:T(8,128)(2,1)S(1)}, u32[]{:S(2)}, u32[]{:S(2)}) collective-permute-start(bf16[576,128]{1,0:T(8,128)(2,1)} %bitcast.55), channel_id=1, source_target_pairs={{0,14},{1,15},{2,12},{3,13},{4,2},{5,3},{6,0},{7,1},{8,6},{9,7},{1... | collective-permute-start | bytes 442376 | tf_op jit(solution)/shard_map/ppermute | solution.py:60
  16.3 1.3 %collective-permute-start.6 = (bf16[576,128]{1,0:T(8,128)(2,1)}, bf16[576,128]{1,0:T(8,128)(2,1)S(1)}, u32[]{:S(2)}, u32[]{:S(2)}) collective-permute-start(bf16[576,128]{1,0:T(8,128)(2,1)} %bitcast.56), channel_id=1, source_target_pairs={{0,26},{1,27},{2,24},{3,25},{4,30},{5,31},{6,28},{7,29},{8,18},{9,... | collective-permute-start | bytes 442376 | tf_op jit(solution)/shard_map/ppermute | solution.py:60
  20.1 5.1 %prologue.1 = (bf16[576,2048]{1,0:T(8,128)(2,1)}, bf16[512,2048]{1,0:T(8,128)(2,1)}) custom-call(bf16[128,4608]{1,0:T(8,128)(2,1)} %q0.1, bf16[128,4608]{1,0:T(8,128)(2,1)} %copy-done, bf16[128,1024]{1,0:T(8,128)(2,1)} %do0.1, bf16[128,1024]{1,0:T(8,128)(2,1)} %copy-done.11, bf16[8,512,128]{2,1,0:T(8,128)(2,1)} %uv.1), custom_call_target="tpu_custom_call" | custom-call | flops 268435456 | bytes 9437184 | tf_op jit(solution)/shard_map/prologue/pallas_call | solution.py:91
  26.1 11.9 %scores.1 = (bf16[1024,2048]{1,0:T(8,128)(2,1)}, bf16[1024,2048]{1,0:T(8,128)(2,1)}, f32[8,2048]{1,0:T(8,128)}, f32[8,2048]{1,0:T(8,128)}) custom-call(s32[16]{0:T(128)} %reshape.438.kblk, s32[4]{0:T(128)} %copy-done.12, bf16[576,128]{1,0:T(8,128)(2,1)} %bitcast.57, bf16[576,128]{1,0:T(8,128)(2,1)} %copy-done.2, bf16[576,128]{1,0:T(8,128)(2,1)} %copy-done.3, ...), custom_call_target="tpu_custom_call" | custom-call | flops 4563402752 | bytes 14680064 | tf_op jit(solution)/shard_map/scores/pallas_call | solution.py:163
  38.1 1.4 %collective-permute-done.9.theirs = f32[8,2048]{1,0:T(8,128)S(1)} collective-permute-done((f32[8,2048]{1,0:T(8,128)}, f32[8,2048]{1,0:T(8,128)S(1)}, u32[]{:S(2)}, u32[]{:S(2)}) %collective-permute-start.9) | collective-permute-done | bytes 65568 | tf_op jit(solution)/shard_map/ppermute | solution.py:60
  40.2 10.6 %grads.1 = (bf16[4,576,128]{2,1,0:T(8,128)(2,1)}, bf16[4,576,128]{2,1,0:T(8,128)(2,1)}, bf16[1024,2048]{1,0:T(8,128)(2,1)}) custom-call(bf16[1024,2048]{1,0:T(8,128)(2,1)} %get-tuple-element.15.e, bf16[1024,2048]{1,0:T(8,128)(2,1)} %get-tuple-element.16.dp, f32[8,2048]{1,0:T(8,128)} %get-tuple-element.17.m, f32[8,2048]{1,0:T(8,128)} %get-tuple-element.18.mine, ...), custom_call_target="tpu_custom_call" | custom-call | flops 4563402752 | bytes 18874368 | tf_op jit(solution)/shard_map/grads/pallas_call | solution.py:233
  50.8 5.4 %query_grad.3 = bf16[576,1024]{1,0:T(8,128)(2,1)} custom-call(bf16[576,128]{1,0:T(8,128)(2,1)} %bitcast.58, bf16[576,128]{1,0:T(8,128)(2,1)} %copy-done.2, bf16[576,128]{1,0:T(8,128)(2,1)} %copy-done.3, bf16[576,128]{1,0:T(8,128)(2,1)} %copy-done.4, bf16[576,128]{1,0:T(8,128)(2,1)} %copy-done.5, bf16[576,128]{1,0:T(8,128)(2,1)} %copy-done.6, ...), custom_call_target="tpu_custom_call" | custom-call | flops 1207959552 | bytes 4194304 | tf_op jit(solution)/shard_map/query_grad/pallas_call | solution.py:285
  56.3 1.8 %collective-permute-start.15 = (bf16[576,128]{1,0:T(8,128)(2,1)S(1)}, bf16[576,128]{1,0:T(8,128)(2,1)S(1)}, u32[]{:S(2)}, u32[]{:S(2)}) collective-permute-start(bf16[576,128]{1,0:T(8,128)(2,1)S(1)} %get-tuple-element.24), channel_id=1, source_target_pairs={{0,12},{1,13},{2,14},{3,15},{4,0},{5,1},{6,2},{7,3},{8,4},{9,5},{1... | collective-permute-start | bytes 442376 | tf_op jit(solution)/shard_map/ppermute | solution.py:60
  58.7 3.8 %collective-permute-start.19 = (bf16[576,128]{1,0:T(8,128)(2,1)S(1)}, bf16[576,128]{1,0:T(8,128)(2,1)S(1)}, u32[]{:S(2)}, u32[]{:S(2)}) collective-permute-start(bf16[576,128]{1,0:T(8,128)(2,1)S(1)} %get-tuple-element.26), channel_id=1, source_target_pairs={{0,30},{1,31},{2,28},{3,29},{4,18},{5,19},{6,16},{7,17},{8,22},{9,... | collective-permute-start | bytes 442376 | tf_op jit(solution)/shard_map/ppermute | solution.py:60
  64.0 4.5 %collective-permute-start.18 = (bf16[576,128]{1,0:T(8,128)(2,1)S(1)}, bf16[576,128]{1,0:T(8,128)(2,1)S(1)}, u32[]{:S(2)}, u32[]{:S(2)}) collective-permute-start(bf16[576,128]{1,0:T(8,128)(2,1)S(1)} %get-tuple-element.30), channel_id=1, source_target_pairs={{0,8},{1,9},{2,10},{3,11},{4,12},{5,13},{6,14},{7,15},{8,0},{9,1},... | collective-permute-start | bytes 442376 | tf_op jit(solution)/shard_map/ppermute | solution.py:60
  68.5 3.2 %collective-permute-start.20 = (bf16[576,128]{1,0:T(8,128)(2,1)S(1)}, bf16[576,128]{1,0:T(8,128)(2,1)S(1)}, u32[]{:S(2)}, u32[]{:S(2)}) collective-permute-start(bf16[576,128]{1,0:T(8,128)(2,1)S(1)} %get-tuple-element.29), channel_id=1, source_target_pairs={{0,6},{1,7},{2,4},{3,5},{4,10},{5,11},{6,8},{7,9},{8,14},{9,15},{1... | collective-permute-start | bytes 442376 | tf_op jit(solution)/shard_map/ppermute | solution.py:60
  71.6 0.7 multiply_sine_fusion
  73.0 7.8 %collective-permute-done.18 = bf16[576,128]{1,0:T(8,128)(2,1)S(1)} collective-permute-done((bf16[576,128]{1,0:T(8,128)(2,1)S(1)}, bf16[576,128]{1,0:T(8,128)(2,1)S(1)}, u32[]{:S(2)}, u32[]{:S(2)}) %collective-permute-start.18) | collective-permute-done | bytes 147488 | tf_op jit(solution)/shard_map/ppermute | solution.py:60
  81.0 4.2 %collective-permute-start.22 = (bf16[576,128]{1,0:T(8,128)(2,1)S(1)}, bf16[576,128]{1,0:T(8,128)(2,1)S(1)}, u32[]{:S(2)}, u32[]{:S(2)}) collective-permute-start(bf16[576,128]{1,0:T(8,128)(2,1)S(1)} %fusion.6), channel_id=1, source_target_pairs={{0,16},{1,17},{2,18},{3,19},{4,20},{5,21},{6,22},{7,23},{8,24},{9,... | collective-permute-start | bytes 442376 | tf_op jit(solution)/shard_map/ppermute | solution.py:60
  85.3 5.3 %query_grad.2.own = bf16[576,1024]{1,0:T(8,128)(2,1)} custom-call(bf16[576,128]{1,0:T(8,128)(2,1)} %bitcast.59, bf16[576,128]{1,0:T(8,128)(2,1)} %copy-done.2, bf16[576,128]{1,0:T(8,128)(2,1)} %copy-done.3, bf16[576,128]{1,0:T(8,128)(2,1)} %copy-done.4, bf16[576,128]{1,0:T(8,128)(2,1)} %copy-done.5, bf16[576,128]{1,0:T(8,128)(2,1)} %copy-done.6, ...), custom_call_target="tpu_custom_call" | custom-call | flops 1207959552 | bytes 4194304 | tf_op jit(solution)/shard_map/query_grad/pallas_call | solution.py:285
  90.5 1.0 copy-done.1
  91.5 6.5 %project.1 = (bf16[4,192,128]{2,1,0:T(8,128)(2,1)}, bf16[4,192,128]{2,1,0:T(8,128)(2,1)}) custom-call(s32[2]{0:T(128)} %pad_add_fusion.place, bf16[576,1024]{1,0:T(8,128)(2,1)} %query_grad.2.own, bf16[576,1024]{1,0:T(8,128)(2,1)} %copy-done.1, f32[32,128]{1,0:T(8,128)} %get-tuple-element.35.cos, f32[32,128]{1,0:T(8,128)} %get-tuple-element.34.sin, ...), custom_call_target="tpu_custom_call" | custom-call | flops 738197504 | bytes 9437184 | tf_op jit(solution)/shard_map/project/pallas_call | solution.py:325
  98.2 3.3 %collective-permute-start.23 = (bf16[576,128]{1,0:T(8,128)(2,1)S(1)}, bf16[576,128]{1,0:T(8,128)(2,1)S(1)}, u32[]{:S(2)}, u32[]{:S(2)}) collective-permute-start(bf16[576,128]{1,0:T(8,128)(2,1)S(1)} %add_convert_fusion.2), channel_id=1, source_target_pairs={{0,64},{1,65},{2,66},{3,67},{4,68},{5,69},{6,70},{7,71},{8,72},{9,... | collective-permute-start | bytes 442376 | tf_op jit(solution)/shard_map/ppermute | solution.py:60
  102.2 2.6 %collective-permute-start.25 = (bf16[576,128]{1,0:T(8,128)(2,1)S(1)}, bf16[576,128]{1,0:T(8,128)(2,1)S(1)}, u32[]{:S(2)}, u32[]{:S(2)}) collective-permute-start(bf16[576,128]{1,0:T(8,128)(2,1)S(1)} %add_convert_fusion.2), channel_id=1, source_target_pairs={{0,96},{1,97},{2,98},{3,99},{4,100},{5,101},{6,102},{7,103},{8,104... | collective-permute-start | bytes 442376 | tf_op jit(solution)/shard_map/ppermute | solution.py:60
  104.7 0.8 collective-permute-done.11
  105.5 1.0 add_convert_fusion
  106.5 1.6 %collective-permute-start.12 = (bf16[192,128]{1,0:T(8,128)(2,1)S(1)}, bf16[192,128]{1,0:T(8,128)(2,1)S(1)}, u32[]{:S(2)}, u32[]{:S(2)}) collective-permute-start(bf16[192,128]{1,0:T(8,128)(2,1)S(1)} %get-tuple-element.31), channel_id=1, source_target_pairs={{0,32},{1,33},{2,34},{3,35},{4,36},{5,37},{6,38},{7,39},{8,40},{9,... | collective-permute-start | bytes 147464 | tf_op jit(solution)/shard_map/ppermute | solution.py:60
  108.2 2.9 %collective-permute-start.13 = (bf16[192,128]{1,0:T(8,128)(2,1)S(1)}, bf16[192,128]{1,0:T(8,128)(2,1)S(1)}, u32[]{:S(2)}, u32[]{:S(2)}) collective-permute-start(bf16[192,128]{1,0:T(8,128)(2,1)S(1)} %get-tuple-element.33), channel_id=1, source_target_pairs={{0,64},{1,65},{2,66},{3,67},{4,68},{5,69},{6,70},{7,71},{8,72},{9,... | collective-permute-start | bytes 147464 | tf_op jit(solution)/shard_map/ppermute | solution.py:60
  111.1 1.3 %collective-permute-start.14 = (bf16[192,128]{1,0:T(8,128)(2,1)S(1)}, bf16[192,128]{1,0:T(8,128)(2,1)S(1)}, u32[]{:S(2)}, u32[]{:S(2)}) collective-permute-start(bf16[192,128]{1,0:T(8,128)(2,1)S(1)} %get-tuple-element.32), channel_id=1, source_target_pairs={{0,96},{1,97},{2,98},{3,99},{4,100},{5,101},{6,102},{7,103},{8,104... | collective-permute-start | bytes 147464 | tf_op jit(solution)/shard_map/ppermute | solution.py:60
  112.4 0.7 fusion.7
  113.8 1.4 %collective-permute-done.14 = bf16[192,128]{1,0:T(8,128)(2,1)S(1)} collective-permute-done((bf16[192,128]{1,0:T(8,128)(2,1)S(1)}, bf16[192,128]{1,0:T(8,128)(2,1)S(1)}, u32[]{:S(2)}, u32[]{:S(2)}) %collective-permute-start.14) | collective-permute-done | bytes 49184 | tf_op jit(solution)/shard_map/ppermute | solution.py:60
  (77 shorter events, 10.1 us)
Async XLA Ops:
  0.6 15.6 %collective-permute-start.7 = (bf16[128,4608]{1,0:T(8,128)(2,1)}, bf16[128,4608]{1,0:T(8,128)(2,1)S(1)}, u32[]{:S(2)}, u32[]{:S(2)}) collective-permute-start(bf16[128,4608]{1,0:T(8,128)(2,1)} %q0.1), channel_id=1, source_target_pairs={{0,1},{1,0},{2,3},{3,2},{4,5},{5,4},{6,7},{7,6},{8,9},{9,8},{10,11... | collective-permute-start | bytes 3538952 | tf_op jit(solution)/shard_map/ppermute | solution.py:60
  0.7 8.8 %collective-permute-start = (bf16[576,128]{1,0:T(8,128)(2,1)}, bf16[576,128]{1,0:T(8,128)(2,1)S(1)}, u32[]{:S(2)}, u32[]{:S(2)}) collective-permute-start(bf16[576,128]{1,0:T(8,128)(2,1)} %bitcast.50), channel_id=1, source_target_pairs={{0,4},{1,5},{2,6},{3,7},{4,8},{5,9},{6,10},{7,11},{8,12},{9,13},{1... | collective-permute-start | bytes 442376 | tf_op jit(solution)/shard_map/ppermute | solution.py:60
  2.8 8.4 %collective-permute-start.1 = (bf16[576,128]{1,0:T(8,128)(2,1)}, bf16[576,128]{1,0:T(8,128)(2,1)S(1)}, u32[]{:S(2)}, u32[]{:S(2)}) collective-permute-start(bf16[576,128]{1,0:T(8,128)(2,1)} %bitcast.51), channel_id=1, source_target_pairs={{0,12},{1,13},{2,14},{3,15},{4,0},{5,1},{6,2},{7,3},{8,4},{9,5},{1... | collective-permute-start | bytes 442376 | tf_op jit(solution)/shard_map/ppermute | solution.py:60
  5.0 20.2 %collective-permute-start.2 = (bf16[576,128]{1,0:T(8,128)(2,1)}, bf16[576,128]{1,0:T(8,128)(2,1)S(1)}, u32[]{:S(2)}, u32[]{:S(2)}) collective-permute-start(bf16[576,128]{1,0:T(8,128)(2,1)} %bitcast.52), channel_id=1, source_target_pairs={{0,2},{1,3},{2,0},{3,1},{4,6},{5,7},{6,4},{7,5},{8,10},{9,11},{10,... | collective-permute-start | bytes 442376 | tf_op jit(solution)/shard_map/ppermute | solution.py:60
  6.5 7.9 %collective-permute-start.8 = (bf16[128,1024]{1,0:T(8,128)(2,1)}, bf16[128,1024]{1,0:T(8,128)(2,1)S(1)}, u32[]{:S(2)}, u32[]{:S(2)}) collective-permute-start(bf16[128,1024]{1,0:T(8,128)(2,1)} %do0.1), channel_id=1, source_target_pairs={{0,1},{1,0},{2,3},{3,2},{4,5},{5,4},{6,7},{7,6},{8,9},{9,8},{10,11... | collective-permute-start | bytes 786440 | tf_op jit(solution)/shard_map/ppermute | solution.py:60
  8.1 17.2 %copy-start.12 = (s32[4]{0:T(128)}, s32[4]{0:T(128)S(1)}, u32[]{:S(2)}) copy-start(s32[4]{0:T(128)S(1)} %reshape.439.qblk) | copy-start | bytes 52
  9.6 15.7 %copy-start.2 = (bf16[576,128]{1,0:T(8,128)(2,1)}, bf16[576,128]{1,0:T(8,128)(2,1)S(1)}, u32[]{:S(2)}) copy-start(bf16[576,128]{1,0:T(8,128)(2,1)S(1)} %collective-permute-done.refs_1_) | copy-start | bytes 442372
  9.6 15.6 %collective-permute-start.3 = (bf16[576,128]{1,0:T(8,128)(2,1)}, bf16[576,128]{1,0:T(8,128)(2,1)S(1)}, u32[]{:S(2)}, u32[]{:S(2)}) collective-permute-start(bf16[576,128]{1,0:T(8,128)(2,1)} %bitcast.53), channel_id=1, source_target_pairs={{0,8},{1,9},{2,10},{3,11},{4,12},{5,13},{6,14},{7,15},{8,0},{9,1},... | collective-permute-start | bytes 442376 | tf_op jit(solution)/shard_map/ppermute | solution.py:60
  11.2 14.1 %copy-start.3 = (bf16[576,128]{1,0:T(8,128)(2,1)}, bf16[576,128]{1,0:T(8,128)(2,1)S(1)}, u32[]{:S(2)}) copy-start(bf16[576,128]{1,0:T(8,128)(2,1)S(1)} %collective-permute-done.1.refs_2_) | copy-start | bytes 442372
  11.2 14.0 %collective-permute-start.4 = (bf16[576,128]{1,0:T(8,128)(2,1)}, bf16[576,128]{1,0:T(8,128)(2,1)S(1)}, u32[]{:S(2)}, u32[]{:S(2)}) collective-permute-start(bf16[576,128]{1,0:T(8,128)(2,1)} %bitcast.54), channel_id=1, source_target_pairs={{0,22},{1,23},{2,20},{3,21},{4,26},{5,27},{6,24},{7,25},{8,30},{9,... | collective-permute-start | bytes 442376 | tf_op jit(solution)/shard_map/ppermute | solution.py:60
  14.4 5.7 %copy-start.11 = (bf16[128,1024]{1,0:T(8,128)(2,1)}, bf16[128,1024]{1,0:T(8,128)(2,1)S(1)}, u32[]{:S(2)}) copy-start(bf16[128,1024]{1,0:T(8,128)(2,1)S(1)} %collective-permute-done.8.do1) | copy-start | bytes 786436
  14.4 10.8 %collective-permute-start.5 = (bf16[576,128]{1,0:T(8,128)(2,1)}, bf16[576,128]{1,0:T(8,128)(2,1)S(1)}, u32[]{:S(2)}, u32[]{:S(2)}) collective-permute-start(bf16[576,128]{1,0:T(8,128)(2,1)} %bitcast.55), channel_id=1, source_target_pairs={{0,14},{1,15},{2,12},{3,13},{4,2},{5,3},{6,0},{7,1},{8,6},{9,7},{1... | collective-permute-start | bytes 442376 | tf_op jit(solution)/shard_map/ppermute | solution.py:60
  16.3 9.0 %collective-permute-start.6 = (bf16[576,128]{1,0:T(8,128)(2,1)}, bf16[576,128]{1,0:T(8,128)(2,1)S(1)}, u32[]{:S(2)}, u32[]{:S(2)}) collective-permute-start(bf16[576,128]{1,0:T(8,128)(2,1)} %bitcast.56), channel_id=1, source_target_pairs={{0,26},{1,27},{2,24},{3,25},{4,30},{5,31},{6,28},{7,29},{8,18},{9,... | collective-permute-start | bytes 442376 | tf_op jit(solution)/shard_map/ppermute | solution.py:60
  38.0 1.5 %collective-permute-start.9 = (f32[8,2048]{1,0:T(8,128)}, f32[8,2048]{1,0:T(8,128)S(1)}, u32[]{:S(2)}, u32[]{:S(2)}) collective-permute-start(f32[8,2048]{1,0:T(8,128)} %get-tuple-element.18.mine), channel_id=1, source_target_pairs={{0,1},{1,0},{2,3},{3,2},{4,5},{5,4},{6,7},{7,6},{8,9},{9,8},{10,11... | collective-permute-start | bytes 196616 | tf_op jit(solution)/shard_map/ppermute | solution.py:60
  50.7 5.5 %copy-start.10 = (bf16[4,576,128]{2,1,0:T(8,128)(2,1)S(1)}, bf16[4,576,128]{2,1,0:T(8,128)(2,1)}, u32[]{:S(2)}) copy-start(bf16[4,576,128]{2,1,0:T(8,128)(2,1)} %get-tuple-element.23) | copy-start | bytes 1769476
  50.8 12.4 %copy-start.9 = (bf16[4,576,128]{2,1,0:T(8,128)(2,1)S(1)}, bf16[4,576,128]{2,1,0:T(8,128)(2,1)}, u32[]{:S(2)}) copy-start(bf16[4,576,128]{2,1,0:T(8,128)(2,1)} %get-tuple-element.22) | copy-start | bytes 1769476
  56.1 34.4 %collective-permute-start.10 = (bf16[576,1024]{1,0:T(8,128)(2,1)}, bf16[576,1024]{1,0:T(8,128)(2,1)S(1)}, u32[]{:S(2)}, u32[]{:S(2)}) collective-permute-start(bf16[576,1024]{1,0:T(8,128)(2,1)} %query_grad.3), channel_id=1, source_target_pairs={{0,1},{1,0},{2,3},{3,2},{4,5},{5,4},{6,7},{7,6},{8,9},{9,8},{10,11... | collective-permute-start | bytes 3538952 | tf_op jit(solution)/shard_map/ppermute | solution.py:60
  56.3 6.8 %collective-permute-start.15 = (bf16[576,128]{1,0:T(8,128)(2,1)S(1)}, bf16[576,128]{1,0:T(8,128)(2,1)S(1)}, u32[]{:S(2)}, u32[]{:S(2)}) collective-permute-start(bf16[576,128]{1,0:T(8,128)(2,1)S(1)} %get-tuple-element.24), channel_id=1, source_target_pairs={{0,12},{1,13},{2,14},{3,15},{4,0},{5,1},{6,2},{7,3},{8,4},{9,5},{1... | collective-permute-start | bytes 442376 | tf_op jit(solution)/shard_map/ppermute | solution.py:60
  58.2 5.8 %collective-permute-start.17 = (bf16[576,128]{1,0:T(8,128)(2,1)S(1)}, bf16[576,128]{1,0:T(8,128)(2,1)S(1)}, u32[]{:S(2)}, u32[]{:S(2)}) collective-permute-start(bf16[576,128]{1,0:T(8,128)(2,1)S(1)} %get-tuple-element.27), channel_id=1, source_target_pairs={{0,2},{1,3},{2,0},{3,1},{4,6},{5,7},{6,4},{7,5},{8,10},{9,11},{10,... | collective-permute-start | bytes 442376 | tf_op jit(solution)/shard_map/ppermute | solution.py:60
  58.7 9.8 %collective-permute-start.19 = (bf16[576,128]{1,0:T(8,128)(2,1)S(1)}, bf16[576,128]{1,0:T(8,128)(2,1)S(1)}, u32[]{:S(2)}, u32[]{:S(2)}) collective-permute-start(bf16[576,128]{1,0:T(8,128)(2,1)S(1)} %get-tuple-element.26), channel_id=1, source_target_pairs={{0,30},{1,31},{2,28},{3,29},{4,18},{5,19},{6,16},{7,17},{8,22},{9,... | collective-permute-start | bytes 442376 | tf_op jit(solution)/shard_map/ppermute | solution.py:60
  62.5 10.5 %collective-permute-start.21 = (bf16[576,128]{1,0:T(8,128)(2,1)S(1)}, bf16[576,128]{1,0:T(8,128)(2,1)S(1)}, u32[]{:S(2)}, u32[]{:S(2)}) collective-permute-start(bf16[576,128]{1,0:T(8,128)(2,1)S(1)} %get-tuple-element.25), channel_id=1, source_target_pairs={{0,26},{1,27},{2,24},{3,25},{4,30},{5,31},{6,28},{7,29},{8,18},{9,... | collective-permute-start | bytes 442376 | tf_op jit(solution)/shard_map/ppermute | solution.py:60
  63.2 9.8 %collective-permute-start.16 = (bf16[576,128]{1,0:T(8,128)(2,1)S(1)}, bf16[576,128]{1,0:T(8,128)(2,1)S(1)}, u32[]{:S(2)}, u32[]{:S(2)}) collective-permute-start(bf16[576,128]{1,0:T(8,128)(2,1)S(1)} %get-tuple-element.28), channel_id=1, source_target_pairs={{0,4},{1,5},{2,6},{3,7},{4,8},{5,9},{6,10},{7,11},{8,12},{9,13},{1... | collective-permute-start | bytes 442376 | tf_op jit(solution)/shard_map/ppermute | solution.py:60
  64.0 16.9 %collective-permute-start.18 = (bf16[576,128]{1,0:T(8,128)(2,1)S(1)}, bf16[576,128]{1,0:T(8,128)(2,1)S(1)}, u32[]{:S(2)}, u32[]{:S(2)}) collective-permute-start(bf16[576,128]{1,0:T(8,128)(2,1)S(1)} %get-tuple-element.30), channel_id=1, source_target_pairs={{0,8},{1,9},{2,10},{3,11},{4,12},{5,13},{6,14},{7,15},{8,0},{9,1},... | collective-permute-start | bytes 442376 | tf_op jit(solution)/shard_map/ppermute | solution.py:60
  68.5 12.4 %collective-permute-start.20 = (bf16[576,128]{1,0:T(8,128)(2,1)S(1)}, bf16[576,128]{1,0:T(8,128)(2,1)S(1)}, u32[]{:S(2)}, u32[]{:S(2)}) collective-permute-start(bf16[576,128]{1,0:T(8,128)(2,1)S(1)} %get-tuple-element.29), channel_id=1, source_target_pairs={{0,6},{1,7},{2,4},{3,5},{4,10},{5,11},{6,8},{7,9},{8,14},{9,15},{1... | collective-permute-start | bytes 442376 | tf_op jit(solution)/shard_map/ppermute | solution.py:60
  81.0 17.2 %collective-permute-start.22 = (bf16[576,128]{1,0:T(8,128)(2,1)S(1)}, bf16[576,128]{1,0:T(8,128)(2,1)S(1)}, u32[]{:S(2)}, u32[]{:S(2)}) collective-permute-start(bf16[576,128]{1,0:T(8,128)(2,1)S(1)} %fusion.6), channel_id=1, source_target_pairs={{0,16},{1,17},{2,18},{3,19},{4,20},{5,21},{6,22},{7,23},{8,24},{9,... | collective-permute-start | bytes 442376 | tf_op jit(solution)/shard_map/ppermute | solution.py:60
  98.1 7.5 %collective-permute-start.11 = (bf16[4,192,128]{2,1,0:T(8,128)(2,1)}, bf16[4,192,128]{2,1,0:T(8,128)(2,1)S(1)}, u32[]{:S(2)}, u32[]{:S(2)}) collective-permute-start(bf16[4,192,128]{2,1,0:T(8,128)(2,1)} %get-tuple-element.21), channel_id=1, source_target_pairs={{0,16},{1,17},{2,18},{3,19},{4,20},{5,21},{6,22},{7,23},{8,24},{9,... | collective-permute-start | bytes 589832 | tf_op jit(solution)/shard_map/ppermute | solution.py:60
  98.2 12.9 %collective-permute-start.23 = (bf16[576,128]{1,0:T(8,128)(2,1)S(1)}, bf16[576,128]{1,0:T(8,128)(2,1)S(1)}, u32[]{:S(2)}, u32[]{:S(2)}) collective-permute-start(bf16[576,128]{1,0:T(8,128)(2,1)S(1)} %add_convert_fusion.2), channel_id=1, source_target_pairs={{0,64},{1,65},{2,66},{3,67},{4,68},{5,69},{6,70},{7,71},{8,72},{9,... | collective-permute-start | bytes 442376 | tf_op jit(solution)/shard_map/ppermute | solution.py:60
  101.5 10.9 %collective-permute-start.24 = (bf16[576,128]{1,0:T(8,128)(2,1)S(1)}, bf16[576,128]{1,0:T(8,128)(2,1)S(1)}, u32[]{:S(2)}, u32[]{:S(2)}) collective-permute-start(bf16[576,128]{1,0:T(8,128)(2,1)S(1)} %add_convert_fusion.2), channel_id=1, source_target_pairs={{0,32},{1,33},{2,34},{3,35},{4,36},{5,37},{6,38},{7,39},{8,40},{9,... | collective-permute-start | bytes 442376 | tf_op jit(solution)/shard_map/ppermute | solution.py:60
  102.2 10.3 %collective-permute-start.25 = (bf16[576,128]{1,0:T(8,128)(2,1)S(1)}, bf16[576,128]{1,0:T(8,128)(2,1)S(1)}, u32[]{:S(2)}, u32[]{:S(2)}) collective-permute-start(bf16[576,128]{1,0:T(8,128)(2,1)S(1)} %add_convert_fusion.2), channel_id=1, source_target_pairs={{0,96},{1,97},{2,98},{3,99},{4,100},{5,101},{6,102},{7,103},{8,104... | collective-permute-start | bytes 442376 | tf_op jit(solution)/shard_map/ppermute | solution.py:60
  106.5 6.7 %collective-permute-start.12 = (bf16[192,128]{1,0:T(8,128)(2,1)S(1)}, bf16[192,128]{1,0:T(8,128)(2,1)S(1)}, u32[]{:S(2)}, u32[]{:S(2)}) collective-permute-start(bf16[192,128]{1,0:T(8,128)(2,1)S(1)} %get-tuple-element.31), channel_id=1, source_target_pairs={{0,32},{1,33},{2,34},{3,35},{4,36},{5,37},{6,38},{7,39},{8,40},{9,... | collective-permute-start | bytes 147464 | tf_op jit(solution)/shard_map/ppermute | solution.py:60
  108.2 5.6 %collective-permute-start.13 = (bf16[192,128]{1,0:T(8,128)(2,1)S(1)}, bf16[192,128]{1,0:T(8,128)(2,1)S(1)}, u32[]{:S(2)}, u32[]{:S(2)}) collective-permute-start(bf16[192,128]{1,0:T(8,128)(2,1)S(1)} %get-tuple-element.33), channel_id=1, source_target_pairs={{0,64},{1,65},{2,66},{3,67},{4,68},{5,69},{6,70},{7,71},{8,72},{9,... | collective-permute-start | bytes 147464 | tf_op jit(solution)/shard_map/ppermute | solution.py:60
  111.1 4.1 %collective-permute-start.14 = (bf16[192,128]{1,0:T(8,128)(2,1)S(1)}, bf16[192,128]{1,0:T(8,128)(2,1)S(1)}, u32[]{:S(2)}, u32[]{:S(2)}) collective-permute-start(bf16[192,128]{1,0:T(8,128)(2,1)S(1)} %get-tuple-element.32), channel_id=1, source_target_pairs={{0,96},{1,97},{2,98},{3,99},{4,100},{5,101},{6,102},{7,103},{8,104... | collective-permute-start | bytes 147464 | tf_op jit(solution)/shard_map/ppermute | solution.py:60
  (8 other events, 9.1 us)

commit v2 on v0

v2 whole, which is shorter than its diff:
```python
import functools

import jax
import jax.numpy as jnp
from jax import lax
from jax.experimental import pallas as pl
from jax.experimental.pallas import tpu as pltpu
from jax.sharding import Mesh
from jax.sharding import PartitionSpec as P

D_LAT = 512
D_ROPE = 64
D_NOPE = 128
D_V = 128
BLOCK = 64
ROW = D_LAT + D_ROPE
HALF = D_ROPE // 2
N_Y, N_XH, N_Z, N_XL = 4, 2, 4, 2
N_X = N_XH * N_XL
TOK = 128
HEADS_L = 8
SHARDS = N_Z * N_XL
KEYS = SHARDS * TOK
HROWS = HEADS_L * TOK
ROWS = 2 * HROWS
F_ROWS = HEADS_L * (D_NOPE + D_ROPE)
C_COLS = 192
SCALE = (D_NOPE + D_ROPE) ** -0.5
K_SCALE = SCALE * 1.4426950408889634
MASKED = -1e30
AXES = ("y", "xh", "z", "xl", "core")
TN = 256

SLOTS = ((0, 0), (0, 1), (1, 0), (3, 0), (2, 0), (1, 1), (3, 1), (2, 1))
EARLY = 4

NT = (((1,), (1,)), ((), ()))
NN = (((1,), (0,)), ((), ()))
bf16 = jnp.bfloat16
f32 = jnp.float32


def dot(a, b, dims=NN):
    return lax.dot_general(a, b, dims, preferred_element_type=f32)


def shift(x, dy=0, dx=0, dz=0, dxl=0, dcore=0):
    pairs = []
    for y in range(N_Y):
        for xh in range(N_XH):
            for z in range(N_Z):
                for xl in range(N_XL):
                    for c in range(2):
                        a = (xh * N_XL + xl + dx) % N_X
                        to = ((y + dy) % N_Y) * N_XH + a // N_XL
                        to = to * N_Z + (z + dz) % N_Z
                        to = to * N_XL + (a + dxl) % N_XL
                        to = to * 2 + (c + dcore) % 2
                        pairs.append((len(pairs), to))
    return lax.ppermute(x, AXES, pairs)


def params(mib):
    return pltpu.CompilerParams(vmem_limit_bytes=mib * 1024 * 1024)


def cost(flops, exps=0):
    return pl.CostEstimate(flops=flops, bytes_accessed=1024 * 1024, transcendentals=exps)


def vmem():
    return pl.BlockSpec(memory_space=pltpu.VMEM)


def smem():
    return pl.BlockSpec(memory_space=pltpu.SMEM)


def hbm():
    return pl.BlockSpec(memory_space=pltpu.HBM)


def like(*shape, dtype=bf16):
    return jax.ShapeDtypeStruct(shape, dtype)


def kept(*shape, dtype=bf16):
    return pltpu.VMEM(shape, dtype)


def held(*arrays):
    return [pltpu.with_memory_space_constraint(x, pltpu.VMEM) for x in arrays]


def left(x):
    return pltpu.with_memory_space_constraint(x, pltpu.HBM)


def prologue_kernel(q0, q1, do0, do1, uv_hbm, qt, gt, q_own, do_own, uv, sems):
    copies = [
        pltpu.make_async_copy(src, dst, sems.at[i])
        for i, (src, dst) in enumerate(((uv_hbm, uv), (do0, do_own), (q0, q_own)))
    ]
    for c in copies:
        c.start()

    def transpose(s, q):
        for j in range(HEADS_L * ROW // 128):
            t = q[:, j * 128 : (j + 1) * 128].T
            for k in range(2):
                r = j * 128 + k * 64
                h, d = r // ROW, r % ROW
                col = (s * HEADS_L + h) * TOK
                qt[d : d + 64, col : col + TOK] = t[k * 64 : (k + 1) * 64, :]

    def value_grad(s, do):
        for h in range(HEADS_L):
            col = (s * HEADS_L + h) * TOK
            g = dot(uv[h], do[:, h * D_V : (h + 1) * D_V], NT)
            gt[:, col : col + TOK] = g.astype(bf16)

    transpose(1, q1)
    copies[0].wait()
    value_grad(1, do1)
    copies[1].wait()
    value_grad(0, do_own)
    copies[2].wait()
    transpose(0, q_own)


def prologue(q0, q1, do0, do1, uv):
    return pl.pallas_call(
        prologue_kernel,
        out_shape=(kept(ROW, ROWS), kept(D_LAT, ROWS)),
        in_specs=[hbm(), vmem(), hbm(), vmem(), hbm()],
        out_specs=(vmem(), vmem()),
        scratch_shapes=[
            pltpu.VMEM(q0.shape, bf16),
            pltpu.VMEM(do0.shape, bf16),
            pltpu.VMEM(uv.shape, bf16),
            pltpu.SemaphoreType.DMA((3,)),
        ],
        compiler_params=params(10),
        cost_estimate=cost(2 * ROWS * D_V * D_LAT),
        name="prologue",
    )(left(q0), q1, left(do0), do1, left(uv))


def scores_kernel(slots, order, place, qt, gt, *refs):
    n = len(slots)
    kts, refs = refs[:n], refs[n:]
    before = None
    if slots[0]:
        before, refs = refs[0], refs[1:]
    e_out, dp_out, kt_out, m_out, merged, k_nat, bias = refs
    z, xl, core = place[0], place[1], place[2]

    def owner(dz, dxl, c):
        return (lax.rem(z + N_Z - dz, N_Z) * N_XL + lax.rem(xl + dxl, N_XL)) * 2 + c

    lane = lax.broadcasted_iota(jnp.int32, (BLOCK, TOK), 1)
    sub = lax.broadcasted_iota(jnp.int32, (BLOCK, TOK), 0)
    for i, slot in enumerate(slots):
        k_nat[i * TOK : (i + 1) * TOK, :] = kts[i][...].T
        kt_out[:, i * TOK : (i + 1) * TOK] = kts[i][...]
        o = owner(*SLOTS[slot], core)
        for t in range(2):
            q = owner(0, 0, core if t == 0 else 1 - core)
            q_pos = jnp.where(
                lane < BLOCK,
                order[2 * q] * BLOCK + lane,
                order[2 * q + 1] * BLOCK + lane - BLOCK,
            )
            for b in range(2):
                k_pos = order[2 * o + b] * BLOCK + sub
                at = i * TOK + b * BLOCK
                bias[t, at : at + BLOCK, :] = jnp.where(k_pos <= q_pos, 0.0, MASKED)

    @pl.loop(0, ROWS // TN)
    def _(step):
        base = pl.multiple_of(step * TN, TN)
        token_set = step // (HROWS // TN)
        q, g = qt[:, pl.ds(base, TN)], gt[:, pl.ds(base, TN)]
        halves = TN // TOK
        ms, ls, ws = [], [], []
        for i in range(n):
            rows = slice(i * TOK, (i + 1) * TOK)
            sc = dot(k_nat[rows, :], q)
            dp = dot(k_nat[rows, :D_LAT], g)
            b = bias[token_set, rows, :]
            for j in range(halves):
                cols = pl.ds(base + j * TOK, TOK)
                x = sc[:, j * TOK : (j + 1) * TOK] * K_SCALE + b
                m = jnp.max(x, axis=0, keepdims=True)
                e = jnp.exp2(x - m)
                d = dp[:, j * TOK : (j + 1) * TOK]
                ms.append(m)
                ls.append(jnp.sum(e, axis=0, keepdims=True))
                ws.append(jnp.sum(e * d, axis=0, keepdims=True))
                e_out[rows, cols] = e.astype(bf16)
                dp_out[rows, cols] = d.astype(bf16)
                m_out[i : i + 1, cols] = m
        for j in range(halves):
            cols = pl.ds(base + j * TOK, TOK)
            mj, lj, wj = ms[j::halves], ls[j::halves], ws[j::halves]
            if before is not None:
                mj, lj, wj = (
                    a + [before[k : k + 1, cols]] for k, a in enumerate((mj, lj, wj))
                )
            top = functools.reduce(jnp.maximum, mj)
            f = [jnp.exp2(m - top) for m in mj]
            merged[0:1, cols] = top
            merged[1:2, cols] = sum(a * b for a, b in zip(f, lj))
            merged[2:3, cols] = sum(a * b for a, b in zip(f, wj))


def scores(slots, order, place, qt, gt, kts, before=()):
    n = len(slots)
    return pl.pallas_call(
        functools.partial(scores_kernel, slots),
        out_shape=(
            kept(n * TOK, ROWS),
            kept(n * TOK, ROWS),
            kept(ROW, n * TOK),
            like(8, ROWS, dtype=f32),
            like(8, ROWS, dtype=f32),
        ),
        in_specs=[smem(), smem()] + [vmem()] * (2 + n + len(before)),
        out_specs=(vmem(),) * 5,
        scratch_shapes=[pltpu.VMEM((n * TOK, ROW), bf16), pltpu.VMEM((2, n * TOK, TOK), f32)],
        compiler_params=params(8),
        cost_estimate=cost(2 * ROWS * n * TOK * (ROW + D_LAT), ROWS * n * TOK),
        name="scores",
    )(order, place, *held(qt, gt), *kts, *before)


def grads_kernel(counts, *refs):
    n = len(counts)
    es, dps, ms, refs = refs[:n], refs[n : 2 * n], refs[2 * n : 3 * n], refs[3 * n :]
    mine, theirs, qt, gt = refs[:4]
    outs, refs = refs[4 : 4 + N_Z], refs[4 + N_Z :]
    dss, (r_s, rc_s, delta_s, p_s, dk_s, sems) = refs[:n], refs[n:]
    copies = []
    for j in range(2):
        a = slice(j * HROWS, (j + 1) * HROWS)
        b = slice((1 - j) * HROWS, (2 - j) * HROWS)
        m0, m1 = mine[0:1, a], theirs[0:1, b]
        top = jnp.maximum(m0, m1)
        f0, f1 = jnp.exp2(m0 - top), jnp.exp2(m1 - top)
        inv = 1.0 / (f0 * mine[1:2, a] + f1 * theirs[1:2, b])
        delta_s[0:1, a] = (f0 * mine[2:3, a] + f1 * theirs[2:3, b]) * inv
        at = 0
        for m, c in zip(ms, counts):
            r = jnp.exp2(m[:c, a] - top) * inv
            r_s[at : at + c, a] = r
            rc_s[at : at + c, a] = r * SCALE
            at += c
    at = 0
    for e, dp, ds, c in zip(es, dps, dss, counts):
        for k in range(c):
            s = at + k
            rows = slice(k * TOK, (k + 1) * TOK)
            p_rows = slice((s % 4) * TOK, (s % 4 + 1) * TOK)
            for j in range(ROWS // TN):
                cols = slice(j * TN, (j + 1) * TN)
                ef = e[rows, cols].astype(f32)
                p_s[p_rows, cols] = (ef * r_s[s : s + 1, cols]).astype(bf16)
                d = dp[rows, cols].astype(f32) - delta_s[0:1, cols]
                ds[rows, cols] = (ef * rc_s[s : s + 1, cols] * d).astype(bf16)
            if k % 2:
                pair = slice((k - 1) * TOK, (k + 1) * TOK)
                p_pair = slice((s % 4 - 1) * TOK, (s % 4 + 1) * TOK)
                dk = dot(qt[...], ds[pair, :], NT)
                dv = dot(gt[...], p_s[p_pair, :], NT)
                for i in range(2):
                    h = slice(i * TOK, (i + 1) * TOK)
                    o = s - 1 + i
                    dz, dxl = SLOTS[o]
                    dk_s[o, :D_LAT, :] = (dk[:D_LAT, h] + dv[:, h]).astype(bf16)
                    dk_s[o, D_LAT:, :] = dk[D_LAT:, h].astype(bf16)
                    copies.append(pltpu.make_async_copy(dk_s.at[o], outs[dz].at[dxl], sems.at[o]))
                    copies[-1].start()
        at += c
    for copy in copies:
        copy.wait()


def grads(parts, mine, theirs, qt, gt):
    es, dps, ms = zip(*parts)
    counts = tuple(e.shape[0] // TOK for e in es)
    res = pl.pallas_call(
        functools.partial(grads_kernel, counts),
        out_shape=(pltpu.HBM((N_XL, ROW, TOK), bf16),) * N_Z + tuple(kept(*e.shape) for e in es),
        in_specs=[vmem()] * (3 * len(parts) + 4),
        out_specs=(hbm(),) * N_Z + (vmem(),) * len(parts),
        scratch_shapes=[
            pltpu.VMEM((SHARDS, ROWS), f32),
            pltpu.VMEM((SHARDS, ROWS), f32),
            pltpu.VMEM((8, ROWS), f32),
            pltpu.VMEM((4 * TOK, ROWS), bf16),
            pltpu.VMEM((SHARDS, ROW, TOK), bf16),
            pltpu.SemaphoreType.DMA((SHARDS,)),
        ],
        compiler_params=params(8),
        cost_estimate=cost(2 * ROWS * KEYS * (ROW + D_LAT)),
        name="grads",
    )(*held(*es, *dps), *ms, mine, theirs, *held(qt, gt))
    return res[:N_Z], res[N_Z:]


def project_kernel(place, uk, uq, cos, sin, *refs):
    n = (len(refs) - 6) // 2
    dss, kts = refs[:n], refs[n : 2 * n]
    give_send, give_keep, send, keep, ft, cg = refs[2 * n :]
    for t in (1, 0):
        half = slice(t * HROWS, (t + 1) * HROWS)
        dq = sum(dot(kt[...], ds[:, half]) for kt, ds in zip(kts, dss)).astype(bf16)
        out = slice(t * TOK, (t + 1) * TOK)
        for h in range(HEADS_L):
            d = dq[:, h * TOK : (h + 1) * TOK]
            base = h * (D_NOPE + D_ROPE)
            ft[base : base + D_NOPE, out] = dot(uk[h], d[:D_LAT]).astype(bf16)
            a = d[D_LAT : D_LAT + HALF].astype(f32)
            b = d[D_LAT + HALF :].astype(f32)
            base += D_NOPE
            c, s = cos[:, out], sin[:, out]
            ft[base : base + HALF, out] = (a * c + b * s).astype(bf16)
            ft[base + HALF : base + D_ROPE, out] = (b * c - a * s).astype(bf16)
    cg[...] = dot(uq[...], ft[...]).astype(bf16)
    y, xh = place[3], place[4]
    for d in range(N_Y):
        yd = lax.rem(y + d, N_Y)
        away = pl.ds(pl.multiple_of((yd * 2 + 1 - xh) * C_COLS, 64), C_COLS)
        here = pl.ds(pl.multiple_of((yd * 2 + xh) * C_COLS, 64), C_COLS)
        send[d], keep[d] = cg[away, :TOK], cg[here, :TOK]
        give_send[d], give_keep[d] = cg[away, TOK:], cg[here, TOK:]


def project(place, dss, kts, cos, sin, uk, uq):
    q_rank = uq.shape[0]
    return pl.pallas_call(
        project_kernel,
        out_shape=(like(N_Y, C_COLS, TOK),) * 4,
        in_specs=[smem()] + [vmem()] * (4 + 2 * len(dss)),
        out_specs=(vmem(),) * 4,
        scratch_shapes=[pltpu.VMEM((F_ROWS, 2 * TOK), bf16), pltpu.VMEM((q_rank, 2 * TOK), bf16)],
        compiler_params=params(12),
        cost_estimate=cost(4 * HROWS * KEYS * ROW),
        name="project",
    )(place, uk, uq, cos, sin, *held(*dss, *kts))


def combine_kernel(a, a2, b1, b3, c0, c1, c2, c3, *outs):
    total = (a[...].astype(f32) + a2[...].astype(f32)) + (b1[...].astype(f32) + b3[...].astype(f32))
    total = total.astype(bf16)
    for d in range(N_Y):
        outs[d][:ROW, :] = total
        cg = (c0[d].astype(f32) + c1[d].astype(f32)) + (c2[d].astype(f32) + c3[d].astype(f32))
        outs[d][ROW:, :] = cg.astype(bf16)


def combine(*args):
    return pl.pallas_call(
        combine_kernel,
        out_shape=(like(ROW + C_COLS, TOK),) * N_Y,
        in_specs=[vmem()] * 8,
        out_specs=(vmem(),) * N_Y,
        compiler_params=params(8),
        cost_estimate=cost(1024 * 1024),
        name="combine",
    )(*args)


def add(*parts):
    return sum(p.astype(f32) for p in parts).astype(bf16)


def per_device(queries, latent_rows, output_grad, up_query, up_key, up_value, block_order):
    coords = [lax.axis_index(a) for a in ("z", "xl", "core", "y", "xh")]
    place = jnp.stack(coords).astype(jnp.int32)
    z, xl, core = coords[:3]

    own = latent_rows.T
    q_other = shift(queries, dcore=1)
    do_other = shift(output_grad, dcore=1)
    across = shift(own, dxl=1)
    kts = [own, across]
    kts += [shift(own, dz=dz) for dz, _ in SLOTS[2:5]]
    kts += [shift(across, dz=dz) for dz, _ in SLOTS[5:]]

    first = (z * N_XL + xl) * 4
    near = lax.dynamic_slice(block_order, (first,), (4,))
    near = jnp.where(core == 0, near, jnp.roll(near, 2))
    token = jnp.arange(BLOCK, dtype=jnp.int32)
    pos = (near[:, None] * BLOCK + token).reshape(-1)
    frequency = 10000.0 ** (-(2.0 * jnp.arange(HALF, dtype=f32)) / D_ROPE)
    angles = pos.astype(f32)[None, :] * frequency[:, None]
    cos, sin = jnp.cos(angles), jnp.sin(angles)

    qt, gt = prologue(queries, q_other, output_grad, do_other, up_value)
    near, far = tuple(range(EARLY)), tuple(range(EARLY, SHARDS))
    *part0, kt0, m0, merged = scores(near, block_order, place, qt, gt, kts[:EARLY])
    *part1, kt1, m1, mine = scores(far, block_order, place, qt, gt, kts[EARLY:], (merged,))
    theirs = shift(mine, dcore=1)
    dk, dss = grads(((*part0, m0), (*part1, m1)), mine, theirs, qt, gt)

    from_z = [shift(dk[dz], dz=-dz) for dz in range(1, N_Z)]
    a, b = (add(*(p[i] for p in (dk[0], *from_z))) for i in range(N_XL))

    give_send, give_keep, send, keep = project(place, dss, (kt0, kt1), cos, sin, up_key, up_query)

    b1, b3, a2 = shift(b, dx=1), shift(b, dx=3), shift(a, dx=2)
    got = shift(send, dx=2), shift(give_keep, dcore=1), shift(give_send, dx=2, dcore=1)
    mix = combine(a, a2, b1, b3, keep, *got)
    s0, s1, s2, s3 = (shift(m, dy=d) if d else m for d, m in enumerate(mix))
    out = (s0.astype(f32) + s2.astype(f32)) + (s1.astype(f32) + s3.astype(f32))
    out = out.astype(bf16)
    return out[ROW:].T, out[:ROW].T


def solution(mesh):
    fine = Mesh(mesh.devices.reshape(N_Y, N_XH, N_Z, N_XL, 2), AXES)
    head, ctx = ("y", "xh"), ("z", "xl", "core")
    in_specs = (
        P(ctx, head),
        P(ctx, None),
        P(ctx, head),
        P(None, head),
        P(head, None, None),
        P(head, None, None),
        P(),
    )
    out_specs = (P(ctx, head), P(ctx, None))
    return jax.shard_map(
        per_device, mesh=fine, in_specs=in_specs, out_specs=out_specs, check_vma=False
    )
```

time: 314 us -> 80.4 us (0.26)
  waiting for transfers between devices: 219 us -> 17.5 us
  matrix products: 35.4 us -> 0 us
  starting transfers between devices: 0.38 us -> 32.8 us
  other arithmetic: 26.6 us -> 1.27 us
  Pallas kernels: 0 us -> 25.2 us
  local copies, waits for them, and re-layouts: 16.9 us -> 2.29 us
  between operations: 15.3 us -> 0.84 us
    psum x1 -> x0, waiting for transfers between devices: 84.8 us -> none  [per_device(): latent_grad = lax.psum(owned_sum, 'head')]
    reduce_scatter x1 -> x0, waiting for transfers between devices: 71.3 us -> none  [per_device(): lax.psum_scatter(partial_value.astype(jnp.bfloat16), 'head', scatter_dime...]
    unnamed x5 -> x0, waiting for transfers between devices: 56.8 us -> none
    dot_general x10 -> x0, matrix products: 35.4 us -> none  [the longest x2 12.1 us: block_scores(): jnp.einsum('thw,kw->htk', query_heads, key_block, preferred_element_type=...]
    ppermute x0 -> x22, starting transfers between devices: none -> 32.8 us  [shift(): return lax.ppermute(x, AXES, pairs)]
    pallas_call x0 -> x6, Pallas kernels: none -> 25.2 us  [the longest x2 11.3 us: scores(): pl.pallas_call(functools.partial(scores_kernel, slots), out_shape=(kept(n...]
    ppermute x0 -> x22, waiting for transfers between devices: none -> 17.5 us  [shift(): return lax.ppermute(x, AXES, pairs)]
    reduce_min x1 -> x0, other arithmetic: 16.1 us -> none  [grad_step(): jnp.min(key_pos) <= last_query]
  transfers between devices with their start and end apart: 4 -> 22, of which waited for: 4 -> 8; matrix products, arithmetic and copies ran while one was open for 13% -> 3% of each run, Pallas kernels for 0% -> 17%
where the time goes in v2:
time: 80.4 us; the launch traced here: 79.9 us
  starting transfers between devices  32.8 us (41%)
  Pallas kernels  25.2 us (31%)
  waiting for transfers between devices  17.5 us (22%)
  local copies, waits for them, and re-layouts  2.29 us (3%)
  other arithmetic  1.27 us (2%)
  between operations  0.84 us (1%)
    ppermute x22, starting transfers between devices, shift(): return lax.ppermute(x, AXES, pairs)  32.8 us
    ppermute x22, waiting for transfers between devices, shift(): return lax.ppermute(x, AXES, pairs)  17.5 us
    pallas_call x2, Pallas kernels, scores(): pl.pallas_call(functools.partial(scores_kernel, slots), out_shape=(kept(n...  11.3 us
    pallas_call x1, Pallas kernels, grads(): pl.pallas_call(functools.partial(grads_kernel, counts), out_shape=(pltpu....  5.97 us
    pallas_call x1, Pallas kernels, project(): pl.pallas_call(project_kernel, out_shape=(like(N_Y, C_COLS, TOK),) * 4, i...  5.24 us
    pallas_call x1, Pallas kernels, prologue(): pl.pallas_call(prologue_kernel, out_shape=(kept(ROW, ROWS), kept(D_LAT, R...  2.53 us
  transfers between devices with their start and end apart: 22, of which 8 were waited for; matrix products, arithmetic and copies ran while one was open for 3% of the time, Pallas kernels for 17%

profile of v2, /device:TPU:0, one launch (start us, length us, event | category | flops | bytes accessed | tf_op | source)
XLA Modules:
  0.0 79.9 jit_solution(16611369286948022020)
XLA Ops:
  0.7 1.7 %collective-permute-start.2 = (bf16[576,128]{1,0:T(8,128)(2,1)}, bf16[576,128]{1,0:T(8,128)(2,1)S(1)}, u32[]{:S(2)}, u32[]{:S(2)}) collective-permute-start(bf16[576,128]{1,0:T(8,128)(2,1)} %bitcast.16), channel_id=1, source_target_pairs={{0,2},{1,3},{2,0},{3,1},{4,6},{5,7},{6,4},{7,5},{8,10},{9,11},{10,... | collective-permute-start | bytes 442376 | tf_op jit(solution)/shard_map/ppermute | solution.py:60
  2.4 1.9 %collective-permute-start.3 = (bf16[576,128]{1,0:T(8,128)(2,1)}, bf16[576,128]{1,0:T(8,128)(2,1)S(1)}, u32[]{:S(2)}, u32[]{:S(2)}) collective-permute-start(bf16[576,128]{1,0:T(8,128)(2,1)} %bitcast.17), channel_id=1, source_target_pairs={{0,4},{1,5},{2,6},{3,7},{4,8},{5,9},{6,10},{7,11},{8,12},{9,13},{1... | collective-permute-start | bytes 442376 | tf_op jit(solution)/shard_map/ppermute | solution.py:60
  4.3 2.1 %collective-permute-start.4 = (bf16[576,128]{1,0:T(8,128)(2,1)}, bf16[576,128]{1,0:T(8,128)(2,1)S(1)}, u32[]{:S(2)}, u32[]{:S(2)}) collective-permute-start(bf16[576,128]{1,0:T(8,128)(2,1)} %bitcast.18), channel_id=1, source_target_pairs={{0,12},{1,13},{2,14},{3,15},{4,0},{5,1},{6,2},{7,3},{8,4},{9,5},{1... | collective-permute-start | bytes 442376 | tf_op jit(solution)/shard_map/ppermute | solution.py:60
  6.4 0.7 dynamic_slice.3
  7.2 0.7 fusion.2
  8.2 3.0 %collective-permute-start.5 = (bf16[576,128]{1,0:T(8,128)(2,1)}, bf16[576,128]{1,0:T(8,128)(2,1)S(1)}, u32[]{:S(2)}, u32[]{:S(2)}) collective-permute-start(bf16[576,128]{1,0:T(8,128)(2,1)} %bitcast.19), channel_id=1, source_target_pairs={{0,8},{1,9},{2,10},{3,11},{4,12},{5,13},{6,14},{7,15},{8,0},{9,1},... | collective-permute-start | bytes 442376 | tf_op jit(solution)/shard_map/ppermute | solution.py:60
  11.2 1.0 %collective-permute-start.6 = (bf16[576,128]{1,0:T(8,128)(2,1)S(1)}, bf16[576,128]{1,0:T(8,128)(2,1)S(1)}, u32[]{:S(2)}, u32[]{:S(2)}) collective-permute-start(bf16[576,128]{1,0:T(8,128)(2,1)S(1)} %collective-permute-done.2.refs_1_), channel_id=1, source_target_pairs={{0,4},{1,5},{2,6},{3,7},{4,8},{5,9},{6,10},{7,11},{8,12},{9,13},{1... | collective-permute-start | bytes 442376 | tf_op jit(solution)/shard_map/ppermute | solution.py:60
  12.2 2.2 %collective-permute-start.7 = (bf16[576,128]{1,0:T(8,128)(2,1)S(1)}, bf16[576,128]{1,0:T(8,128)(2,1)S(1)}, u32[]{:S(2)}, u32[]{:S(2)}) collective-permute-start(bf16[576,128]{1,0:T(8,128)(2,1)S(1)} %collective-permute-done.2.refs_1_), channel_id=1, source_target_pairs={{0,12},{1,13},{2,14},{3,15},{4,0},{5,1},{6,2},{7,3},{8,4},{9,5},{1... | collective-permute-start | bytes 442376 | tf_op jit(solution)/shard_map/ppermute | solution.py:60
  14.4 2.5 %prologue.1 = (bf16[576,2048]{1,0:T(8,128)(2,1)S(1)}, bf16[512,2048]{1,0:T(8,128)(2,1)S(1)}) custom-call(bf16[128,4608]{1,0:T(8,128)(2,1)} %q0.1, bf16[128,4608]{1,0:T(8,128)(2,1)S(1)} %collective-permute-done.q1, bf16[128,1024]{1,0:T(8,128)(2,1)} %do0.1, bf16[128,1024]{1,0:T(8,128)(2,1)S(1)} %collective-permute-done.1.do1, bf16[8,512,128]{2,1,0:T(8,128)(2,1)} %uv_hbm.1), custom_call_target="tpu_custom_call" | custom-call | flops 268435456 | bytes 1048576 | tf_op jit(solution)/shard_map/prologue/pallas_call | solution.py:132
  17.1 5.6 %scores.2 = (bf16[512,2048]{1,0:T(8,128)(2,1)S(1)}, bf16[512,2048]{1,0:T(8,128)(2,1)S(1)}, bf16[576,512]{1,0:T(8,128)(2,1)S(1)}, f32[8,2048]{1,0:T(8,128)S(1)}, f32[8,2048]{1,0:T(8,128)S(1)}) custom-call(s32[32]{0:T(128)S(1)} %copy-done.1, s32[5]{0:T(128)S(1)} %stack.23.place, bf16[576,2048]{1,0:T(8,128)(2,1)S(1)} %get-tuple-element.28.qt.refs_8_, ...), custom_call_target="tpu_custom_call" | custom-call | flops 2281701376 | bytes 1048576 | tf_op jit(solution)/shard_map/scores/pallas_call | solution.py:219
  22.8 0.9 %collective-permute-done.8.refs_3_ = bf16[576,128]{1,0:T(8,128)(2,1)S(1)} collective-permute-done((bf16[576,128]{1,0:T(8,128)(2,1)S(1)}, bf16[576,128]{1,0:T(8,128)(2,1)S(1)}, u32[]{:S(2)}, u32[]{:S(2)}) %collective-permute-start.8) | collective-permute-done | bytes 147488 | tf_op jit(solution)/shard_map/ppermute | solution.py:60
  23.7 5.6 %scores.3 = (bf16[512,2048]{1,0:T(8,128)(2,1)S(1)}, bf16[512,2048]{1,0:T(8,128)(2,1)S(1)}, bf16[576,512]{1,0:T(8,128)(2,1)S(1)}, f32[8,2048]{1,0:T(8,128)S(1)}, f32[8,2048]{1,0:T(8,128)S(1)}) custom-call(s32[32]{0:T(128)S(1)} %copy-done.1, s32[5]{0:T(128)S(1)} %stack.23.place, bf16[576,2048]{1,0:T(8,128)(2,1)S(1)} %get-tuple-element.28.qt.refs_8_, ...), custom_call_target="tpu_custom_call" | custom-call | flops 2281701376 | bytes 1048576 | tf_op jit(solution)/shard_map/scores/pallas_call | solution.py:219
  29.4 1.2 %collective-permute-done.9.refs_7_ = f32[8,2048]{1,0:T(8,128)S(1)} collective-permute-done((f32[8,2048]{1,0:T(8,128)S(1)}, f32[8,2048]{1,0:T(8,128)S(1)}, u32[]{:S(2)}, u32[]{:S(2)}) %collective-permute-start.9) | collective-permute-done | bytes 65568 | tf_op jit(solution)/shard_map/ppermute | solution.py:60
  30.7 6.0 %grads.1 = (bf16[2,576,128]{2,1,0:T(8,128)(2,1)}, bf16[2,576,128]{2,1,0:T(8,128)(2,1)}, bf16[2,576,128]{2,1,0:T(8,128)(2,1)}, bf16[2,576,128]{2,1,0:T(8,128)(2,1...) custom-call(bf16[512,2048]{1,0:T(8,128)(2,1)S(1)} %get-tuple-element.30.refs_0_, ...), custom_call_target="tpu_custom_call" | custom-call | flops 4563402752 | bytes 1048576 | tf_op jit(solution)/shard_map/grads/pallas_call | solution.py:291
  36.6 1.6 %collective-permute-start.10 = (bf16[2,576,128]{2,1,0:T(8,128)(2,1)}, bf16[2,576,128]{2,1,0:T(8,128)(2,1)S(1)}, u32[]{:S(2)}, u32[]{:S(2)}) collective-permute-start(bf16[2,576,128]{2,1,0:T(8,128)(2,1)} %get-tuple-element.39), channel_id=1, source_target_pairs={{0,12},{1,13},{2,14},{3,15},{4,0},{5,1},{6,2},{7,3},{8,4},{9,5},{1... | collective-permute-start | bytes 884744 | tf_op jit(solution)/shard_map/ppermute | solution.py:60
  38.3 1.1 %collective-permute-start.11 = (bf16[2,576,128]{2,1,0:T(8,128)(2,1)}, bf16[2,576,128]{2,1,0:T(8,128)(2,1)S(1)}, u32[]{:S(2)}, u32[]{:S(2)}) collective-permute-start(bf16[2,576,128]{2,1,0:T(8,128)(2,1)} %get-tuple-element.40), channel_id=1, source_target_pairs={{0,8},{1,9},{2,10},{3,11},{4,12},{5,13},{6,14},{7,15},{8,0},{9,1},... | collective-permute-start | bytes 884744 | tf_op jit(solution)/shard_map/ppermute | solution.py:60
  39.4 1.3 %collective-permute-start.12 = (bf16[2,576,128]{2,1,0:T(8,128)(2,1)}, bf16[2,576,128]{2,1,0:T(8,128)(2,1)S(1)}, u32[]{:S(2)}, u32[]{:S(2)}) collective-permute-start(bf16[2,576,128]{2,1,0:T(8,128)(2,1)} %get-tuple-element.41), channel_id=1, source_target_pairs={{0,4},{1,5},{2,6},{3,7},{4,8},{5,9},{6,10},{7,11},{8,12},{9,13},{1... | collective-permute-start | bytes 884744 | tf_op jit(solution)/shard_map/ppermute | solution.py:60
  41.0 5.2 %project.1 = (bf16[4,192,128]{2,1,0:T(8,128)(2,1)S(1)}, bf16[4,192,128]{2,1,0:T(8,128)(2,1)S(1)}, bf16[4,192,128]{2,1,0:T(8,128)(2,1)S(1)}, bf16[4,192,128]{2,1,0:T(8,128)(2,1)S(1)}) custom-call(s32[5]{0:T(128)S(1)} %stack.23.place, bf16[8,128,512]{2,1,0:T(8,128)(2,1)S(1)} %copy-done, bf16[1536,1536]{1,0:T(8,128)(2,1)S(1)} %bitcast.15, ...), custom_call_target="tpu_custom_call" | custom-call | flops 2415919104 | bytes 1048576 | tf_op jit(solution)/shard_map/project/pallas_call | solution.py:341
  46.2 3.1 %collective-permute-start.16 = (bf16[4,192,128]{2,1,0:T(8,128)(2,1)S(1)}, bf16[4,192,128]{2,1,0:T(8,128)(2,1)S(1)}, u32[]{:S(2)}, u32[]{:S(2)}) collective-permute-start(bf16[4,192,128]{2,1,0:T(8,128)(2,1)S(1)} %get-tuple-element.47), channel_id=1, source_target_pairs={{0,16},{1,17},{2,18},{3,19},{4,20},{5,21},{6,22},{7,23},{8,24},{9,... | collective-permute-start | bytes 589832 | tf_op jit(solution)/shard_map/ppermute | solution.py:60
  49.3 0.6 collective-permute-start.18
  50.0 5.1 %collective-permute-done.12 = bf16[2,576,128]{2,1,0:T(8,128)(2,1)S(1)} collective-permute-done((bf16[2,576,128]{2,1,0:T(8,128)(2,1)}, bf16[2,576,128]{2,1,0:T(8,128)(2,1)S(1)}, u32[]{:S(2)}, u32[]{:S(2)}) %collective-permute-start.12) | collective-permute-done | bytes 294944 | tf_op jit(solution)/shard_map/ppermute | solution.py:60
  55.3 3.1 %collective-permute-start.13 = (bf16[576,128]{1,0:T(8,128)(2,1)S(1)}, bf16[576,128]{1,0:T(8,128)(2,1)S(1)}, u32[]{:S(2)}, u32[]{:S(2)}) collective-permute-start(bf16[576,128]{1,0:T(8,128)(2,1)S(1)} %get-tuple-element.55.a), channel_id=1, source_target_pairs={{0,16},{1,17},{2,18},{3,19},{4,20},{5,21},{6,22},{7,23},{8,24},{9,... | collective-permute-start | bytes 442376 | tf_op jit(solution)/shard_map/ppermute | solution.py:60
  58.9 2.6 %collective-permute-start.15 = (bf16[576,128]{1,0:T(8,128)(2,1)S(1)}, bf16[576,128]{1,0:T(8,128)(2,1)S(1)}, u32[]{:S(2)}, u32[]{:S(2)}) collective-permute-start(bf16[576,128]{1,0:T(8,128)(2,1)S(1)} %get-tuple-element.54), channel_id=1, source_target_pairs={{0,18},{1,19},{2,0},{3,1},{4,22},{5,23},{6,4},{7,5},{8,26},{9,27},... | collective-permute-start | bytes 442376 | tf_op jit(solution)/shard_map/ppermute | solution.py:60
  61.6 1.9 %collective-permute-done.13.a2 = bf16[576,128]{1,0:T(8,128)(2,1)S(1)} collective-permute-done((bf16[576,128]{1,0:T(8,128)(2,1)S(1)}, bf16[576,128]{1,0:T(8,128)(2,1)S(1)}, u32[]{:S(2)}, u32[]{:S(2)}) %collective-permute-start.13) | collective-permute-done | bytes 147488 | tf_op jit(solution)/shard_map/ppermute | solution.py:60
  63.6 2.3 %collective-permute-done.14.b1 = bf16[576,128]{1,0:T(8,128)(2,1)S(1)} collective-permute-done((bf16[576,128]{1,0:T(8,128)(2,1)S(1)}, bf16[576,128]{1,0:T(8,128)(2,1)S(1)}, u32[]{:S(2)}, u32[]{:S(2)}) %collective-permute-start.14) | collective-permute-done | bytes 147488 | tf_op jit(solution)/shard_map/ppermute | solution.py:60
  66.1 3.3 %collective-permute-start.19 = (bf16[768,128]{1,0:T(8,128)(2,1)S(1)}, bf16[768,128]{1,0:T(8,128)(2,1)S(1)}, u32[]{:S(2)}, u32[]{:S(2)}) collective-permute-start(bf16[768,128]{1,0:T(8,128)(2,1)S(1)} %get-tuple-element.51), channel_id=1, source_target_pairs={{0,64},{1,65},{2,66},{3,67},{4,68},{5,69},{6,70},{7,71},{8,72},{9,... | collective-permute-start | bytes 589832 | tf_op jit(solution)/shard_map/ppermute | solution.py:60
  69.3 0.7 collective-permute-start.20
  70.0 2.6 %collective-permute-start.21 = (bf16[768,128]{1,0:T(8,128)(2,1)S(1)}, bf16[768,128]{1,0:T(8,128)(2,1)S(1)}, u32[]{:S(2)}, u32[]{:S(2)}) collective-permute-start(bf16[768,128]{1,0:T(8,128)(2,1)S(1)} %get-tuple-element.53), channel_id=1, source_target_pairs={{0,96},{1,97},{2,98},{3,99},{4,100},{5,101},{6,102},{7,103},{8,104... | collective-permute-start | bytes 589832 | tf_op jit(solution)/shard_map/ppermute | solution.py:60
  72.6 2.9 %collective-permute-done.19 = bf16[768,128]{1,0:T(8,128)(2,1)S(1)} collective-permute-done((bf16[768,128]{1,0:T(8,128)(2,1)S(1)}, bf16[768,128]{1,0:T(8,128)(2,1)S(1)}, u32[]{:S(2)}, u32[]{:S(2)}) %collective-permute-start.19) | collective-permute-done | bytes 196640 | tf_op jit(solution)/shard_map/ppermute | solution.py:60
  75.5 2.6 %collective-permute-done.20 = bf16[768,128]{1,0:T(8,128)(2,1)S(1)} collective-permute-done((bf16[768,128]{1,0:T(8,128)(2,1)S(1)}, bf16[768,128]{1,0:T(8,128)(2,1)S(1)}, u32[]{:S(2)}, u32[]{:S(2)}) %collective-permute-start.20) | collective-permute-done | bytes 196640 | tf_op jit(solution)/shard_map/ppermute | solution.py:60
  78.6 0.7 slice_bitcast_fusion
  79.2 0.6 slice_bitcast_fusion.1
  (43 shorter events, 2.2 us)
Async XLA Ops:
  0.6 16.4 %copy-start.2 = (bf16[128,576]{0,1:T(8,128)(2,1)S(1)}, bf16[128,576]{0,1:T(8,128)(2,1)}, u32[]{:S(2)}) copy-start(bf16[128,576]{0,1:T(8,128)(2,1)} %param.8) | copy-start | bytes 442372
  0.6 16.4 %copy-start.1 = (s32[32]{0:T(128)S(1)}, s32[32]{0:T(128)}, u32[]{:S(2)}) copy-start(s32[32]{0:T(128)} %order.3) | copy-start | bytes 388
  0.7 11.6 %collective-permute-start = (bf16[128,4608]{1,0:T(8,128)(2,1)}, bf16[128,4608]{1,0:T(8,128)(2,1)S(1)}, u32[]{:S(2)}, u32[]{:S(2)}) collective-permute-start(bf16[128,4608]{1,0:T(8,128)(2,1)} %q0.1), channel_id=1, source_target_pairs={{0,1},{1,0},{2,3},{3,2},{4,5},{5,4},{6,7},{7,6},{8,9},{9,8},{10,11... | collective-permute-start | bytes 3538952 | tf_op jit(solution)/shard_map/ppermute | solution.py:60
  0.7 7.5 %collective-permute-start.2 = (bf16[576,128]{1,0:T(8,128)(2,1)}, bf16[576,128]{1,0:T(8,128)(2,1)S(1)}, u32[]{:S(2)}, u32[]{:S(2)}) collective-permute-start(bf16[576,128]{1,0:T(8,128)(2,1)} %bitcast.16), channel_id=1, source_target_pairs={{0,2},{1,3},{2,0},{3,1},{4,6},{5,7},{6,4},{7,5},{8,10},{9,11},{10,... | collective-permute-start | bytes 442376 | tf_op jit(solution)/shard_map/ppermute | solution.py:60
  2.4 14.6 %collective-permute-start.3 = (bf16[576,128]{1,0:T(8,128)(2,1)}, bf16[576,128]{1,0:T(8,128)(2,1)S(1)}, u32[]{:S(2)}, u32[]{:S(2)}) collective-permute-start(bf16[576,128]{1,0:T(8,128)(2,1)} %bitcast.17), channel_id=1, source_target_pairs={{0,4},{1,5},{2,6},{3,7},{4,8},{5,9},{6,10},{7,11},{8,12},{9,13},{1... | collective-permute-start | bytes 442376 | tf_op jit(solution)/shard_map/ppermute | solution.py:60
  4.3 12.7 %collective-permute-start.4 = (bf16[576,128]{1,0:T(8,128)(2,1)}, bf16[576,128]{1,0:T(8,128)(2,1)S(1)}, u32[]{:S(2)}, u32[]{:S(2)}) collective-permute-start(bf16[576,128]{1,0:T(8,128)(2,1)} %bitcast.18), channel_id=1, source_target_pairs={{0,12},{1,13},{2,14},{3,15},{4,0},{5,1},{6,2},{7,3},{8,4},{9,5},{1... | collective-permute-start | bytes 442376 | tf_op jit(solution)/shard_map/ppermute | solution.py:60
  6.4 4.7 %collective-permute-start.1 = (bf16[128,1024]{1,0:T(8,128)(2,1)}, bf16[128,1024]{1,0:T(8,128)(2,1)S(1)}, u32[]{:S(2)}, u32[]{:S(2)}) collective-permute-start(bf16[128,1024]{1,0:T(8,128)(2,1)} %do0.1), channel_id=1, source_target_pairs={{0,1},{1,0},{2,3},{3,2},{4,5},{5,4},{6,7},{7,6},{8,9},{9,8},{10,11... | collective-permute-start | bytes 786440 | tf_op jit(solution)/shard_map/ppermute | solution.py:60
  8.2 14.5 %collective-permute-start.5 = (bf16[576,128]{1,0:T(8,128)(2,1)}, bf16[576,128]{1,0:T(8,128)(2,1)S(1)}, u32[]{:S(2)}, u32[]{:S(2)}) collective-permute-start(bf16[576,128]{1,0:T(8,128)(2,1)} %bitcast.19), channel_id=1, source_target_pairs={{0,8},{1,9},{2,10},{3,11},{4,12},{5,13},{6,14},{7,15},{8,0},{9,1},... | collective-permute-start | bytes 442376 | tf_op jit(solution)/shard_map/ppermute | solution.py:60
  11.2 11.6 %collective-permute-start.6 = (bf16[576,128]{1,0:T(8,128)(2,1)S(1)}, bf16[576,128]{1,0:T(8,128)(2,1)S(1)}, u32[]{:S(2)}, u32[]{:S(2)}) collective-permute-start(bf16[576,128]{1,0:T(8,128)(2,1)S(1)} %collective-permute-done.2.refs_1_), channel_id=1, source_target_pairs={{0,4},{1,5},{2,6},{3,7},{4,8},{5,9},{6,10},{7,11},{8,12},{9,13},{1... | collective-permute-start | bytes 442376 | tf_op jit(solution)/shard_map/ppermute | solution.py:60
  12.2 10.5 %collective-permute-start.7 = (bf16[576,128]{1,0:T(8,128)(2,1)S(1)}, bf16[576,128]{1,0:T(8,128)(2,1)S(1)}, u32[]{:S(2)}, u32[]{:S(2)}) collective-permute-start(bf16[576,128]{1,0:T(8,128)(2,1)S(1)} %collective-permute-done.2.refs_1_), channel_id=1, source_target_pairs={{0,12},{1,13},{2,14},{3,15},{4,0},{5,1},{6,2},{7,3},{8,4},{9,5},{1... | collective-permute-start | bytes 442376 | tf_op jit(solution)/shard_map/ppermute | solution.py:60
  17.0 6.7 %collective-permute-start.8 = (bf16[576,128]{1,0:T(8,128)(2,1)S(1)}, bf16[576,128]{1,0:T(8,128)(2,1)S(1)}, u32[]{:S(2)}, u32[]{:S(2)}) collective-permute-start(bf16[576,128]{1,0:T(8,128)(2,1)S(1)} %collective-permute-done.2.refs_1_), channel_id=1, source_target_pairs={{0,8},{1,9},{2,10},{3,11},{4,12},{5,13},{6,14},{7,15},{8,0},{9,1},... | collective-permute-start | bytes 442376 | tf_op jit(solution)/shard_map/ppermute | solution.py:60
  29.3 1.3 %collective-permute-start.9 = (f32[8,2048]{1,0:T(8,128)S(1)}, f32[8,2048]{1,0:T(8,128)S(1)}, u32[]{:S(2)}, u32[]{:S(2)}) collective-permute-start(f32[8,2048]{1,0:T(8,128)S(1)} %get-tuple-element.37.refs_6_), channel_id=1, source_target_pairs={{0,1},{1,0},{2,3},{3,2},{4,5},{5,4},{6,7},{7,6},{8,9},{9,8},{10,11... | collective-permute-start | bytes 196616 | tf_op jit(solution)/shard_map/ppermute | solution.py:60
  30.7 10.3 %slice-start = ((s8[4718592]{0:T(1024)(128)(4,1)}), s8[4194304]{0:T(1024)(128)(4,1)S(1)}, s32[]{:S(2)}) async-start(s8[4718592]{0:T(1024)(128)(4,1)} %bitcast.14), calls=%async_computation | async-start | bytes 8388608
  30.7 10.3 %slice-start.1 = ((s8[4718592]{0:T(1024)(128)(4,1)}), s8[524288]{0:T(1024)(128)(4,1)S(1)}, s32[]{:S(2)}) async-start(s8[4718592]{0:T(1024)(128)(4,1)} %bitcast.14), calls=%async_computation.1 | async-start | bytes 1048576
  30.7 10.3 %copy-start = (bf16[8,128,512]{2,1,0:T(8,128)(2,1)S(1)}, bf16[8,128,512]{2,1,0:T(8,128)(2,1)}, u32[]{:S(2)}) copy-start(bf16[8,128,512]{2,1,0:T(8,128)(2,1)} %uk.1) | copy-start | bytes 3145732
  36.6 12.7 %collective-permute-start.10 = (bf16[2,576,128]{2,1,0:T(8,128)(2,1)}, bf16[2,576,128]{2,1,0:T(8,128)(2,1)S(1)}, u32[]{:S(2)}, u32[]{:S(2)}) collective-permute-start(bf16[2,576,128]{2,1,0:T(8,128)(2,1)} %get-tuple-element.39), channel_id=1, source_target_pairs={{0,12},{1,13},{2,14},{3,15},{4,0},{5,1},{6,2},{7,3},{8,4},{9,5},{1... | collective-permute-start | bytes 884744 | tf_op jit(solution)/shard_map/ppermute | solution.py:60
  38.3 11.7 %collective-permute-start.11 = (bf16[2,576,128]{2,1,0:T(8,128)(2,1)}, bf16[2,576,128]{2,1,0:T(8,128)(2,1)S(1)}, u32[]{:S(2)}, u32[]{:S(2)}) collective-permute-start(bf16[2,576,128]{2,1,0:T(8,128)(2,1)} %get-tuple-element.40), channel_id=1, source_target_pairs={{0,8},{1,9},{2,10},{3,11},{4,12},{5,13},{6,14},{7,15},{8,0},{9,1},... | collective-permute-start | bytes 884744 | tf_op jit(solution)/shard_map/ppermute | solution.py:60
  39.4 15.7 %collective-permute-start.12 = (bf16[2,576,128]{2,1,0:T(8,128)(2,1)}, bf16[2,576,128]{2,1,0:T(8,128)(2,1)S(1)}, u32[]{:S(2)}, u32[]{:S(2)}) collective-permute-start(bf16[2,576,128]{2,1,0:T(8,128)(2,1)} %get-tuple-element.41), channel_id=1, source_target_pairs={{0,4},{1,5},{2,6},{3,7},{4,8},{5,9},{6,10},{7,11},{8,12},{9,13},{1... | collective-permute-start | bytes 884744 | tf_op jit(solution)/shard_map/ppermute | solution.py:60
  41.0 14.1 %copy-start.3 = (bf16[2,576,128]{2,1,0:T(8,128)(2,1)S(1)}, bf16[2,576,128]{2,1,0:T(8,128)(2,1)}, u32[]{:S(2)}) copy-start(bf16[2,576,128]{2,1,0:T(8,128)(2,1)} %get-tuple-element.38) | copy-start | bytes 884740
  46.2 12.7 %collective-permute-start.16 = (bf16[4,192,128]{2,1,0:T(8,128)(2,1)S(1)}, bf16[4,192,128]{2,1,0:T(8,128)(2,1)S(1)}, u32[]{:S(2)}, u32[]{:S(2)}) collective-permute-start(bf16[4,192,128]{2,1,0:T(8,128)(2,1)S(1)} %get-tuple-element.47), channel_id=1, source_target_pairs={{0,16},{1,17},{2,18},{3,19},{4,20},{5,21},{6,22},{7,23},{8,24},{9,... | collective-permute-start | bytes 589832 | tf_op jit(solution)/shard_map/ppermute | solution.py:60
  49.3 12.3 %collective-permute-start.17 = (bf16[4,192,128]{2,1,0:T(8,128)(2,1)S(1)}, bf16[4,192,128]{2,1,0:T(8,128)(2,1)S(1)}, u32[]{:S(2)}, u32[]{:S(2)}) collective-permute-start(bf16[4,192,128]{2,1,0:T(8,128)(2,1)S(1)} %get-tuple-element.48), channel_id=1, source_target_pairs={{0,1},{1,0},{2,3},{3,2},{4,5},{5,4},{6,7},{7,6},{8,9},{9,8},{10,11... | collective-permute-start | bytes 589832 | tf_op jit(solution)/shard_map/ppermute | solution.py:60
  49.3 12.3 %collective-permute-start.18 = (bf16[4,192,128]{2,1,0:T(8,128)(2,1)S(1)}, bf16[4,192,128]{2,1,0:T(8,128)(2,1)S(1)}, u32[]{:S(2)}, u32[]{:S(2)}) collective-permute-start(bf16[4,192,128]{2,1,0:T(8,128)(2,1)S(1)} %get-tuple-element.49), channel_id=1, source_target_pairs={{0,17},{1,16},{2,19},{3,18},{4,21},{5,20},{6,23},{7,22},{8,25},{9,... | collective-permute-start | bytes 589832 | tf_op jit(solution)/shard_map/ppermute | solution.py:60
  55.3 8.3 %collective-permute-start.13 = (bf16[576,128]{1,0:T(8,128)(2,1)S(1)}, bf16[576,128]{1,0:T(8,128)(2,1)S(1)}, u32[]{:S(2)}, u32[]{:S(2)}) collective-permute-start(bf16[576,128]{1,0:T(8,128)(2,1)S(1)} %get-tuple-element.55.a), channel_id=1, source_target_pairs={{0,16},{1,17},{2,18},{3,19},{4,20},{5,21},{6,22},{7,23},{8,24},{9,... | collective-permute-start | bytes 442376 | tf_op jit(solution)/shard_map/ppermute | solution.py:60
  58.4 7.5 %collective-permute-start.14 = (bf16[576,128]{1,0:T(8,128)(2,1)S(1)}, bf16[576,128]{1,0:T(8,128)(2,1)S(1)}, u32[]{:S(2)}, u32[]{:S(2)}) collective-permute-start(bf16[576,128]{1,0:T(8,128)(2,1)S(1)} %get-tuple-element.54), channel_id=1, source_target_pairs={{0,2},{1,3},{2,16},{3,17},{4,6},{5,7},{6,20},{7,21},{8,10},{9,11},... | collective-permute-start | bytes 442376 | tf_op jit(solution)/shard_map/ppermute | solution.py:60
  58.9 6.9 %collective-permute-start.15 = (bf16[576,128]{1,0:T(8,128)(2,1)S(1)}, bf16[576,128]{1,0:T(8,128)(2,1)S(1)}, u32[]{:S(2)}, u32[]{:S(2)}) collective-permute-start(bf16[576,128]{1,0:T(8,128)(2,1)S(1)} %get-tuple-element.54), channel_id=1, source_target_pairs={{0,18},{1,19},{2,0},{3,1},{4,22},{5,23},{6,4},{7,5},{8,26},{9,27},... | collective-permute-start | bytes 442376 | tf_op jit(solution)/shard_map/ppermute | solution.py:60
  66.1 9.4 %collective-permute-start.19 = (bf16[768,128]{1,0:T(8,128)(2,1)S(1)}, bf16[768,128]{1,0:T(8,128)(2,1)S(1)}, u32[]{:S(2)}, u32[]{:S(2)}) collective-permute-start(bf16[768,128]{1,0:T(8,128)(2,1)S(1)} %get-tuple-element.51), channel_id=1, source_target_pairs={{0,64},{1,65},{2,66},{3,67},{4,68},{5,69},{6,70},{7,71},{8,72},{9,... | collective-permute-start | bytes 589832 | tf_op jit(solution)/shard_map/ppermute | solution.py:60
  69.3 8.8 %collective-permute-start.20 = (bf16[768,128]{1,0:T(8,128)(2,1)S(1)}, bf16[768,128]{1,0:T(8,128)(2,1)S(1)}, u32[]{:S(2)}, u32[]{:S(2)}) collective-permute-start(bf16[768,128]{1,0:T(8,128)(2,1)S(1)} %get-tuple-element.52), channel_id=1, source_target_pairs={{0,32},{1,33},{2,34},{3,35},{4,36},{5,37},{6,38},{7,39},{8,40},{9,... | collective-permute-start | bytes 589832 | tf_op jit(solution)/shard_map/ppermute | solution.py:60
  70.0 8.5 %collective-permute-start.21 = (bf16[768,128]{1,0:T(8,128)(2,1)S(1)}, bf16[768,128]{1,0:T(8,128)(2,1)S(1)}, u32[]{:S(2)}, u32[]{:S(2)}) collective-permute-start(bf16[768,128]{1,0:T(8,128)(2,1)S(1)} %get-tuple-element.53), channel_id=1, source_target_pairs={{0,96},{1,97},{2,98},{3,99},{4,100},{5,101},{6,102},{7,103},{8,104... | collective-permute-start | bytes 589832 | tf_op jit(solution)/shard_map/ppermute | solution.py:60

commit v3 on v2

--- a/solution.py
+++ b/solution.py
@@ -2,6 +2,7 @@
 
 import jax
 import jax.numpy as jnp
+import numpy as np
 from jax import lax
 from jax.experimental import pallas as pl
 from jax.experimental.pallas import tpu as pltpu
@@ -31,8 +32,8 @@
 AXES = ("y", "xh", "z", "xl", "core")
 TN = 256
 
-SLOTS = ((0, 0), (0, 1), (1, 0), (3, 0), (2, 0), (1, 1), (3, 1), (2, 1))
-EARLY = 4
+SLOTS = ((0, 0), (1, 0), (3, 0), (2, 0), (0, 1), (1, 1), (3, 1), (2, 1))
+GROUPS = ((0, 1, 2, 3), (4, 5), (6, 7))
 
 NT = (((1,), (1,)), ((), ()))
 NN = (((1,), (0,)), ((), ()))
@@ -96,7 +97,7 @@
     return pltpu.with_memory_space_constraint(x, pltpu.HBM)
 
 
-def prologue_kernel(q0, q1, do0, do1, uv_hbm, qt, gt, q_own, do_own, uv, sems):
+def prologue_kernel(q0, q1, do0, do1, uv_hbm, qt, gt, done, q_own, do_own, uv, sems):
     copies = [
         pltpu.make_async_copy(src, dst, sems.at[i])
         for i, (src, dst) in enumerate(((uv_hbm, uv), (do0, do_own), (q0, q_own)))
@@ -126,14 +127,15 @@
     value_grad(0, do_own)
     copies[2].wait()
     transpose(0, q_own)
+    done[...] = jnp.zeros_like(done)
 
 
 def prologue(q0, q1, do0, do1, uv):
     return pl.pallas_call(
         prologue_kernel,
-        out_shape=(kept(ROW, ROWS), kept(D_LAT, ROWS)),
+        out_shape=(kept(ROW, ROWS), kept(D_LAT, ROWS), like(8, 128, dtype=f32)),
         in_specs=[hbm(), vmem(), hbm(), vmem(), hbm()],
-        out_specs=(vmem(), vmem()),
+        out_specs=(vmem(),) * 3,
         scratch_shapes=[
             pltpu.VMEM(q0.shape, bf16),
             pltpu.VMEM(do0.shape, bf16),
@@ -176,9 +178,8 @@
                 at = i * TOK + b * BLOCK
                 bias[t, at : at + BLOCK, :] = jnp.where(k_pos <= q_pos, 0.0, MASKED)
 
-    @pl.loop(0, ROWS // TN)
-    def _(step):
-        base = pl.multiple_of(step * TN, TN)
+    for step in range(ROWS // TN):
+        base = step * TN
         token_set = step // (HROWS // TN)
         q, g = qt[:, pl.ds(base, TN)], gt[:, pl.ds(base, TN)]
         halves = TN // TOK
@@ -308,11 +309,17 @@
     return res[:N_Z], res[N_Z:]
 
 
-def project_kernel(place, uk, uq, cos, sin, *refs):
+def project_kernel(order, place, uk, uq, frequency, *refs):
     n = (len(refs) - 6) // 2
+    lane = lax.broadcasted_iota(jnp.int32, (HALF, TOK), 1)
     dss, kts = refs[:n], refs[n : 2 * n]
-    give_send, give_keep, send, keep, ft, cg = refs[2 * n :]
+    outs, (ft, cg) = refs[2 * n : -2], refs[-2:]
     for t in (1, 0):
+        c = place[2] if t == 0 else 1 - place[2]
+        at = ((place[0] * N_XL + place[1]) * 2 + c) * 2
+        block = jnp.where(lane < BLOCK, order[at], order[at + 1])
+        angle = (block * BLOCK + lane % BLOCK).astype(f32) * frequency[...]
+        cos, sin = jnp.cos(angle), jnp.sin(angle)
         half = slice(t * HROWS, (t + 1) * HROWS)
         dq = sum(dot(kt[...], ds[:, half]) for kt, ds in zip(kts, dss)).astype(bf16)
         out = slice(t * TOK, (t + 1) * TOK)
@@ -323,52 +330,52 @@
             a = d[D_LAT : D_LAT + HALF].astype(f32)
             b = d[D_LAT + HALF :].astype(f32)
             base += D_NOPE
-            c, s = cos[:, out], sin[:, out]
-            ft[base : base + HALF, out] = (a * c + b * s).astype(bf16)
-            ft[base + HALF : base + D_ROPE, out] = (b * c - a * s).astype(bf16)
+            ft[base : base + HALF, out] = (a * cos + b * sin).astype(bf16)
+            ft[base + HALF : base + D_ROPE, out] = (b * cos - a * sin).astype(bf16)
     cg[...] = dot(uq[...], ft[...]).astype(bf16)
     y, xh = place[3], place[4]
     for d in range(N_Y):
         yd = lax.rem(y + d, N_Y)
-        away = pl.ds(pl.multiple_of((yd * 2 + 1 - xh) * C_COLS, 64), C_COLS)
-        here = pl.ds(pl.multiple_of((yd * 2 + xh) * C_COLS, 64), C_COLS)
-        send[d], keep[d] = cg[away, :TOK], cg[here, :TOK]
-        give_send[d], give_keep[d] = cg[away, TOK:], cg[here, TOK:]
-
-
-def project(place, dss, kts, cos, sin, uk, uq):
+        for k, h in enumerate((xh, 1 - xh)):
+            rows = pl.ds(pl.multiple_of((yd * N_XH + h) * C_COLS, 64), C_COLS)
+            for t in range(2):
+                outs[d][t, k] = cg[rows, t * TOK : (t + 1) * TOK]
+
+
+def project(order, place, dss, kts, uk, uq):
+    k = np.arange(HALF, dtype=np.float32)[:, None]
+    frequency = np.float32(10000.0) ** (-(2.0 * k) / D_ROPE)
+    frequency = jnp.asarray(np.broadcast_to(frequency, (HALF, TOK)), f32)
     q_rank = uq.shape[0]
     return pl.pallas_call(
         project_kernel,
-        out_shape=(like(N_Y, C_COLS, TOK),) * 4,
-        in_specs=[smem()] + [vmem()] * (4 + 2 * len(dss)),
+        out_shape=(like(2, N_XH, C_COLS, TOK),) * N_Y,
+        in_specs=[smem()] * 2 + [vmem()] * (3 + 2 * len(dss)),
         out_specs=(vmem(),) * 4,
         scratch_shapes=[pltpu.VMEM((F_ROWS, 2 * TOK), bf16), pltpu.VMEM((q_rank, 2 * TOK), bf16)],
         compiler_params=params(12),
         cost_estimate=cost(4 * HROWS * KEYS * ROW),
         name="project",
-    )(place, uk, uq, cos, sin, *held(*dss, *kts))
-
-
-def combine_kernel(a, a2, b1, b3, c0, c1, c2, c3, *outs):
-    total = (a[...].astype(f32) + a2[...].astype(f32)) + (b1[...].astype(f32) + b3[...].astype(f32))
-    total = total.astype(bf16)
-    for d in range(N_Y):
-        outs[d][:ROW, :] = total
-        cg = (c0[d].astype(f32) + c1[d].astype(f32)) + (c2[d].astype(f32) + c3[d].astype(f32))
-        outs[d][ROW:, :] = cg.astype(bf16)
-
-
-def combine(*args):
+    )(order, place, uk, uq, frequency, *held(*dss, *kts))
+
+
+def gather_kernel(p0, p1, p2, p3, *outs):
+    for t in range(2):
+        for k in range(N_XH):
+            a, b, c, d = (p[t, k].astype(f32) for p in (p0, p1, p2, p3))
+            outs[2 * t + k][...] = ((a + c) + (b + d)).astype(bf16)
+
+
+def gather(*parts):
     return pl.pallas_call(
-        combine_kernel,
-        out_shape=(like(ROW + C_COLS, TOK),) * N_Y,
-        in_specs=[vmem()] * 8,
-        out_specs=(vmem(),) * N_Y,
-        compiler_params=params(8),
-        cost_estimate=cost(1024 * 1024),
-        name="combine",
-    )(*args)
+        gather_kernel,
+        out_shape=(like(C_COLS, TOK),) * 4,
+        in_specs=[vmem()] * N_Y,
+        out_specs=(vmem(),) * 4,
+        compiler_params=params(4),
+        cost_estimate=cost(0),
+        name="gather",
+    )(*parts)
 
 
 def add(*parts):
@@ -378,44 +385,40 @@
 def per_device(queries, latent_rows, output_grad, up_query, up_key, up_value, block_order):
     coords = [lax.axis_index(a) for a in ("z", "xl", "core", "y", "xh")]
     place = jnp.stack(coords).astype(jnp.int32)
-    z, xl, core = coords[:3]
 
     own = latent_rows.T
     q_other = shift(queries, dcore=1)
     do_other = shift(output_grad, dcore=1)
-    across = shift(own, dxl=1)
-    kts = [own, across]
-    kts += [shift(own, dz=dz) for dz, _ in SLOTS[2:5]]
-    kts += [shift(across, dz=dz) for dz, _ in SLOTS[5:]]
-
-    first = (z * N_XL + xl) * 4
-    near = lax.dynamic_slice(block_order, (first,), (4,))
-    near = jnp.where(core == 0, near, jnp.roll(near, 2))
-    token = jnp.arange(BLOCK, dtype=jnp.int32)
-    pos = (near[:, None] * BLOCK + token).reshape(-1)
-    frequency = 10000.0 ** (-(2.0 * jnp.arange(HALF, dtype=f32)) / D_ROPE)
-    angles = pos.astype(f32)[None, :] * frequency[:, None]
-    cos, sin = jnp.cos(angles), jnp.sin(angles)
-
-    qt, gt = prologue(queries, q_other, output_grad, do_other, up_value)
-    near, far = tuple(range(EARLY)), tuple(range(EARLY, SHARDS))
-    *part0, kt0, m0, merged = scores(near, block_order, place, qt, gt, kts[:EARLY])
-    *part1, kt1, m1, mine = scores(far, block_order, place, qt, gt, kts[EARLY:], (merged,))
+    kts = [own] + [shift(own, dz=dz) for dz, _ in SLOTS[1:N_Z]]
+    qt, gt, done = prologue(queries, q_other, output_grad, do_other, up_value)
+    for i, dx in enumerate((1, 3, 1, 3)):
+        kt = lax.optimization_barrier((kts[i], done))[0] if i else kts[0]
+        kts.append(shift(kt, dx=dx))
+
+    parts, kt_parts, mine = [], [], ()
+    for slots in GROUPS:
+        took = kts[slots[0] : slots[-1] + 1]
+        e, dp, kt, m, mine = scores(slots, block_order, place, qt, gt, took, mine)
+        parts.append((e, dp, m))
+        kt_parts.append(kt)
+        mine = (mine,)
+    mine = mine[0]
     theirs = shift(mine, dcore=1)
-    dk, dss = grads(((*part0, m0), (*part1, m1)), mine, theirs, qt, gt)
+    dk, dss = grads(parts, mine, theirs, qt, gt)
 
     from_z = [shift(dk[dz], dz=-dz) for dz in range(1, N_Z)]
     a, b = (add(*(p[i] for p in (dk[0], *from_z))) for i in range(N_XL))
 
-    give_send, give_keep, send, keep = project(place, dss, (kt0, kt1), cos, sin, up_key, up_query)
+    cg = project(block_order, place, dss, kt_parts, up_key, up_query)
 
     b1, b3, a2 = shift(b, dx=1), shift(b, dx=3), shift(a, dx=2)
+    total = ((a.astype(f32) + a2.astype(f32)) + (b1.astype(f32) + b3.astype(f32))).astype(bf16)
+    s1, s2, s3 = (shift(total, dy=d).astype(f32) for d in range(1, N_Y))
+    total = ((total.astype(f32) + s2) + (s1 + s3)).astype(bf16)
+
+    keep, send, give_keep, give_send = gather(cg[0], *(shift(cg[d], dy=d) for d in range(1, N_Y)))
     got = shift(send, dx=2), shift(give_keep, dcore=1), shift(give_send, dx=2, dcore=1)
-    mix = combine(a, a2, b1, b3, keep, *got)
-    s0, s1, s2, s3 = (shift(m, dy=d) if d else m for d, m in enumerate(mix))
-    out = (s0.astype(f32) + s2.astype(f32)) + (s1.astype(f32) + s3.astype(f32))
-    out = out.astype(bf16)
-    return out[ROW:].T, out[:ROW].T
+    return add(keep, *got).T, total.T
 
 
 def solution(mesh):

time: 80.4 us -> 75.2 us (0.935)
  waiting for transfers between devices: 17.5 us -> 10.9 us
  starting transfers between devices: 32.8 us -> 38.4 us
  Pallas kernels: 25.2 us -> 22.9 us
  local copies, waits for them, and re-layouts: 2.29 us -> 0.18 us
    ppermute x22 -> x25, waiting for transfers between devices: 17.5 us -> 10.9 us  [shift(): return lax.ppermute(x, AXES, pairs)]
    ppermute x22 -> x25, starting transfers between devices: 32.8 us -> 38.4 us  [shift(): return lax.ppermute(x, AXES, pairs)]
    pallas_call x2 -> x3, Pallas kernels: 11.3 us -> 8.52 us  [scores(): pl.pallas_call(functools.partial(scores_kernel, slots), out_shape=(kept(n...]
    transpose x0 -> x2, other arithmetic: none -> 1.39 us  [per_device(): return (add(keep, *got).T, total.T)]
    transpose x2 -> x0, local copies, waits for them, and re-layouts: 1.29 us -> none  [per_device(): return (out[ROW:].T, out[:ROW].T)]
  transfers between devices with their start and end apart: 22 -> 25, of which waited for: 8 -> 8; matrix products, arithmetic and copies ran while one was open for 3% -> 1% of each run, Pallas kernels for 17% -> 20%
where the time goes in v3:
time: 75.2 us; the launch traced here: 74.8 us
  starting transfers between devices  38.4 us (51%)
  Pallas kernels  22.9 us (30%)
  waiting for transfers between devices  10.9 us (14%)
  other arithmetic  1.63 us (2%)
  between operations  0.8 us (1%)
    ppermute x25, starting transfers between devices, shift(): return lax.ppermute(x, AXES, pairs)  38.4 us
    ppermute x25, waiting for transfers between devices, shift(): return lax.ppermute(x, AXES, pairs)  10.9 us
    pallas_call x3, Pallas kernels, scores(): pl.pallas_call(functools.partial(scores_kernel, slots), out_shape=(kept(n...  8.52 us
    pallas_call x1, Pallas kernels, grads(): pl.pallas_call(functools.partial(grads_kernel, counts), out_shape=(pltpu....  5.91 us
    pallas_call x1, Pallas kernels, project(): pl.pallas_call(project_kernel, out_shape=(like(2, N_XH, C_COLS, TOK),) *...  5.16 us
    pallas_call x1, Pallas kernels, prologue(): pl.pallas_call(prologue_kernel, out_shape=(kept(ROW, ROWS), kept(D_LAT, R...  3.17 us
  transfers between devices with their start and end apart: 25, of which 8 were waited for; matrix products, arithmetic and copies ran while one was open for 1% of the time, Pallas kernels for 20%

profile of v3, /device:TPU:0, one launch (start us, length us, event | category | flops | bytes accessed | tf_op | source)
XLA Modules:
  0.0 74.8 jit_solution(16230642215130952149)
XLA Ops:
  1.2 2.0 %collective-permute-start.2 = (bf16[576,128]{1,0:T(8,128)(2,1)}, bf16[576,128]{1,0:T(8,128)(2,1)S(1)}, u32[]{:S(2)}, u32[]{:S(2)}) collective-permute-start(bf16[576,128]{1,0:T(8,128)(2,1)} %bitcast.16), channel_id=1, source_target_pairs={{0,4},{1,5},{2,6},{3,7},{4,8},{5,9},{6,10},{7,11},{8,12},{9,13},{1... | collective-permute-start | bytes 442376 | tf_op jit(solution)/shard_map/ppermute | solution.py:61
  3.2 2.1 %collective-permute-start.3 = (bf16[576,128]{1,0:T(8,128)(2,1)}, bf16[576,128]{1,0:T(8,128)(2,1)S(1)}, u32[]{:S(2)}, u32[]{:S(2)}) collective-permute-start(bf16[576,128]{1,0:T(8,128)(2,1)} %bitcast.17), channel_id=1, source_target_pairs={{0,12},{1,13},{2,14},{3,15},{4,0},{5,1},{6,2},{7,3},{8,4},{9,5},{1... | collective-permute-start | bytes 442376 | tf_op jit(solution)/shard_map/ppermute | solution.py:61
  5.4 1.9 %collective-permute-start.4 = (bf16[576,128]{1,0:T(8,128)(2,1)}, bf16[576,128]{1,0:T(8,128)(2,1)S(1)}, u32[]{:S(2)}, u32[]{:S(2)}) collective-permute-start(bf16[576,128]{1,0:T(8,128)(2,1)} %bitcast.18), channel_id=1, source_target_pairs={{0,8},{1,9},{2,10},{3,11},{4,12},{5,13},{6,14},{7,15},{8,0},{9,1},... | collective-permute-start | bytes 442376 | tf_op jit(solution)/shard_map/ppermute | solution.py:61
  7.3 1.5 %collective-permute-start.5 = (bf16[576,128]{1,0:T(8,128)(2,1)}, bf16[576,128]{1,0:T(8,128)(2,1)S(1)}, u32[]{:S(2)}, u32[]{:S(2)}) collective-permute-start(bf16[576,128]{1,0:T(8,128)(2,1)} %bitcast.19), channel_id=1, source_target_pairs={{0,2},{1,3},{2,16},{3,17},{4,6},{5,7},{6,20},{7,21},{8,10},{9,11},... | collective-permute-start | bytes 442376 | tf_op jit(solution)/shard_map/ppermute | solution.py:61
  8.8 3.2 %prologue.1 = (bf16[576,2048]{1,0:T(8,128)(2,1)S(1)}, bf16[512,2048]{1,0:T(8,128)(2,1)S(1)}, f32[8,128]{1,0:T(8,128)}) custom-call(bf16[128,4608]{1,0:T(8,128)(2,1)} %q0.1, bf16[128,4608]{1,0:T(8,128)(2,1)S(1)} %collective-permute-done.q1, bf16[128,1024]{1,0:T(8,128)(2,1)} %do0.1, bf16[128,1024]{1,0:T(8,128)(2,1)S(1)} %collective-permute-done.1.do1, ...), custom_call_target="tpu_custom_call" | custom-call | flops 268435456 | bytes 1048576 | tf_op jit(solution)/shard_map/prologue/pallas_call | solution.py:134
  12.0 1.8 %collective-permute-start.6 = (bf16[576,128]{1,0:T(8,128)(2,1)S(1)}, bf16[576,128]{1,0:T(8,128)(2,1)S(1)}, u32[]{:S(2)}, u32[]{:S(2)}) collective-permute-start(bf16[576,128]{1,0:T(8,128)(2,1)S(1)} %collective-permute-done.2.refs_1_), channel_id=1, source_target_pairs={{0,18},{1,19},{2,0},{3,1},{4,22},{5,23},{6,4},{7,5},{8,26},{9,27},... | collective-permute-start | bytes 442376 | tf_op jit(solution)/shard_map/ppermute | solution.py:61
  14.1 3.0 %collective-permute-start.8 = (bf16[576,128]{1,0:T(8,128)(2,1)S(1)}, bf16[576,128]{1,0:T(8,128)(2,1)S(1)}, u32[]{:S(2)}, u32[]{:S(2)}) collective-permute-start(bf16[576,128]{1,0:T(8,128)(2,1)S(1)} %collective-permute-done.4.refs_3_), channel_id=1, source_target_pairs={{0,18},{1,19},{2,0},{3,1},{4,22},{5,23},{6,4},{7,5},{8,26},{9,27},... | collective-permute-start | bytes 442376 | tf_op jit(solution)/shard_map/ppermute | solution.py:61
  17.1 3.9 %scores.3 = (bf16[512,2048]{1,0:T(8,128)(2,1)S(1)}, bf16[512,2048]{1,0:T(8,128)(2,1)S(1)}, bf16[576,512]{1,0:T(8,128)(2,1)S(1)}, f32[8,2048]{1,0:T(8,128)S(1)}, f32[8,2048]{1,0:T(8,128)S(1)}) custom-call(s32[32]{0:T(128)S(1)} %copy-done.1, s32[5]{0:T(128)S(1)} %stack.23.place, bf16[576,2048]{1,0:T(8,128)(2,1)S(1)} %get-tuple-element.38.qt.refs_11_, ...), custom_call_target="tpu_custom_call" | custom-call | flops 2281701376 | bytes 1048576 | tf_op jit(solution)/shard_map/scores/pallas_call | solution.py:220
  21.0 2.3 %scores.4 = (bf16[256,2048]{1,0:T(8,128)(2,1)S(1)}, bf16[256,2048]{1,0:T(8,128)(2,1)S(1)}, bf16[576,256]{1,0:T(8,128)(2,1)S(1)}, f32[8,2048]{1,0:T(8,128)S(1)}, f32[8,2048]{1,0:T(8,128)S(1)}) custom-call(s32[32]{0:T(128)S(1)} %copy-done.1, s32[5]{0:T(128)S(1)} %stack.23.place, bf16[576,2048]{1,0:T(8,128)(2,1)S(1)} %get-tuple-element.38.qt.refs_11_, ...), custom_call_target="tpu_custom_call" | custom-call | flops 1140850688 | bytes 1048576 | tf_op jit(solution)/shard_map/scores/pallas_call | solution.py:220
  23.3 2.3 %scores.5 = (bf16[256,2048]{1,0:T(8,128)(2,1)S(1)}, bf16[256,2048]{1,0:T(8,128)(2,1)S(1)}, bf16[576,256]{1,0:T(8,128)(2,1)S(1)}, f32[8,2048]{1,0:T(8,128)S(1)}, f32[8,2048]{1,0:T(8,128)S(1)}) custom-call(s32[32]{0:T(128)S(1)} %copy-done.1, s32[5]{0:T(128)S(1)} %stack.23.place, bf16[576,2048]{1,0:T(8,128)(2,1)S(1)} %get-tuple-element.38.qt.refs_11_, ...), custom_call_target="tpu_custom_call" | custom-call | flops 1140850688 | bytes 1048576 | tf_op jit(solution)/shard_map/scores/pallas_call | solution.py:220
  25.9 1.2 %collective-permute-done.9.refs_10_ = f32[8,2048]{1,0:T(8,128)S(1)} collective-permute-done((f32[8,2048]{1,0:T(8,128)S(1)}, f32[8,2048]{1,0:T(8,128)S(1)}, u32[]{:S(2)}, u32[]{:S(2)}) %collective-permute-start.9) | collective-permute-done | bytes 65568 | tf_op jit(solution)/shard_map/ppermute | solution.py:61
  27.2 5.9 %grads.1 = (bf16[2,576,128]{2,1,0:T(8,128)(2,1)}, bf16[2,576,128]{2,1,0:T(8,128)(2,1)}, bf16[2,576,128]{2,1,0:T(8,128)(2,1)}, bf16[2,576,128]{2,1,0:T(8,128)(2,1...) custom-call(bf16[512,2048]{1,0:T(8,128)(2,1)S(1)} %get-tuple-element.40.refs_0_, ...), custom_call_target="tpu_custom_call" | custom-call | flops 4563402752 | bytes 1048576 | tf_op jit(solution)/shard_map/grads/pallas_call | solution.py:292
  33.1 2.0 %collective-permute-start.16 = (bf16[2,576,128]{2,1,0:T(8,128)(2,1)}, bf16[2,576,128]{2,1,0:T(8,128)(2,1)S(1)}, u32[]{:S(2)}, u32[]{:S(2)}) collective-permute-start(bf16[2,576,128]{2,1,0:T(8,128)(2,1)} %get-tuple-element.71), channel_id=1, source_target_pairs={{0,12},{1,13},{2,14},{3,15},{4,0},{5,1},{6,2},{7,3},{8,4},{9,5},{1... | collective-permute-start | bytes 884744 | tf_op jit(solution)/shard_map/ppermute | solution.py:61
  35.1 1.5 %collective-permute-start.17 = (bf16[2,576,128]{2,1,0:T(8,128)(2,1)}, bf16[2,576,128]{2,1,0:T(8,128)(2,1)S(1)}, u32[]{:S(2)}, u32[]{:S(2)}) collective-permute-start(bf16[2,576,128]{2,1,0:T(8,128)(2,1)} %get-tuple-element.72), channel_id=1, source_target_pairs={{0,8},{1,9},{2,10},{3,11},{4,12},{5,13},{6,14},{7,15},{8,0},{9,1},... | collective-permute-start | bytes 884744 | tf_op jit(solution)/shard_map/ppermute | solution.py:61
  36.6 1.3 %collective-permute-start.18 = (bf16[2,576,128]{2,1,0:T(8,128)(2,1)}, bf16[2,576,128]{2,1,0:T(8,128)(2,1)S(1)}, u32[]{:S(2)}, u32[]{:S(2)}) collective-permute-start(bf16[2,576,128]{2,1,0:T(8,128)(2,1)} %get-tuple-element.73), channel_id=1, source_target_pairs={{0,4},{1,5},{2,6},{3,7},{4,8},{5,9},{6,10},{7,11},{8,12},{9,13},{1... | collective-permute-start | bytes 884744 | tf_op jit(solution)/shard_map/ppermute | solution.py:61
  38.0 5.2 %project.1 = (bf16[2,2,192,128]{3,2,1,0:T(8,128)(2,1)S(1)}, bf16[2,2,192,128]{3,2,1,0:T(8,128)(2,1)S(1)}, bf16[2,2,192,128]{3,2,1,0:T(8,128)(2,1)S(1)}, bf16[2,2,192,128]{3,2,1,0:T(8,128)(2,1)S(1)}) custom-call(s32[32]{0:T(128)S(1)} %copy-done.1, s32[5]{0:T(128)S(1)} %stack.23.place, bf16[8,128,512]{2,1,0:T(8,128)(2,1)S(1)} %copy-done, ...), custom_call_target="tpu_custom_call" | custom-call | flops 2415919104 | bytes 1048576 | tf_op jit(solution)/shard_map/project/pallas_call | solution.py:350
  43.2 1.6 %collective-permute-start.10 = (bf16[2,2,192,128]{3,2,1,0:T(8,128)(2,1)S(1)}, bf16[2,2,192,128]{3,2,1,0:T(8,128)(2,1)S(1)}, u32[]{:S(2)}, u32[]{:S(2)}) collective-permute-start(bf16[2,2,192,128]{3,2,1,0:T(8,128)(2,1)S(1)} %get-tuple-element.63), channel_id=1, source_target_pairs={{0,32},{1,33},{2,34},{3,35},{4,36},{5,37},{6,38},{7,39},{8,40},{9,... | collective-permute-start | bytes 589832 | tf_op jit(solution)/shard_map/ppermute | solution.py:61
  44.9 2.9 %collective-permute-start.11 = (bf16[2,2,192,128]{3,2,1,0:T(8,128)(2,1)S(1)}, bf16[2,2,192,128]{3,2,1,0:T(8,128)(2,1)S(1)}, u32[]{:S(2)}, u32[]{:S(2)}) collective-permute-start(bf16[2,2,192,128]{3,2,1,0:T(8,128)(2,1)S(1)} %get-tuple-element.64), channel_id=1, source_target_pairs={{0,64},{1,65},{2,66},{3,67},{4,68},{5,69},{6,70},{7,71},{8,72},{9,... | collective-permute-start | bytes 589832 | tf_op jit(solution)/shard_map/ppermute | solution.py:61
  47.8 0.6 collective-permute-done.16
  48.4 3.0 %collective-permute-start.12 = (bf16[2,2,192,128]{3,2,1,0:T(8,128)(2,1)S(1)}, bf16[2,2,192,128]{3,2,1,0:T(8,128)(2,1)S(1)}, u32[]{:S(2)}, u32[]{:S(2)}) collective-permute-start(bf16[2,2,192,128]{3,2,1,0:T(8,128)(2,1)S(1)} %get-tuple-element.65), channel_id=1, source_target_pairs={{0,96},{1,97},{2,98},{3,99},{4,100},{5,101},{6,102},{7,103},{8,104... | collective-permute-start | bytes 589832 | tf_op jit(solution)/shard_map/ppermute | solution.py:61
  52.1 1.6 %collective-permute-start.19 = (bf16[576,128]{1,0:T(8,128)(2,1)S(1)}, bf16[576,128]{1,0:T(8,128)(2,1)S(1)}, u32[]{:S(2)}, u32[]{:S(2)}) collective-permute-start(bf16[576,128]{1,0:T(8,128)(2,1)S(1)} %get-tuple-element.74), channel_id=1, source_target_pairs={{0,16},{1,17},{2,18},{3,19},{4,20},{5,21},{6,22},{7,23},{8,24},{9,... | collective-permute-start | bytes 442376 | tf_op jit(solution)/shard_map/ppermute | solution.py:61
  54.3 2.6 %collective-permute-start.21 = (bf16[576,128]{1,0:T(8,128)(2,1)S(1)}, bf16[576,128]{1,0:T(8,128)(2,1)S(1)}, u32[]{:S(2)}, u32[]{:S(2)}) collective-permute-start(bf16[576,128]{1,0:T(8,128)(2,1)S(1)} %get-tuple-element.75), channel_id=1, source_target_pairs={{0,18},{1,19},{2,0},{3,1},{4,22},{5,23},{6,4},{7,5},{8,26},{9,27},... | collective-permute-start | bytes 442376 | tf_op jit(solution)/shard_map/ppermute | solution.py:61
  57.1 0.9 %collective-permute-start.13 = (bf16[192,128]{1,0:T(8,128)(2,1)S(1)}, bf16[192,128]{1,0:T(8,128)(2,1)S(1)}, u32[]{:S(2)}, u32[]{:S(2)}) collective-permute-start(bf16[192,128]{1,0:T(8,128)(2,1)S(1)} %get-tuple-element.67), channel_id=1, source_target_pairs={{0,16},{1,17},{2,18},{3,19},{4,20},{5,21},{6,22},{7,23},{8,24},{9,... | collective-permute-start | bytes 147464 | tf_op jit(solution)/shard_map/ppermute | solution.py:61
  57.9 2.5 %collective-permute-done.19 = bf16[576,128]{1,0:T(8,128)(2,1)S(1)} collective-permute-done((bf16[576,128]{1,0:T(8,128)(2,1)S(1)}, bf16[576,128]{1,0:T(8,128)(2,1)S(1)}, u32[]{:S(2)}, u32[]{:S(2)}) %collective-permute-start.19) | collective-permute-done | bytes 147488 | tf_op jit(solution)/shard_map/ppermute | solution.py:61
  60.8 2.4 %collective-permute-done.20 = bf16[576,128]{1,0:T(8,128)(2,1)S(1)} collective-permute-done((bf16[576,128]{1,0:T(8,128)(2,1)S(1)}, bf16[576,128]{1,0:T(8,128)(2,1)S(1)}, u32[]{:S(2)}, u32[]{:S(2)}) %collective-permute-start.20) | collective-permute-done | bytes 147488 | tf_op jit(solution)/shard_map/ppermute | solution.py:61
  63.2 3.3 %collective-permute-start.22 = (bf16[576,128]{1,0:T(8,128)(2,1)S(1)}, bf16[576,128]{1,0:T(8,128)(2,1)S(1)}, u32[]{:S(2)}, u32[]{:S(2)}) collective-permute-start(bf16[576,128]{1,0:T(8,128)(2,1)S(1)} %add_convert_fusion.1), channel_id=1, source_target_pairs={{0,64},{1,65},{2,66},{3,67},{4,68},{5,69},{6,70},{7,71},{8,72},{9,... | collective-permute-start | bytes 442376 | tf_op jit(solution)/shard_map/ppermute | solution.py:61
  66.5 0.7 collective-permute-start.23
  67.2 2.6 %collective-permute-start.24 = (bf16[576,128]{1,0:T(8,128)(2,1)S(1)}, bf16[576,128]{1,0:T(8,128)(2,1)S(1)}, u32[]{:S(2)}, u32[]{:S(2)}) collective-permute-start(bf16[576,128]{1,0:T(8,128)(2,1)S(1)} %add_convert_fusion.1), channel_id=1, source_target_pairs={{0,96},{1,97},{2,98},{3,99},{4,100},{5,101},{6,102},{7,103},{8,104... | collective-permute-start | bytes 442376 | tf_op jit(solution)/shard_map/ppermute | solution.py:61
  69.8 0.7 fusion.3
  70.4 1.1 %collective-permute-done.22 = bf16[576,128]{1,0:T(8,128)(2,1)S(1)} collective-permute-done((bf16[576,128]{1,0:T(8,128)(2,1)S(1)}, bf16[576,128]{1,0:T(8,128)(2,1)S(1)}, u32[]{:S(2)}, u32[]{:S(2)}) %collective-permute-start.22) | collective-permute-done | bytes 147488 | tf_op jit(solution)/shard_map/ppermute | solution.py:61
  71.5 2.4 %collective-permute-done.23 = bf16[576,128]{1,0:T(8,128)(2,1)S(1)} collective-permute-done((bf16[576,128]{1,0:T(8,128)(2,1)S(1)}, bf16[576,128]{1,0:T(8,128)(2,1)S(1)}, u32[]{:S(2)}, u32[]{:S(2)}) %collective-permute-start.23) | collective-permute-done | bytes 147488 | tf_op jit(solution)/shard_map/ppermute | solution.py:61
  74.1 0.7 fusion.2
  (46 shorter events, 3.4 us)
Async XLA Ops:
  0.6 16.4 %copy-start.2 = (bf16[128,576]{0,1:T(8,128)(2,1)S(1)}, bf16[128,576]{0,1:T(8,128)(2,1)}, u32[]{:S(2)}) copy-start(bf16[128,576]{0,1:T(8,128)(2,1)} %param.9) | copy-start | bytes 442372
  0.6 16.4 %copy-start.1 = (s32[32]{0:T(128)S(1)}, s32[32]{0:T(128)}, u32[]{:S(2)}) copy-start(s32[32]{0:T(128)} %order.7) | copy-start | bytes 388
  0.7 8.2 %collective-permute-start = (bf16[128,4608]{1,0:T(8,128)(2,1)}, bf16[128,4608]{1,0:T(8,128)(2,1)S(1)}, u32[]{:S(2)}, u32[]{:S(2)}) collective-permute-start(bf16[128,4608]{1,0:T(8,128)(2,1)} %q0.1), channel_id=1, source_target_pairs={{0,1},{1,0},{2,3},{3,2},{4,5},{5,4},{6,7},{7,6},{8,9},{9,8},{10,11... | collective-permute-start | bytes 3538952 | tf_op jit(solution)/shard_map/ppermute | solution.py:61
  0.7 6.6 %collective-permute-start.1 = (bf16[128,1024]{1,0:T(8,128)(2,1)}, bf16[128,1024]{1,0:T(8,128)(2,1)S(1)}, u32[]{:S(2)}, u32[]{:S(2)}) collective-permute-start(bf16[128,1024]{1,0:T(8,128)(2,1)} %do0.1), channel_id=1, source_target_pairs={{0,1},{1,0},{2,3},{3,2},{4,5},{5,4},{6,7},{7,6},{8,9},{9,8},{10,11... | collective-permute-start | bytes 786440 | tf_op jit(solution)/shard_map/ppermute | solution.py:61
  1.2 10.8 %collective-permute-start.2 = (bf16[576,128]{1,0:T(8,128)(2,1)}, bf16[576,128]{1,0:T(8,128)(2,1)S(1)}, u32[]{:S(2)}, u32[]{:S(2)}) collective-permute-start(bf16[576,128]{1,0:T(8,128)(2,1)} %bitcast.16), channel_id=1, source_target_pairs={{0,4},{1,5},{2,6},{3,7},{4,8},{5,9},{6,10},{7,11},{8,12},{9,13},{1... | collective-permute-start | bytes 442376 | tf_op jit(solution)/shard_map/ppermute | solution.py:61
  3.2 10.6 %collective-permute-start.3 = (bf16[576,128]{1,0:T(8,128)(2,1)}, bf16[576,128]{1,0:T(8,128)(2,1)S(1)}, u32[]{:S(2)}, u32[]{:S(2)}) collective-permute-start(bf16[576,128]{1,0:T(8,128)(2,1)} %bitcast.17), channel_id=1, source_target_pairs={{0,12},{1,13},{2,14},{3,15},{4,0},{5,1},{6,2},{7,3},{8,4},{9,5},{1... | collective-permute-start | bytes 442376 | tf_op jit(solution)/shard_map/ppermute | solution.py:61
  5.4 8.7 %collective-permute-start.4 = (bf16[576,128]{1,0:T(8,128)(2,1)}, bf16[576,128]{1,0:T(8,128)(2,1)S(1)}, u32[]{:S(2)}, u32[]{:S(2)}) collective-permute-start(bf16[576,128]{1,0:T(8,128)(2,1)} %bitcast.18), channel_id=1, source_target_pairs={{0,8},{1,9},{2,10},{3,11},{4,12},{5,13},{6,14},{7,15},{8,0},{9,1},... | collective-permute-start | bytes 442376 | tf_op jit(solution)/shard_map/ppermute | solution.py:61
  7.3 13.7 %collective-permute-start.5 = (bf16[576,128]{1,0:T(8,128)(2,1)}, bf16[576,128]{1,0:T(8,128)(2,1)S(1)}, u32[]{:S(2)}, u32[]{:S(2)}) collective-permute-start(bf16[576,128]{1,0:T(8,128)(2,1)} %bitcast.19), channel_id=1, source_target_pairs={{0,2},{1,3},{2,16},{3,17},{4,6},{5,7},{6,20},{7,21},{8,10},{9,11},... | collective-permute-start | bytes 442376 | tf_op jit(solution)/shard_map/ppermute | solution.py:61
  12.0 9.0 %collective-permute-start.6 = (bf16[576,128]{1,0:T(8,128)(2,1)S(1)}, bf16[576,128]{1,0:T(8,128)(2,1)S(1)}, u32[]{:S(2)}, u32[]{:S(2)}) collective-permute-start(bf16[576,128]{1,0:T(8,128)(2,1)S(1)} %collective-permute-done.2.refs_1_), channel_id=1, source_target_pairs={{0,18},{1,19},{2,0},{3,1},{4,22},{5,23},{6,4},{7,5},{8,26},{9,27},... | collective-permute-start | bytes 442376 | tf_op jit(solution)/shard_map/ppermute | solution.py:61
  13.8 9.5 %collective-permute-start.7 = (bf16[576,128]{1,0:T(8,128)(2,1)S(1)}, bf16[576,128]{1,0:T(8,128)(2,1)S(1)}, u32[]{:S(2)}, u32[]{:S(2)}) collective-permute-start(bf16[576,128]{1,0:T(8,128)(2,1)S(1)} %collective-permute-done.3.refs_2_), channel_id=1, source_target_pairs={{0,2},{1,3},{2,16},{3,17},{4,6},{5,7},{6,20},{7,21},{8,10},{9,11},... | collective-permute-start | bytes 442376 | tf_op jit(solution)/shard_map/ppermute | solution.py:61
  14.1 9.2 %collective-permute-start.8 = (bf16[576,128]{1,0:T(8,128)(2,1)S(1)}, bf16[576,128]{1,0:T(8,128)(2,1)S(1)}, u32[]{:S(2)}, u32[]{:S(2)}) collective-permute-start(bf16[576,128]{1,0:T(8,128)(2,1)S(1)} %collective-permute-done.4.refs_3_), channel_id=1, source_target_pairs={{0,18},{1,19},{2,0},{3,1},{4,22},{5,23},{6,4},{7,5},{8,26},{9,27},... | collective-permute-start | bytes 442376 | tf_op jit(solution)/shard_map/ppermute | solution.py:61
  25.6 1.5 %collective-permute-start.9 = (f32[8,2048]{1,0:T(8,128)S(1)}, f32[8,2048]{1,0:T(8,128)S(1)}, u32[]{:S(2)}, u32[]{:S(2)}) collective-permute-start(f32[8,2048]{1,0:T(8,128)S(1)} %get-tuple-element.55.refs_9_), channel_id=1, source_target_pairs={{0,1},{1,0},{2,3},{3,2},{4,5},{5,4},{6,7},{7,6},{8,9},{9,8},{10,11... | collective-permute-start | bytes 196616 | tf_op jit(solution)/shard_map/ppermute | solution.py:61
  27.2 10.9 %slice-start = ((s8[4718592]{0:T(1024)(128)(4,1)}), s8[4194304]{0:T(1024)(128)(4,1)S(1)}, s32[]{:S(2)}) async-start(s8[4718592]{0:T(1024)(128)(4,1)} %bitcast.14), calls=%async_computation | async-start | bytes 8388608
  27.2 10.8 %copy-start.4 = (f32[32]{0:T(128)S(1)}, f32[32]{0:T(128)}, u32[]{:S(2)}) copy-start(f32[32]{0:T(128)} %constant.21.clone) | copy-start | bytes 388
  27.2 10.9 %slice-start.1 = ((s8[4718592]{0:T(1024)(128)(4,1)}), s8[524288]{0:T(1024)(128)(4,1)S(1)}, s32[]{:S(2)}) async-start(s8[4718592]{0:T(1024)(128)(4,1)} %bitcast.14), calls=%async_computation.1 | async-start | bytes 1048576
  27.2 10.9 %copy-start = (bf16[8,128,512]{2,1,0:T(8,128)(2,1)S(1)}, bf16[8,128,512]{2,1,0:T(8,128)(2,1)}, u32[]{:S(2)}) copy-start(bf16[8,128,512]{2,1,0:T(8,128)(2,1)} %uk.1) | copy-start | bytes 3145732
  33.1 15.3 %collective-permute-start.16 = (bf16[2,576,128]{2,1,0:T(8,128)(2,1)}, bf16[2,576,128]{2,1,0:T(8,128)(2,1)S(1)}, u32[]{:S(2)}, u32[]{:S(2)}) collective-permute-start(bf16[2,576,128]{2,1,0:T(8,128)(2,1)} %get-tuple-element.71), channel_id=1, source_target_pairs={{0,12},{1,13},{2,14},{3,15},{4,0},{5,1},{6,2},{7,3},{8,4},{9,5},{1... | collective-permute-start | bytes 884744 | tf_op jit(solution)/shard_map/ppermute | solution.py:61
  35.1 16.3 %collective-permute-start.17 = (bf16[2,576,128]{2,1,0:T(8,128)(2,1)}, bf16[2,576,128]{2,1,0:T(8,128)(2,1)S(1)}, u32[]{:S(2)}, u32[]{:S(2)}) collective-permute-start(bf16[2,576,128]{2,1,0:T(8,128)(2,1)} %get-tuple-element.72), channel_id=1, source_target_pairs={{0,8},{1,9},{2,10},{3,11},{4,12},{5,13},{6,14},{7,15},{8,0},{9,1},... | collective-permute-start | bytes 884744 | tf_op jit(solution)/shard_map/ppermute | solution.py:61
  36.6 15.3 %collective-permute-start.18 = (bf16[2,576,128]{2,1,0:T(8,128)(2,1)}, bf16[2,576,128]{2,1,0:T(8,128)(2,1)S(1)}, u32[]{:S(2)}, u32[]{:S(2)}) collective-permute-start(bf16[2,576,128]{2,1,0:T(8,128)(2,1)} %get-tuple-element.73), channel_id=1, source_target_pairs={{0,4},{1,5},{2,6},{3,7},{4,8},{5,9},{6,10},{7,11},{8,12},{9,13},{1... | collective-permute-start | bytes 884744 | tf_op jit(solution)/shard_map/ppermute | solution.py:61
  38.0 13.9 %copy-start.3 = (bf16[2,576,128]{2,1,0:T(8,128)(2,1)S(1)}, bf16[2,576,128]{2,1,0:T(8,128)(2,1)}, u32[]{:S(2)}) copy-start(bf16[2,576,128]{2,1,0:T(8,128)(2,1)} %get-tuple-element.70) | copy-start | bytes 884740
  43.2 11.1 %collective-permute-start.10 = (bf16[2,2,192,128]{3,2,1,0:T(8,128)(2,1)S(1)}, bf16[2,2,192,128]{3,2,1,0:T(8,128)(2,1)S(1)}, u32[]{:S(2)}, u32[]{:S(2)}) collective-permute-start(bf16[2,2,192,128]{3,2,1,0:T(8,128)(2,1)S(1)} %get-tuple-element.63), channel_id=1, source_target_pairs={{0,32},{1,33},{2,34},{3,35},{4,36},{5,37},{6,38},{7,39},{8,40},{9,... | collective-permute-start | bytes 589832 | tf_op jit(solution)/shard_map/ppermute | solution.py:61
  44.9 12.1 %collective-permute-start.11 = (bf16[2,2,192,128]{3,2,1,0:T(8,128)(2,1)S(1)}, bf16[2,2,192,128]{3,2,1,0:T(8,128)(2,1)S(1)}, u32[]{:S(2)}, u32[]{:S(2)}) collective-permute-start(bf16[2,2,192,128]{3,2,1,0:T(8,128)(2,1)S(1)} %get-tuple-element.64), channel_id=1, source_target_pairs={{0,64},{1,65},{2,66},{3,67},{4,68},{5,69},{6,70},{7,71},{8,72},{9,... | collective-permute-start | bytes 589832 | tf_op jit(solution)/shard_map/ppermute | solution.py:61
  48.4 8.6 %collective-permute-start.12 = (bf16[2,2,192,128]{3,2,1,0:T(8,128)(2,1)S(1)}, bf16[2,2,192,128]{3,2,1,0:T(8,128)(2,1)S(1)}, u32[]{:S(2)}, u32[]{:S(2)}) collective-permute-start(bf16[2,2,192,128]{3,2,1,0:T(8,128)(2,1)S(1)} %get-tuple-element.65), channel_id=1, source_target_pairs={{0,96},{1,97},{2,98},{3,99},{4,100},{5,101},{6,102},{7,103},{8,104... | collective-permute-start | bytes 589832 | tf_op jit(solution)/shard_map/ppermute | solution.py:61
  52.1 8.3 %collective-permute-start.19 = (bf16[576,128]{1,0:T(8,128)(2,1)S(1)}, bf16[576,128]{1,0:T(8,128)(2,1)S(1)}, u32[]{:S(2)}, u32[]{:S(2)}) collective-permute-start(bf16[576,128]{1,0:T(8,128)(2,1)S(1)} %get-tuple-element.74), channel_id=1, source_target_pairs={{0,16},{1,17},{2,18},{3,19},{4,20},{5,21},{6,22},{7,23},{8,24},{9,... | collective-permute-start | bytes 442376 | tf_op jit(solution)/shard_map/ppermute | solution.py:61
  53.7 9.4 %collective-permute-start.20 = (bf16[576,128]{1,0:T(8,128)(2,1)S(1)}, bf16[576,128]{1,0:T(8,128)(2,1)S(1)}, u32[]{:S(2)}, u32[]{:S(2)}) collective-permute-start(bf16[576,128]{1,0:T(8,128)(2,1)S(1)} %get-tuple-element.75), channel_id=1, source_target_pairs={{0,2},{1,3},{2,16},{3,17},{4,6},{5,7},{6,20},{7,21},{8,10},{9,11},... | collective-permute-start | bytes 442376 | tf_op jit(solution)/shard_map/ppermute | solution.py:61
  54.3 8.8 %collective-permute-start.21 = (bf16[576,128]{1,0:T(8,128)(2,1)S(1)}, bf16[576,128]{1,0:T(8,128)(2,1)S(1)}, u32[]{:S(2)}, u32[]{:S(2)}) collective-permute-start(bf16[576,128]{1,0:T(8,128)(2,1)S(1)} %get-tuple-element.75), channel_id=1, source_target_pairs={{0,18},{1,19},{2,0},{3,1},{4,22},{5,23},{6,4},{7,5},{8,26},{9,27},... | collective-permute-start | bytes 442376 | tf_op jit(solution)/shard_map/ppermute | solution.py:61
  57.1 10.1 %collective-permute-start.13 = (bf16[192,128]{1,0:T(8,128)(2,1)S(1)}, bf16[192,128]{1,0:T(8,128)(2,1)S(1)}, u32[]{:S(2)}, u32[]{:S(2)}) collective-permute-start(bf16[192,128]{1,0:T(8,128)(2,1)S(1)} %get-tuple-element.67), channel_id=1, source_target_pairs={{0,16},{1,17},{2,18},{3,19},{4,20},{5,21},{6,22},{7,23},{8,24},{9,... | collective-permute-start | bytes 147464 | tf_op jit(solution)/shard_map/ppermute | solution.py:61
  57.9 11.8 %collective-permute-start.14 = (bf16[192,128]{1,0:T(8,128)(2,1)S(1)}, bf16[192,128]{1,0:T(8,128)(2,1)S(1)}, u32[]{:S(2)}, u32[]{:S(2)}) collective-permute-start(bf16[192,128]{1,0:T(8,128)(2,1)S(1)} %get-tuple-element.68), channel_id=1, source_target_pairs={{0,1},{1,0},{2,3},{3,2},{4,5},{5,4},{6,7},{7,6},{8,9},{9,8},{10,11... | collective-permute-start | bytes 147464 | tf_op jit(solution)/shard_map/ppermute | solution.py:61
  60.4 9.3 %collective-permute-start.15 = (bf16[192,128]{1,0:T(8,128)(2,1)S(1)}, bf16[192,128]{1,0:T(8,128)(2,1)S(1)}, u32[]{:S(2)}, u32[]{:S(2)}) collective-permute-start(bf16[192,128]{1,0:T(8,128)(2,1)S(1)} %get-tuple-element.69), channel_id=1, source_target_pairs={{0,17},{1,16},{2,19},{3,18},{4,21},{5,20},{6,23},{7,22},{8,25},{9,... | collective-permute-start | bytes 147464 | tf_op jit(solution)/shard_map/ppermute | solution.py:61
  63.2 8.3 %collective-permute-start.22 = (bf16[576,128]{1,0:T(8,128)(2,1)S(1)}, bf16[576,128]{1,0:T(8,128)(2,1)S(1)}, u32[]{:S(2)}, u32[]{:S(2)}) collective-permute-start(bf16[576,128]{1,0:T(8,128)(2,1)S(1)} %add_convert_fusion.1), channel_id=1, source_target_pairs={{0,64},{1,65},{2,66},{3,67},{4,68},{5,69},{6,70},{7,71},{8,72},{9,... | collective-permute-start | bytes 442376 | tf_op jit(solution)/shard_map/ppermute | solution.py:61
  66.5 7.4 %collective-permute-start.23 = (bf16[576,128]{1,0:T(8,128)(2,1)S(1)}, bf16[576,128]{1,0:T(8,128)(2,1)S(1)}, u32[]{:S(2)}, u32[]{:S(2)}) collective-permute-start(bf16[576,128]{1,0:T(8,128)(2,1)S(1)} %add_convert_fusion.1), channel_id=1, source_target_pairs={{0,32},{1,33},{2,34},{3,35},{4,36},{5,37},{6,38},{7,39},{8,40},{9,... | collective-permute-start | bytes 442376 | tf_op jit(solution)/shard_map/ppermute | solution.py:61
  67.2 6.9 %collective-permute-start.24 = (bf16[576,128]{1,0:T(8,128)(2,1)S(1)}, bf16[576,128]{1,0:T(8,128)(2,1)S(1)}, u32[]{:S(2)}, u32[]{:S(2)}) collective-permute-start(bf16[576,128]{1,0:T(8,128)(2,1)S(1)} %add_convert_fusion.1), channel_id=1, source_target_pairs={{0,96},{1,97},{2,98},{3,99},{4,100},{5,101},{6,102},{7,103},{8,104... | collective-permute-start | bytes 442376 | tf_op jit(solution)/shard_map/ppermute | solution.py:61

commit v4 on v3

--- a/solution.py
+++ b/solution.py
@@ -32,7 +32,7 @@
 AXES = ("y", "xh", "z", "xl", "core")
 TN = 256
 
-SLOTS = ((0, 0), (1, 0), (3, 0), (2, 0), (0, 1), (1, 1), (3, 1), (2, 1))
+SLOTS = ((1, 0), (3, 0), (0, 0), (2, 0), (1, 1), (3, 1), (0, 1), (2, 1))
 GROUPS = ((0, 1, 2, 3), (4, 5), (6, 7))
 
 NT = (((1,), (1,)), ((), ()))
@@ -235,13 +235,11 @@
     )(order, place, *held(qt, gt), *kts, *before)
 
 
-def grads_kernel(counts, *refs):
-    n = len(counts)
+def grads_kernel(picks, *refs):
+    n = len(picks)
     es, dps, ms, refs = refs[:n], refs[n : 2 * n], refs[2 * n : 3 * n], refs[3 * n :]
     mine, theirs, qt, gt = refs[:4]
-    outs, refs = refs[4 : 4 + N_Z], refs[4 + N_Z :]
-    dss, (r_s, rc_s, delta_s, p_s, dk_s, sems) = refs[:n], refs[n:]
-    copies = []
+    outs, dss, (r_s, rc_s, delta_s, p_s) = refs[4:6], refs[6 : 6 + n], refs[6 + n :]
     for j in range(2):
         a = slice(j * HROWS, (j + 1) * HROWS)
         b = slice((1 - j) * HROWS, (2 - j) * HROWS)
@@ -250,88 +248,75 @@
         f0, f1 = jnp.exp2(m0 - top), jnp.exp2(m1 - top)
         inv = 1.0 / (f0 * mine[1:2, a] + f1 * theirs[1:2, b])
         delta_s[0:1, a] = (f0 * mine[2:3, a] + f1 * theirs[2:3, b]) * inv
-        at = 0
-        for m, c in zip(ms, counts):
-            r = jnp.exp2(m[:c, a] - top) * inv
-            r_s[at : at + c, a] = r
-            rc_s[at : at + c, a] = r * SCALE
-            at += c
-    at = 0
-    for e, dp, ds, c in zip(es, dps, dss, counts):
-        for k in range(c):
-            s = at + k
-            rows = slice(k * TOK, (k + 1) * TOK)
-            p_rows = slice((s % 4) * TOK, (s % 4 + 1) * TOK)
+        for i, (m, at) in enumerate(zip(ms, picks)):
+            r = jnp.exp2(m[at : at + 2, a] - top) * inv
+            r_s[2 * i : 2 * i + 2, a] = r
+            rc_s[2 * i : 2 * i + 2, a] = r * SCALE
+    for i, (e, dp, ds, at) in enumerate(zip(es, dps, dss, picks)):
+        for k in range(2):
+            s = 2 * i + k
+            rows = slice((at + k) * TOK, (at + k + 1) * TOK)
+            to = slice(k * TOK, (k + 1) * TOK)
+            p_to = slice(s * TOK, (s + 1) * TOK)
             for j in range(ROWS // TN):
                 cols = slice(j * TN, (j + 1) * TN)
                 ef = e[rows, cols].astype(f32)
-                p_s[p_rows, cols] = (ef * r_s[s : s + 1, cols]).astype(bf16)
+                p_s[p_to, cols] = (ef * r_s[s : s + 1, cols]).astype(bf16)
                 d = dp[rows, cols].astype(f32) - delta_s[0:1, cols]
-                ds[rows, cols] = (ef * rc_s[s : s + 1, cols] * d).astype(bf16)
-            if k % 2:
-                pair = slice((k - 1) * TOK, (k + 1) * TOK)
-                p_pair = slice((s % 4 - 1) * TOK, (s % 4 + 1) * TOK)
-                dk = dot(qt[...], ds[pair, :], NT)
-                dv = dot(gt[...], p_s[p_pair, :], NT)
-                for i in range(2):
-                    h = slice(i * TOK, (i + 1) * TOK)
-                    o = s - 1 + i
-                    dz, dxl = SLOTS[o]
-                    dk_s[o, :D_LAT, :] = (dk[:D_LAT, h] + dv[:, h]).astype(bf16)
-                    dk_s[o, D_LAT:, :] = dk[D_LAT:, h].astype(bf16)
-                    copies.append(pltpu.make_async_copy(dk_s.at[o], outs[dz].at[dxl], sems.at[o]))
-                    copies[-1].start()
-        at += c
-    for copy in copies:
-        copy.wait()
+                ds[to, cols] = (ef * rc_s[s : s + 1, cols] * d).astype(bf16)
+        dk = dot(qt[...], ds[...], NT)
+        dv = dot(gt[...], p_s[2 * i * TOK : (2 * i + 2) * TOK, :], NT)
+        for k in range(2):
+            h = slice(k * TOK, (k + 1) * TOK)
+            outs[k][i, :D_LAT, :] = (dk[:D_LAT, h] + dv[:, h]).astype(bf16)
+            outs[k][i, D_LAT:, :] = dk[D_LAT:, h].astype(bf16)
 
 
 def grads(parts, mine, theirs, qt, gt):
-    es, dps, ms = zip(*parts)
-    counts = tuple(e.shape[0] // TOK for e in es)
+    es, dps, ms, picks = zip(*parts)
+    n = len(parts)
     res = pl.pallas_call(
-        functools.partial(grads_kernel, counts),
-        out_shape=(pltpu.HBM((N_XL, ROW, TOK), bf16),) * N_Z + tuple(kept(*e.shape) for e in es),
-        in_specs=[vmem()] * (3 * len(parts) + 4),
-        out_specs=(hbm(),) * N_Z + (vmem(),) * len(parts),
+        functools.partial(grads_kernel, picks),
+        out_shape=(like(N_XL, ROW, TOK),) * 2 + (kept(2 * TOK, ROWS),) * n,
+        in_specs=[vmem()] * (3 * n + 4),
+        out_specs=(vmem(),) * (2 + n),
         scratch_shapes=[
-            pltpu.VMEM((SHARDS, ROWS), f32),
-            pltpu.VMEM((SHARDS, ROWS), f32),
             pltpu.VMEM((8, ROWS), f32),
-            pltpu.VMEM((4 * TOK, ROWS), bf16),
-            pltpu.VMEM((SHARDS, ROW, TOK), bf16),
-            pltpu.SemaphoreType.DMA((SHARDS,)),
+            pltpu.VMEM((8, ROWS), f32),
+            pltpu.VMEM((8, ROWS), f32),
+            pltpu.VMEM((2 * n * TOK, ROWS), bf16),
         ],
         compiler_params=params(8),
-        cost_estimate=cost(2 * ROWS * KEYS * (ROW + D_LAT)),
+        cost_estimate=cost(2 * ROWS * n * 2 * TOK * (ROW + D_LAT)),
         name="grads",
     )(*held(*es, *dps), *ms, mine, theirs, *held(qt, gt))
-    return res[:N_Z], res[N_Z:]
+    return res[:2], res[2:]
 
 
 def project_kernel(order, place, uk, uq, frequency, *refs):
-    n = (len(refs) - 6) // 2
+    dss, (near, far0, far1), refs = refs[:N_Z], refs[N_Z : N_Z + 3], refs[N_Z + 3 :]
+    kts = near[:, : 2 * TOK], far0[...], near[:, 2 * TOK :], far1[...]
+    outs, (ft, cg) = refs[:N_Y], refs[N_Y:]
     lane = lax.broadcasted_iota(jnp.int32, (HALF, TOK), 1)
-    dss, kts = refs[:n], refs[n : 2 * n]
-    outs, (ft, cg) = refs[2 * n : -2], refs[-2:]
-    for t in (1, 0):
+    angles, dqs = [], []
+    for t in range(2):
         c = place[2] if t == 0 else 1 - place[2]
         at = ((place[0] * N_XL + place[1]) * 2 + c) * 2
         block = jnp.where(lane < BLOCK, order[at], order[at + 1])
-        angle = (block * BLOCK + lane % BLOCK).astype(f32) * frequency[...]
-        cos, sin = jnp.cos(angle), jnp.sin(angle)
+        angles.append((block * BLOCK + lane % BLOCK).astype(f32) * frequency[...])
         half = slice(t * HROWS, (t + 1) * HROWS)
-        dq = sum(dot(kt[...], ds[:, half]) for kt, ds in zip(kts, dss)).astype(bf16)
-        out = slice(t * TOK, (t + 1) * TOK)
-        for h in range(HEADS_L):
-            d = dq[:, h * TOK : (h + 1) * TOK]
-            base = h * (D_NOPE + D_ROPE)
-            ft[base : base + D_NOPE, out] = dot(uk[h], d[:D_LAT]).astype(bf16)
-            a = d[D_LAT : D_LAT + HALF].astype(f32)
-            b = d[D_LAT + HALF :].astype(f32)
-            base += D_NOPE
-            ft[base : base + HALF, out] = (a * cos + b * sin).astype(bf16)
-            ft[base + HALF : base + D_ROPE, out] = (b * cos - a * sin).astype(bf16)
+        dqs.append(sum(dot(kt, ds[:, half]) for kt, ds in zip(kts, dss)).astype(bf16))
+    angle = jnp.concatenate(angles, axis=1)
+    cos, sin = jnp.cos(angle), jnp.sin(angle)
+    for h in range(HEADS_L):
+        d = jnp.concatenate([dq[:, h * TOK : (h + 1) * TOK] for dq in dqs], axis=1)
+        base = h * (D_NOPE + D_ROPE)
+        ft[base : base + D_NOPE, :] = dot(uk[h], d[:D_LAT]).astype(bf16)
+        a = d[D_LAT : D_LAT + HALF].astype(f32)
+        b = d[D_LAT + HALF :].astype(f32)
+        base += D_NOPE
+        ft[base : base + HALF, :] = (a * cos + b * sin).astype(bf16)
+        ft[base + HALF : base + D_ROPE, :] = (b * cos - a * sin).astype(bf16)
     cg[...] = dot(uq[...], ft[...]).astype(bf16)
     y, xh = place[3], place[4]
     for d in range(N_Y):
@@ -350,7 +335,7 @@
     return pl.pallas_call(
         project_kernel,
         out_shape=(like(2, N_XH, C_COLS, TOK),) * N_Y,
-        in_specs=[smem()] * 2 + [vmem()] * (3 + 2 * len(dss)),
+        in_specs=[smem()] * 2 + [vmem()] * (3 + len(dss) + len(kts)),
         out_specs=(vmem(),) * 4,
         scratch_shapes=[pltpu.VMEM((F_ROWS, 2 * TOK), bf16), pltpu.VMEM((q_rank, 2 * TOK), bf16)],
         compiler_params=params(12),
@@ -362,7 +347,7 @@
 def gather_kernel(p0, p1, p2, p3, *outs):
     for t in range(2):
         for k in range(N_XH):
-            a, b, c, d = (p[t, k].astype(f32) for p in (p0, p1, p2, p3))
+            a, b, d, c = (p[t, k].astype(f32) for p in (p0, p1, p2, p3))
             outs[2 * t + k][...] = ((a + c) + (b + d)).astype(bf16)
 
 
@@ -389,10 +374,10 @@
     own = latent_rows.T
     q_other = shift(queries, dcore=1)
     do_other = shift(output_grad, dcore=1)
-    kts = [own] + [shift(own, dz=dz) for dz, _ in SLOTS[1:N_Z]]
+    kts = [shift(own, dz=dz) if dz else own for dz, _ in SLOTS[:N_Z]]
     qt, gt, done = prologue(queries, q_other, output_grad, do_other, up_value)
-    for i, dx in enumerate((1, 3, 1, 3)):
-        kt = lax.optimization_barrier((kts[i], done))[0] if i else kts[0]
+    for (dz, _), kt, dx in zip(SLOTS, kts[:], (1, 3, 1, 3)):
+        kt = lax.optimization_barrier((kt, done))[0] if dz else kt
         kts.append(shift(kt, dx=dx))
 
     parts, kt_parts, mine = [], [], ()
@@ -404,19 +389,22 @@
         mine = (mine,)
     mine = mine[0]
     theirs = shift(mine, dcore=1)
-    dk, dss = grads(parts, mine, theirs, qt, gt)
-
-    from_z = [shift(dk[dz], dz=-dz) for dz in range(1, N_Z)]
-    a, b = (add(*(p[i] for p in (dk[0], *from_z))) for i in range(N_XL))
+    near, far0, far1 = parts
+    (dk1, dk3), dss = grads([(*near, 0), (*far0, 0)], mine, theirs, qt, gt)
+    (dk0, dk2), more = grads([(*near, 2), (*far1, 0)], mine, theirs, qt, gt)
+    dss = *dss, *more
+
+    from_z = [shift(dk, dz=-dz) for dz, dk in ((1, dk1), (3, dk3), (2, dk2))]
+    a, b = (add(*(p[i] for p in (dk0, *from_z))) for i in range(N_XL))
 
     cg = project(block_order, place, dss, kt_parts, up_key, up_query)
 
     b1, b3, a2 = shift(b, dx=1), shift(b, dx=3), shift(a, dx=2)
     total = ((a.astype(f32) + a2.astype(f32)) + (b1.astype(f32) + b3.astype(f32))).astype(bf16)
-    s1, s2, s3 = (shift(total, dy=d).astype(f32) for d in range(1, N_Y))
+    s1, s3, s2 = (shift(total, dy=d).astype(f32) for d in (1, 3, 2))
     total = ((total.astype(f32) + s2) + (s1 + s3)).astype(bf16)
 
-    keep, send, give_keep, give_send = gather(cg[0], *(shift(cg[d], dy=d) for d in range(1, N_Y)))
+    keep, send, give_keep, give_send = gather(cg[0], *(shift(cg[d], dy=d) for d in (1, 3, 2)))
     got = shift(send, dx=2), shift(give_keep, dcore=1), shift(give_send, dx=2, dcore=1)
     return add(keep, *got).T, total.T
 

time: 75.2 us -> 70.6 us (0.939)
  waiting for transfers between devices: 10.9 us -> 8.75 us
  starting transfers between devices: 38.4 us -> 36.5 us
  Pallas kernels: 22.9 us -> 22 us
    ppermute x25, waiting for transfers between devices: 10.9 us -> 8.75 us  [shift(): return lax.ppermute(x, AXES, pairs)]
    ppermute x25, starting transfers between devices: 38.4 us -> 36.5 us  [shift(): return lax.ppermute(x, AXES, pairs)]
    pallas_call x1 -> x2, Pallas kernels: 5.91 us -> 5.24 us  [grads(): pl.pallas_call(functools.partial(grads_kernel, picks), out_shape=(like(N_...]
  transfers between devices with their start and end apart: 25 -> 25, of which waited for: 8 -> 5; matrix products, arithmetic and copies ran while one was open for 1% -> 1% of each run, Pallas kernels for 20% -> 24%
where the time goes in v4:
time: 70.6 us; the launch traced here: 69.8 us
  starting transfers between devices  36.5 us (52%)
  Pallas kernels  22 us (31%)
  waiting for transfers between devices  8.75 us (12%)
  other arithmetic  1.63 us (2%)
  between operations  0.8 us (1%)
    ppermute x25, starting transfers between devices, shift(): return lax.ppermute(x, AXES, pairs)  36.5 us
    ppermute x25, waiting for transfers between devices, shift(): return lax.ppermute(x, AXES, pairs)  8.75 us
    pallas_call x3, Pallas kernels, scores(): pl.pallas_call(functools.partial(scores_kernel, slots), out_shape=(kept(n...  8.53 us
    pallas_call x2, Pallas kernels, grads(): pl.pallas_call(functools.partial(grads_kernel, picks), out_shape=(like(N_...  5.24 us
    pallas_call x1, Pallas kernels, project(): pl.pallas_call(project_kernel, out_shape=(like(2, N_XH, C_COLS, TOK),) *...  4.92 us
    pallas_call x1, Pallas kernels, prologue(): pl.pallas_call(prologue_kernel, out_shape=(kept(ROW, ROWS), kept(D_LAT, R...  3.17 us
  transfers between devices with their start and end apart: 25, of which 5 were waited for; matrix products, arithmetic and copies ran while one was open for 1% of the time, Pallas kernels for 24%

profile of v4, /device:TPU:0, one launch (start us, length us, event | category | flops | bytes accessed | tf_op | source)
XLA Modules:
  0.0 69.8 jit_solution(1888551616588101082)
XLA Ops:
  1.2 2.0 %collective-permute-start.2 = (bf16[576,128]{1,0:T(8,128)(2,1)}, bf16[576,128]{1,0:T(8,128)(2,1)S(1)}, u32[]{:S(2)}, u32[]{:S(2)}) collective-permute-start(bf16[576,128]{1,0:T(8,128)(2,1)} %bitcast.16), channel_id=1, source_target_pairs={{0,4},{1,5},{2,6},{3,7},{4,8},{5,9},{6,10},{7,11},{8,12},{9,13},{1... | collective-permute-start | bytes 442376 | tf_op jit(solution)/shard_map/ppermute | solution.py:61
  3.2 2.1 %collective-permute-start.3 = (bf16[576,128]{1,0:T(8,128)(2,1)}, bf16[576,128]{1,0:T(8,128)(2,1)S(1)}, u32[]{:S(2)}, u32[]{:S(2)}) collective-permute-start(bf16[576,128]{1,0:T(8,128)(2,1)} %bitcast.17), channel_id=1, source_target_pairs={{0,12},{1,13},{2,14},{3,15},{4,0},{5,1},{6,2},{7,3},{8,4},{9,5},{1... | collective-permute-start | bytes 442376 | tf_op jit(solution)/shard_map/ppermute | solution.py:61
  5.4 1.9 %collective-permute-start.4 = (bf16[576,128]{1,0:T(8,128)(2,1)}, bf16[576,128]{1,0:T(8,128)(2,1)S(1)}, u32[]{:S(2)}, u32[]{:S(2)}) collective-permute-start(bf16[576,128]{1,0:T(8,128)(2,1)} %bitcast.18), channel_id=1, source_target_pairs={{0,8},{1,9},{2,10},{3,11},{4,12},{5,13},{6,14},{7,15},{8,0},{9,1},... | collective-permute-start | bytes 442376 | tf_op jit(solution)/shard_map/ppermute | solution.py:61
  7.3 1.5 %collective-permute-start.7 = (bf16[576,128]{1,0:T(8,128)(2,1)}, bf16[576,128]{1,0:T(8,128)(2,1)S(1)}, u32[]{:S(2)}, u32[]{:S(2)}) collective-permute-start(bf16[576,128]{1,0:T(8,128)(2,1)} %bitcast.19), channel_id=1, source_target_pairs={{0,2},{1,3},{2,16},{3,17},{4,6},{5,7},{6,20},{7,21},{8,10},{9,11},... | collective-permute-start | bytes 442376 | tf_op jit(solution)/shard_map/ppermute | solution.py:61
  8.8 3.2 %prologue.1 = (bf16[576,2048]{1,0:T(8,128)(2,1)S(1)}, bf16[512,2048]{1,0:T(8,128)(2,1)S(1)}, f32[8,128]{1,0:T(8,128)}) custom-call(bf16[128,4608]{1,0:T(8,128)(2,1)} %q0.1, bf16[128,4608]{1,0:T(8,128)(2,1)S(1)} %collective-permute-done.q1, bf16[128,1024]{1,0:T(8,128)(2,1)} %do0.1, bf16[128,1024]{1,0:T(8,128)(2,1)S(1)} %collective-permute-done.1.do1, ...), custom_call_target="tpu_custom_call" | custom-call | flops 268435456 | bytes 1048576 | tf_op jit(solution)/shard_map/prologue/pallas_call | solution.py:134
  12.0 1.6 %collective-permute-start.5 = (bf16[576,128]{1,0:T(8,128)(2,1)S(1)}, bf16[576,128]{1,0:T(8,128)(2,1)S(1)}, u32[]{:S(2)}, u32[]{:S(2)}) collective-permute-start(bf16[576,128]{1,0:T(8,128)(2,1)S(1)} %collective-permute-done.2.refs_0_), channel_id=1, source_target_pairs={{0,2},{1,3},{2,16},{3,17},{4,6},{5,7},{6,20},{7,21},{8,10},{9,11},... | collective-permute-start | bytes 442376 | tf_op jit(solution)/shard_map/ppermute | solution.py:61
  13.6 1.7 %collective-permute-start.6 = (bf16[576,128]{1,0:T(8,128)(2,1)S(1)}, bf16[576,128]{1,0:T(8,128)(2,1)S(1)}, u32[]{:S(2)}, u32[]{:S(2)}) collective-permute-start(bf16[576,128]{1,0:T(8,128)(2,1)S(1)} %collective-permute-done.3.refs_1_), channel_id=1, source_target_pairs={{0,18},{1,19},{2,0},{3,1},{4,22},{5,23},{6,4},{7,5},{8,26},{9,27},... | collective-permute-start | bytes 442376 | tf_op jit(solution)/shard_map/ppermute | solution.py:61
  15.3 1.5 %collective-permute-start.8 = (bf16[576,128]{1,0:T(8,128)(2,1)S(1)}, bf16[576,128]{1,0:T(8,128)(2,1)S(1)}, u32[]{:S(2)}, u32[]{:S(2)}) collective-permute-start(bf16[576,128]{1,0:T(8,128)(2,1)S(1)} %collective-permute-done.4.refs_3_), channel_id=1, source_target_pairs={{0,18},{1,19},{2,0},{3,1},{4,22},{5,23},{6,4},{7,5},{8,26},{9,27},... | collective-permute-start | bytes 442376 | tf_op jit(solution)/shard_map/ppermute | solution.py:61
  16.8 3.9 %scores.3 = (bf16[512,2048]{1,0:T(8,128)(2,1)S(1)}, bf16[512,2048]{1,0:T(8,128)(2,1)S(1)}, bf16[576,512]{1,0:T(8,128)(2,1)S(1)}, f32[8,2048]{1,0:T(8,128)S(1)}, f32[8,2048]{1,0:T(8,128)S(1)}) custom-call(s32[32]{0:T(128)S(1)} %copy-done.1, s32[5]{0:T(128)S(1)} %stack.23.place, bf16[576,2048]{1,0:T(8,128)(2,1)S(1)} %get-tuple-element.39.qt.refs_8_, ...), custom_call_target="tpu_custom_call" | custom-call | flops 2281701376 | bytes 1048576 | tf_op jit(solution)/shard_map/scores/pallas_call | solution.py:220
  20.7 2.3 %scores.4 = (bf16[256,2048]{1,0:T(8,128)(2,1)S(1)}, bf16[256,2048]{1,0:T(8,128)(2,1)S(1)}, bf16[576,256]{1,0:T(8,128)(2,1)S(1)}, f32[8,2048]{1,0:T(8,128)S(1)}, f32[8,2048]{1,0:T(8,128)S(1)}) custom-call(s32[32]{0:T(128)S(1)} %copy-done.1, s32[5]{0:T(128)S(1)} %stack.23.place, bf16[576,2048]{1,0:T(8,128)(2,1)S(1)} %get-tuple-element.39.qt.refs_8_, ...), custom_call_target="tpu_custom_call" | custom-call | flops 1140850688 | bytes 1048576 | tf_op jit(solution)/shard_map/scores/pallas_call | solution.py:220
  23.0 2.3 %scores.5 = (bf16[256,2048]{1,0:T(8,128)(2,1)S(1)}, bf16[256,2048]{1,0:T(8,128)(2,1)S(1)}, bf16[576,256]{1,0:T(8,128)(2,1)S(1)}, f32[8,2048]{1,0:T(8,128)S(1)}, f32[8,2048]{1,0:T(8,128)S(1)}) custom-call(s32[32]{0:T(128)S(1)} %copy-done.1, s32[5]{0:T(128)S(1)} %stack.23.place, bf16[576,2048]{1,0:T(8,128)(2,1)S(1)} %get-tuple-element.39.qt.refs_8_, ...), custom_call_target="tpu_custom_call" | custom-call | flops 1140850688 | bytes 1048576 | tf_op jit(solution)/shard_map/scores/pallas_call | solution.py:220
  25.6 1.2 %collective-permute-done.9.refs_7_ = f32[8,2048]{1,0:T(8,128)S(1)} collective-permute-done((f32[8,2048]{1,0:T(8,128)S(1)}, f32[8,2048]{1,0:T(8,128)S(1)}, u32[]{:S(2)}, u32[]{:S(2)}) %collective-permute-start.9) | collective-permute-done | bytes 65568 | tf_op jit(solution)/shard_map/ppermute | solution.py:61
  26.9 2.6 %grads.3 = (bf16[2,576,128]{2,1,0:T(8,128)(2,1)S(1)}, bf16[2,576,128]{2,1,0:T(8,128)(2,1)S(1)}, bf16[256,2048]{1,0:T(8,128)(2,1)S(1)}, bf16[256,2048]{1,0:T(8,128)(2,1)S(1)}) custom-call(bf16[512,2048]{1,0:T(8,128)(2,1)S(1)} %get-tuple-element.41.refs_0_, bf16[256,2048]{1,0:T(8,128)(2,1)S(1)} %get-tuple-element.56.refs_1_, ...), custom_call_target="tpu_custom_call" | custom-call | flops 2281701376 | bytes 1048576 | tf_op jit(solution)/shard_map/grads/pallas_call | solution.py:278
  29.5 2.5 %collective-permute-start.18 = (bf16[2,576,128]{2,1,0:T(8,128)(2,1)S(1)}, bf16[2,576,128]{2,1,0:T(8,128)(2,1)S(1)}, u32[]{:S(2)}, u32[]{:S(2)}) collective-permute-start(bf16[2,576,128]{2,1,0:T(8,128)(2,1)S(1)} %get-tuple-element.75), channel_id=1, source_target_pairs={{0,8},{1,9},{2,10},{3,11},{4,12},{5,13},{6,14},{7,15},{8,0},{9,1},... | collective-permute-start | bytes 884744 | tf_op jit(solution)/shard_map/ppermute | solution.py:61
  32.1 2.6 %grads.2 = (bf16[2,576,128]{2,1,0:T(8,128)(2,1)S(1)}, bf16[2,576,128]{2,1,0:T(8,128)(2,1)S(1)}, bf16[256,2048]{1,0:T(8,128)(2,1)S(1)}, bf16[256,2048]{1,0:T(8,128)(2,1)S(1)}) custom-call(bf16[512,2048]{1,0:T(8,128)(2,1)S(1)} %get-tuple-element.41.refs_0_, bf16[256,2048]{1,0:T(8,128)(2,1)S(1)} %get-tuple-element.46.refs_1_, ...), custom_call_target="tpu_custom_call" | custom-call | flops 2281701376 | bytes 1048576 | tf_op jit(solution)/shard_map/grads/pallas_call | solution.py:278
  34.7 1.5 %collective-permute-start.16 = (bf16[2,576,128]{2,1,0:T(8,128)(2,1)S(1)}, bf16[2,576,128]{2,1,0:T(8,128)(2,1)S(1)}, u32[]{:S(2)}, u32[]{:S(2)}) collective-permute-start(bf16[2,576,128]{2,1,0:T(8,128)(2,1)S(1)} %get-tuple-element.73), channel_id=1, source_target_pairs={{0,12},{1,13},{2,14},{3,15},{4,0},{5,1},{6,2},{7,3},{8,4},{9,5},{1... | collective-permute-start | bytes 884744 | tf_op jit(solution)/shard_map/ppermute | solution.py:61
  36.9 4.9 %project.1 = (bf16[2,2,192,128]{3,2,1,0:T(8,128)(2,1)S(1)}, bf16[2,2,192,128]{3,2,1,0:T(8,128)(2,1)S(1)}, bf16[2,2,192,128]{3,2,1,0:T(8,128)(2,1)S(1)}, bf16[2,2,192,128]{3,2,1,0:T(8,128)(2,1)S(1)}) custom-call(s32[32]{0:T(128)S(1)} %copy-done.1, s32[5]{0:T(128)S(1)} %stack.23.place, bf16[8,128,512]{2,1,0:T(8,128)(2,1)S(1)} %copy-done, ...), custom_call_target="tpu_custom_call" | custom-call | flops 2415919104 | bytes 1048576 | tf_op jit(solution)/shard_map/project/pallas_call | solution.py:335
  41.8 1.6 %collective-permute-start.10 = (bf16[2,2,192,128]{3,2,1,0:T(8,128)(2,1)S(1)}, bf16[2,2,192,128]{3,2,1,0:T(8,128)(2,1)S(1)}, u32[]{:S(2)}, u32[]{:S(2)}) collective-permute-start(bf16[2,2,192,128]{3,2,1,0:T(8,128)(2,1)S(1)} %get-tuple-element.65), channel_id=1, source_target_pairs={{0,32},{1,33},{2,34},{3,35},{4,36},{5,37},{6,38},{7,39},{8,40},{9,... | collective-permute-start | bytes 589832 | tf_op jit(solution)/shard_map/ppermute | solution.py:61
  43.4 1.7 %collective-permute-start.11 = (bf16[2,2,192,128]{3,2,1,0:T(8,128)(2,1)S(1)}, bf16[2,2,192,128]{3,2,1,0:T(8,128)(2,1)S(1)}, u32[]{:S(2)}, u32[]{:S(2)}) collective-permute-start(bf16[2,2,192,128]{3,2,1,0:T(8,128)(2,1)S(1)} %get-tuple-element.66), channel_id=1, source_target_pairs={{0,96},{1,97},{2,98},{3,99},{4,100},{5,101},{6,102},{7,103},{8,104... | collective-permute-start | bytes 589832 | tf_op jit(solution)/shard_map/ppermute | solution.py:61
  45.1 2.0 %collective-permute-start.12 = (bf16[2,2,192,128]{3,2,1,0:T(8,128)(2,1)S(1)}, bf16[2,2,192,128]{3,2,1,0:T(8,128)(2,1)S(1)}, u32[]{:S(2)}, u32[]{:S(2)}) collective-permute-start(bf16[2,2,192,128]{3,2,1,0:T(8,128)(2,1)S(1)} %get-tuple-element.67), channel_id=1, source_target_pairs={{0,64},{1,65},{2,66},{3,67},{4,68},{5,69},{6,70},{7,71},{8,72},{9,... | collective-permute-start | bytes 589832 | tf_op jit(solution)/shard_map/ppermute | solution.py:61
  47.3 0.9 %collective-permute-start.19 = (bf16[576,128]{1,0:T(8,128)(2,1)S(1)}, bf16[576,128]{1,0:T(8,128)(2,1)S(1)}, u32[]{:S(2)}, u32[]{:S(2)}) collective-permute-start(bf16[576,128]{1,0:T(8,128)(2,1)S(1)} %get-tuple-element.76), channel_id=1, source_target_pairs={{0,16},{1,17},{2,18},{3,19},{4,20},{5,21},{6,22},{7,23},{8,24},{9,... | collective-permute-start | bytes 442376 | tf_op jit(solution)/shard_map/ppermute | solution.py:61
  48.2 1.7 %collective-permute-start.20 = (bf16[576,128]{1,0:T(8,128)(2,1)S(1)}, bf16[576,128]{1,0:T(8,128)(2,1)S(1)}, u32[]{:S(2)}, u32[]{:S(2)}) collective-permute-start(bf16[576,128]{1,0:T(8,128)(2,1)S(1)} %get-tuple-element.77), channel_id=1, source_target_pairs={{0,2},{1,3},{2,16},{3,17},{4,6},{5,7},{6,20},{7,21},{8,10},{9,11},... | collective-permute-start | bytes 442376 | tf_op jit(solution)/shard_map/ppermute | solution.py:61
  49.9 1.5 %collective-permute-start.21 = (bf16[576,128]{1,0:T(8,128)(2,1)S(1)}, bf16[576,128]{1,0:T(8,128)(2,1)S(1)}, u32[]{:S(2)}, u32[]{:S(2)}) collective-permute-start(bf16[576,128]{1,0:T(8,128)(2,1)S(1)} %get-tuple-element.77), channel_id=1, source_target_pairs={{0,18},{1,19},{2,0},{3,1},{4,22},{5,23},{6,4},{7,5},{8,26},{9,27},... | collective-permute-start | bytes 442376 | tf_op jit(solution)/shard_map/ppermute | solution.py:61
  51.4 1.5 %collective-permute-done.11.p2 = bf16[2,2,192,128]{3,2,1,0:T(8,128)(2,1)S(1)} collective-permute-done((bf16[2,2,192,128]{3,2,1,0:T(8,128)(2,1)S(1)}, bf16[2,2,192,128]{3,2,1,0:T(8,128)(2,1)S(1)}, u32[]{:S(2)}, u32[]{:S(2)}) %collective-permute-start.11) | collective-permute-done | bytes 196640 | tf_op jit(solution)/shard_map/ppermute | solution.py:61
  52.9 1.8 %collective-permute-done.12.p3 = bf16[2,2,192,128]{3,2,1,0:T(8,128)(2,1)S(1)} collective-permute-done((bf16[2,2,192,128]{3,2,1,0:T(8,128)(2,1)S(1)}, bf16[2,2,192,128]{3,2,1,0:T(8,128)(2,1)S(1)}, u32[]{:S(2)}, u32[]{:S(2)}) %collective-permute-start.12) | collective-permute-done | bytes 196640 | tf_op jit(solution)/shard_map/ppermute | solution.py:61
  54.8 0.9 %collective-permute-start.13 = (bf16[192,128]{1,0:T(8,128)(2,1)S(1)}, bf16[192,128]{1,0:T(8,128)(2,1)S(1)}, u32[]{:S(2)}, u32[]{:S(2)}) collective-permute-start(bf16[192,128]{1,0:T(8,128)(2,1)S(1)} %get-tuple-element.69), channel_id=1, source_target_pairs={{0,16},{1,17},{2,18},{3,19},{4,20},{5,21},{6,22},{7,23},{8,24},{9,... | collective-permute-start | bytes 147464 | tf_op jit(solution)/shard_map/ppermute | solution.py:61
  55.7 2.8 %collective-permute-start.15 = (bf16[192,128]{1,0:T(8,128)(2,1)S(1)}, bf16[192,128]{1,0:T(8,128)(2,1)S(1)}, u32[]{:S(2)}, u32[]{:S(2)}) collective-permute-start(bf16[192,128]{1,0:T(8,128)(2,1)S(1)} %get-tuple-element.71), channel_id=1, source_target_pairs={{0,17},{1,16},{2,19},{3,18},{4,21},{5,20},{6,23},{7,22},{8,25},{9,... | collective-permute-start | bytes 147464 | tf_op jit(solution)/shard_map/ppermute | solution.py:61
  58.6 2.4 %collective-permute-start.22 = (bf16[576,128]{1,0:T(8,128)(2,1)S(1)}, bf16[576,128]{1,0:T(8,128)(2,1)S(1)}, u32[]{:S(2)}, u32[]{:S(2)}) collective-permute-start(bf16[576,128]{1,0:T(8,128)(2,1)S(1)} %add_convert_fusion.1), channel_id=1, source_target_pairs={{0,64},{1,65},{2,66},{3,67},{4,68},{5,69},{6,70},{7,71},{8,72},{9,... | collective-permute-start | bytes 442376 | tf_op jit(solution)/shard_map/ppermute | solution.py:61
  61.4 2.8 %collective-permute-start.24 = (bf16[576,128]{1,0:T(8,128)(2,1)S(1)}, bf16[576,128]{1,0:T(8,128)(2,1)S(1)}, u32[]{:S(2)}, u32[]{:S(2)}) collective-permute-start(bf16[576,128]{1,0:T(8,128)(2,1)S(1)} %add_convert_fusion.1), channel_id=1, source_target_pairs={{0,96},{1,97},{2,98},{3,99},{4,100},{5,101},{6,102},{7,103},{8,104... | collective-permute-start | bytes 442376 | tf_op jit(solution)/shard_map/ppermute | solution.py:61
  64.9 2.0 %collective-permute-done.22 = bf16[576,128]{1,0:T(8,128)(2,1)S(1)} collective-permute-done((bf16[576,128]{1,0:T(8,128)(2,1)S(1)}, bf16[576,128]{1,0:T(8,128)(2,1)S(1)}, u32[]{:S(2)}, u32[]{:S(2)}) %collective-permute-start.22) | collective-permute-done | bytes 147488 | tf_op jit(solution)/shard_map/ppermute | solution.py:61
  66.9 2.2 %collective-permute-done.23 = bf16[576,128]{1,0:T(8,128)(2,1)S(1)} collective-permute-done((bf16[576,128]{1,0:T(8,128)(2,1)S(1)}, bf16[576,128]{1,0:T(8,128)(2,1)S(1)}, u32[]{:S(2)}, u32[]{:S(2)}) %collective-permute-start.23) | collective-permute-done | bytes 147488 | tf_op jit(solution)/shard_map/ppermute | solution.py:61
  69.1 0.7 %fusion.2 = bf16[128,576]{0,1:T(8,128)(2,1)} fusion(bf16[576,128]{1,0:T(8,128)(2,1)S(1)} %collective-permute-done.24, bf16[576,128]{1,0:T(8,128)(2,1)S(1)} %collective-permute-done.23, bf16[576,128]{1,0:T(8,128)(2,1)S(1)} %collective-permute-done.22, bf16[576,128]{1,0:T(8,128)(2,1)S(1)} %add_convert_fusion.1), kind=kLoop, calls=%fused_computation.6 | loop fusion | flops 589824 | bytes 737280 | tf_op jit(solution)/shard_map/transpose | solution.py:409
  (45 shorter events, 3.1 us)
Async XLA Ops:
  0.6 16.1 %copy-start.2 = (bf16[128,576]{0,1:T(8,128)(2,1)S(1)}, bf16[128,576]{0,1:T(8,128)(2,1)}, u32[]{:S(2)}) copy-start(bf16[128,576]{0,1:T(8,128)(2,1)} %param.9) | copy-start | bytes 442372
  0.6 16.1 %copy-start.1 = (s32[32]{0:T(128)S(1)}, s32[32]{0:T(128)}, u32[]{:S(2)}) copy-start(s32[32]{0:T(128)} %order.7) | copy-start | bytes 388
  0.7 8.2 %collective-permute-start = (bf16[128,4608]{1,0:T(8,128)(2,1)}, bf16[128,4608]{1,0:T(8,128)(2,1)S(1)}, u32[]{:S(2)}, u32[]{:S(2)}) collective-permute-start(bf16[128,4608]{1,0:T(8,128)(2,1)} %q0.1), channel_id=1, source_target_pairs={{0,1},{1,0},{2,3},{3,2},{4,5},{5,4},{6,7},{7,6},{8,9},{9,8},{10,11... | collective-permute-start | bytes 3538952 | tf_op jit(solution)/shard_map/ppermute | solution.py:61
  0.7 6.6 %collective-permute-start.1 = (bf16[128,1024]{1,0:T(8,128)(2,1)}, bf16[128,1024]{1,0:T(8,128)(2,1)S(1)}, u32[]{:S(2)}, u32[]{:S(2)}) collective-permute-start(bf16[128,1024]{1,0:T(8,128)(2,1)} %do0.1), channel_id=1, source_target_pairs={{0,1},{1,0},{2,3},{3,2},{4,5},{5,4},{6,7},{7,6},{8,9},{9,8},{10,11... | collective-permute-start | bytes 786440 | tf_op jit(solution)/shard_map/ppermute | solution.py:61
  1.2 10.8 %collective-permute-start.2 = (bf16[576,128]{1,0:T(8,128)(2,1)}, bf16[576,128]{1,0:T(8,128)(2,1)S(1)}, u32[]{:S(2)}, u32[]{:S(2)}) collective-permute-start(bf16[576,128]{1,0:T(8,128)(2,1)} %bitcast.16), channel_id=1, source_target_pairs={{0,4},{1,5},{2,6},{3,7},{4,8},{5,9},{6,10},{7,11},{8,12},{9,13},{1... | collective-permute-start | bytes 442376 | tf_op jit(solution)/shard_map/ppermute | solution.py:61
  3.2 10.3 %collective-permute-start.3 = (bf16[576,128]{1,0:T(8,128)(2,1)}, bf16[576,128]{1,0:T(8,128)(2,1)S(1)}, u32[]{:S(2)}, u32[]{:S(2)}) collective-permute-start(bf16[576,128]{1,0:T(8,128)(2,1)} %bitcast.17), channel_id=1, source_target_pairs={{0,12},{1,13},{2,14},{3,15},{4,0},{5,1},{6,2},{7,3},{8,4},{9,5},{1... | collective-permute-start | bytes 442376 | tf_op jit(solution)/shard_map/ppermute | solution.py:61
  5.4 10.0 %collective-permute-start.4 = (bf16[576,128]{1,0:T(8,128)(2,1)}, bf16[576,128]{1,0:T(8,128)(2,1)S(1)}, u32[]{:S(2)}, u32[]{:S(2)}) collective-permute-start(bf16[576,128]{1,0:T(8,128)(2,1)} %bitcast.18), channel_id=1, source_target_pairs={{0,8},{1,9},{2,10},{3,11},{4,12},{5,13},{6,14},{7,15},{8,0},{9,1},... | collective-permute-start | bytes 442376 | tf_op jit(solution)/shard_map/ppermute | solution.py:61
  7.3 15.7 %collective-permute-start.7 = (bf16[576,128]{1,0:T(8,128)(2,1)}, bf16[576,128]{1,0:T(8,128)(2,1)S(1)}, u32[]{:S(2)}, u32[]{:S(2)}) collective-permute-start(bf16[576,128]{1,0:T(8,128)(2,1)} %bitcast.19), channel_id=1, source_target_pairs={{0,2},{1,3},{2,16},{3,17},{4,6},{5,7},{6,20},{7,21},{8,10},{9,11},... | collective-permute-start | bytes 442376 | tf_op jit(solution)/shard_map/ppermute | solution.py:61
  12.0 8.7 %collective-permute-start.5 = (bf16[576,128]{1,0:T(8,128)(2,1)S(1)}, bf16[576,128]{1,0:T(8,128)(2,1)S(1)}, u32[]{:S(2)}, u32[]{:S(2)}) collective-permute-start(bf16[576,128]{1,0:T(8,128)(2,1)S(1)} %collective-permute-done.2.refs_0_), channel_id=1, source_target_pairs={{0,2},{1,3},{2,16},{3,17},{4,6},{5,7},{6,20},{7,21},{8,10},{9,11},... | collective-permute-start | bytes 442376 | tf_op jit(solution)/shard_map/ppermute | solution.py:61
  13.6 7.1 %collective-permute-start.6 = (bf16[576,128]{1,0:T(8,128)(2,1)S(1)}, bf16[576,128]{1,0:T(8,128)(2,1)S(1)}, u32[]{:S(2)}, u32[]{:S(2)}) collective-permute-start(bf16[576,128]{1,0:T(8,128)(2,1)S(1)} %collective-permute-done.3.refs_1_), channel_id=1, source_target_pairs={{0,18},{1,19},{2,0},{3,1},{4,22},{5,23},{6,4},{7,5},{8,26},{9,27},... | collective-permute-start | bytes 442376 | tf_op jit(solution)/shard_map/ppermute | solution.py:61
  15.3 7.7 %collective-permute-start.8 = (bf16[576,128]{1,0:T(8,128)(2,1)S(1)}, bf16[576,128]{1,0:T(8,128)(2,1)S(1)}, u32[]{:S(2)}, u32[]{:S(2)}) collective-permute-start(bf16[576,128]{1,0:T(8,128)(2,1)S(1)} %collective-permute-done.4.refs_3_), channel_id=1, source_target_pairs={{0,18},{1,19},{2,0},{3,1},{4,22},{5,23},{6,4},{7,5},{8,26},{9,27},... | collective-permute-start | bytes 442376 | tf_op jit(solution)/shard_map/ppermute | solution.py:61
  25.4 1.5 %collective-permute-start.9 = (f32[8,2048]{1,0:T(8,128)S(1)}, f32[8,2048]{1,0:T(8,128)S(1)}, u32[]{:S(2)}, u32[]{:S(2)}) collective-permute-start(f32[8,2048]{1,0:T(8,128)S(1)} %get-tuple-element.53.refs_6_), channel_id=1, source_target_pairs={{0,1},{1,0},{2,3},{3,2},{4,5},{5,4},{6,7},{7,6},{8,9},{9,8},{10,11... | collective-permute-start | bytes 196616 | tf_op jit(solution)/shard_map/ppermute | solution.py:61
  29.5 15.6 %collective-permute-start.18 = (bf16[2,576,128]{2,1,0:T(8,128)(2,1)S(1)}, bf16[2,576,128]{2,1,0:T(8,128)(2,1)S(1)}, u32[]{:S(2)}, u32[]{:S(2)}) collective-permute-start(bf16[2,576,128]{2,1,0:T(8,128)(2,1)S(1)} %get-tuple-element.75), channel_id=1, source_target_pairs={{0,8},{1,9},{2,10},{3,11},{4,12},{5,13},{6,14},{7,15},{8,0},{9,1},... | collective-permute-start | bytes 884744 | tf_op jit(solution)/shard_map/ppermute | solution.py:61
  32.0 4.8 %slice-start = ((s8[4718592]{0:T(1024)(128)(4,1)}), s8[4194304]{0:T(1024)(128)(4,1)S(1)}, s32[]{:S(2)}) async-start(s8[4718592]{0:T(1024)(128)(4,1)} %bitcast.14), calls=%async_computation | async-start | bytes 8388608
  32.1 4.7 %copy-start.3 = (f32[32]{0:T(128)S(1)}, f32[32]{0:T(128)}, u32[]{:S(2)}) copy-start(f32[32]{0:T(128)} %constant.21.clone) | copy-start | bytes 388
  32.1 4.8 %slice-start.1 = ((s8[4718592]{0:T(1024)(128)(4,1)}), s8[524288]{0:T(1024)(128)(4,1)S(1)}, s32[]{:S(2)}) async-start(s8[4718592]{0:T(1024)(128)(4,1)} %bitcast.14), calls=%async_computation.1 | async-start | bytes 1048576
  32.1 4.8 %copy-start = (bf16[8,128,512]{2,1,0:T(8,128)(2,1)S(1)}, bf16[8,128,512]{2,1,0:T(8,128)(2,1)}, u32[]{:S(2)}) copy-start(bf16[8,128,512]{2,1,0:T(8,128)(2,1)} %uk.1) | copy-start | bytes 3145732
  34.7 12.4 %collective-permute-start.16 = (bf16[2,576,128]{2,1,0:T(8,128)(2,1)S(1)}, bf16[2,576,128]{2,1,0:T(8,128)(2,1)S(1)}, u32[]{:S(2)}, u32[]{:S(2)}) collective-permute-start(bf16[2,576,128]{2,1,0:T(8,128)(2,1)S(1)} %get-tuple-element.73), channel_id=1, source_target_pairs={{0,12},{1,13},{2,14},{3,15},{4,0},{5,1},{6,2},{7,3},{8,4},{9,5},{1... | collective-permute-start | bytes 884744 | tf_op jit(solution)/shard_map/ppermute | solution.py:61
  36.1 11.0 %collective-permute-start.17 = (bf16[2,576,128]{2,1,0:T(8,128)(2,1)S(1)}, bf16[2,576,128]{2,1,0:T(8,128)(2,1)S(1)}, u32[]{:S(2)}, u32[]{:S(2)}) collective-permute-start(bf16[2,576,128]{2,1,0:T(8,128)(2,1)S(1)} %get-tuple-element.74), channel_id=1, source_target_pairs={{0,4},{1,5},{2,6},{3,7},{4,8},{5,9},{6,10},{7,11},{8,12},{9,13},{1... | collective-permute-start | bytes 884744 | tf_op jit(solution)/shard_map/ppermute | solution.py:61
  41.8 8.1 %collective-permute-start.10 = (bf16[2,2,192,128]{3,2,1,0:T(8,128)(2,1)S(1)}, bf16[2,2,192,128]{3,2,1,0:T(8,128)(2,1)S(1)}, u32[]{:S(2)}, u32[]{:S(2)}) collective-permute-start(bf16[2,2,192,128]{3,2,1,0:T(8,128)(2,1)S(1)} %get-tuple-element.65), channel_id=1, source_target_pairs={{0,32},{1,33},{2,34},{3,35},{4,36},{5,37},{6,38},{7,39},{8,40},{9,... | collective-permute-start | bytes 589832 | tf_op jit(solution)/shard_map/ppermute | solution.py:61
  43.4 9.4 %collective-permute-start.11 = (bf16[2,2,192,128]{3,2,1,0:T(8,128)(2,1)S(1)}, bf16[2,2,192,128]{3,2,1,0:T(8,128)(2,1)S(1)}, u32[]{:S(2)}, u32[]{:S(2)}) collective-permute-start(bf16[2,2,192,128]{3,2,1,0:T(8,128)(2,1)S(1)} %get-tuple-element.66), channel_id=1, source_target_pairs={{0,96},{1,97},{2,98},{3,99},{4,100},{5,101},{6,102},{7,103},{8,104... | collective-permute-start | bytes 589832 | tf_op jit(solution)/shard_map/ppermute | solution.py:61
  45.1 9.6 %collective-permute-start.12 = (bf16[2,2,192,128]{3,2,1,0:T(8,128)(2,1)S(1)}, bf16[2,2,192,128]{3,2,1,0:T(8,128)(2,1)S(1)}, u32[]{:S(2)}, u32[]{:S(2)}) collective-permute-start(bf16[2,2,192,128]{3,2,1,0:T(8,128)(2,1)S(1)} %get-tuple-element.67), channel_id=1, source_target_pairs={{0,64},{1,65},{2,66},{3,67},{4,68},{5,69},{6,70},{7,71},{8,72},{9,... | collective-permute-start | bytes 589832 | tf_op jit(solution)/shard_map/ppermute | solution.py:61
  47.3 8.4 %collective-permute-start.19 = (bf16[576,128]{1,0:T(8,128)(2,1)S(1)}, bf16[576,128]{1,0:T(8,128)(2,1)S(1)}, u32[]{:S(2)}, u32[]{:S(2)}) collective-permute-start(bf16[576,128]{1,0:T(8,128)(2,1)S(1)} %get-tuple-element.76), channel_id=1, source_target_pairs={{0,16},{1,17},{2,18},{3,19},{4,20},{5,21},{6,22},{7,23},{8,24},{9,... | collective-permute-start | bytes 442376 | tf_op jit(solution)/shard_map/ppermute | solution.py:61
  48.2 10.3 %collective-permute-start.20 = (bf16[576,128]{1,0:T(8,128)(2,1)S(1)}, bf16[576,128]{1,0:T(8,128)(2,1)S(1)}, u32[]{:S(2)}, u32[]{:S(2)}) collective-permute-start(bf16[576,128]{1,0:T(8,128)(2,1)S(1)} %get-tuple-element.77), channel_id=1, source_target_pairs={{0,2},{1,3},{2,16},{3,17},{4,6},{5,7},{6,20},{7,21},{8,10},{9,11},... | collective-permute-start | bytes 442376 | tf_op jit(solution)/shard_map/ppermute | solution.py:61
  49.9 8.6 %collective-permute-start.21 = (bf16[576,128]{1,0:T(8,128)(2,1)S(1)}, bf16[576,128]{1,0:T(8,128)(2,1)S(1)}, u32[]{:S(2)}, u32[]{:S(2)}) collective-permute-start(bf16[576,128]{1,0:T(8,128)(2,1)S(1)} %get-tuple-element.77), channel_id=1, source_target_pairs={{0,18},{1,19},{2,0},{3,1},{4,22},{5,23},{6,4},{7,5},{8,26},{9,27},... | collective-permute-start | bytes 442376 | tf_op jit(solution)/shard_map/ppermute | solution.py:61
  54.8 6.6 %collective-permute-start.13 = (bf16[192,128]{1,0:T(8,128)(2,1)S(1)}, bf16[192,128]{1,0:T(8,128)(2,1)S(1)}, u32[]{:S(2)}, u32[]{:S(2)}) collective-permute-start(bf16[192,128]{1,0:T(8,128)(2,1)S(1)} %get-tuple-element.69), channel_id=1, source_target_pairs={{0,16},{1,17},{2,18},{3,19},{4,20},{5,21},{6,22},{7,23},{8,24},{9,... | collective-permute-start | bytes 147464 | tf_op jit(solution)/shard_map/ppermute | solution.py:61
  55.7 8.6 %collective-permute-start.14 = (bf16[192,128]{1,0:T(8,128)(2,1)S(1)}, bf16[192,128]{1,0:T(8,128)(2,1)S(1)}, u32[]{:S(2)}, u32[]{:S(2)}) collective-permute-start(bf16[192,128]{1,0:T(8,128)(2,1)S(1)} %get-tuple-element.70), channel_id=1, source_target_pairs={{0,1},{1,0},{2,3},{3,2},{4,5},{5,4},{6,7},{7,6},{8,9},{9,8},{10,11... | collective-permute-start | bytes 147464 | tf_op jit(solution)/shard_map/ppermute | solution.py:61
  55.7 8.6 %collective-permute-start.15 = (bf16[192,128]{1,0:T(8,128)(2,1)S(1)}, bf16[192,128]{1,0:T(8,128)(2,1)S(1)}, u32[]{:S(2)}, u32[]{:S(2)}) collective-permute-start(bf16[192,128]{1,0:T(8,128)(2,1)S(1)} %get-tuple-element.71), channel_id=1, source_target_pairs={{0,17},{1,16},{2,19},{3,18},{4,21},{5,20},{6,23},{7,22},{8,25},{9,... | collective-permute-start | bytes 147464 | tf_op jit(solution)/shard_map/ppermute | solution.py:61
  58.6 8.3 %collective-permute-start.22 = (bf16[576,128]{1,0:T(8,128)(2,1)S(1)}, bf16[576,128]{1,0:T(8,128)(2,1)S(1)}, u32[]{:S(2)}, u32[]{:S(2)}) collective-permute-start(bf16[576,128]{1,0:T(8,128)(2,1)S(1)} %add_convert_fusion.1), channel_id=1, source_target_pairs={{0,64},{1,65},{2,66},{3,67},{4,68},{5,69},{6,70},{7,71},{8,72},{9,... | collective-permute-start | bytes 442376 | tf_op jit(solution)/shard_map/ppermute | solution.py:61
  61.0 8.1 %collective-permute-start.23 = (bf16[576,128]{1,0:T(8,128)(2,1)S(1)}, bf16[576,128]{1,0:T(8,128)(2,1)S(1)}, u32[]{:S(2)}, u32[]{:S(2)}) collective-permute-start(bf16[576,128]{1,0:T(8,128)(2,1)S(1)} %add_convert_fusion.1), channel_id=1, source_target_pairs={{0,32},{1,33},{2,34},{3,35},{4,36},{5,37},{6,38},{7,39},{8,40},{9,... | collective-permute-start | bytes 442376 | tf_op jit(solution)/shard_map/ppermute | solution.py:61
  61.4 7.7 %collective-permute-start.24 = (bf16[576,128]{1,0:T(8,128)(2,1)S(1)}, bf16[576,128]{1,0:T(8,128)(2,1)S(1)}, u32[]{:S(2)}, u32[]{:S(2)}) collective-permute-start(bf16[576,128]{1,0:T(8,128)(2,1)S(1)} %add_convert_fusion.1), channel_id=1, source_target_pairs={{0,96},{1,97},{2,98},{3,99},{4,100},{5,101},{6,102},{7,103},{8,104... | collective-permute-start | bytes 442376 | tf_op jit(solution)/shard_map/ppermute | solution.py:61

commit v5 on v4

--- a/solution.py
+++ b/solution.py
@@ -31,6 +31,7 @@
 MASKED = -1e30
 AXES = ("y", "xh", "z", "xl", "core")
 TN = 256
+CUTS = 4
 
 SLOTS = ((1, 0), (3, 0), (0, 0), (2, 0), (1, 1), (3, 1), (0, 1), (2, 1))
 GROUPS = ((0, 1, 2, 3), (4, 5), (6, 7))
@@ -98,12 +99,17 @@
 
 
 def prologue_kernel(q0, q1, do0, do1, uv_hbm, qt, gt, done, q_own, do_own, uv, sems):
-    copies = [
-        pltpu.make_async_copy(src, dst, sems.at[i])
-        for i, (src, dst) in enumerate(((uv_hbm, uv), (do0, do_own), (q0, q_own)))
-    ]
-    for c in copies:
-        c.start()
+    copies = []
+    for i, (src, dst) in enumerate(((uv_hbm, uv), (do0, do_own), (q0, q_own))):
+        part = src.shape[0] // CUTS
+        for k in range(CUTS):
+            rows = pl.ds(k * part, part)
+            copies.append(pltpu.make_async_copy(src.at[rows], dst.at[rows], sems.at[i, k]))
+            copies[-1].start()
+
+    def wait(i):
+        for c in copies[i * CUTS : (i + 1) * CUTS]:
+            c.wait()
 
     def transpose(s, q):
         for j in range(HEADS_L * ROW // 128):
@@ -121,11 +127,11 @@
             gt[:, col : col + TOK] = g.astype(bf16)
 
     transpose(1, q1)
-    copies[0].wait()
+    wait(0)
     value_grad(1, do1)
-    copies[1].wait()
+    wait(1)
     value_grad(0, do_own)
-    copies[2].wait()
+    wait(2)
     transpose(0, q_own)
     done[...] = jnp.zeros_like(done)
 
@@ -140,7 +146,7 @@
             pltpu.VMEM(q0.shape, bf16),
             pltpu.VMEM(do0.shape, bf16),
             pltpu.VMEM(uv.shape, bf16),
-            pltpu.SemaphoreType.DMA((3,)),
+            pltpu.SemaphoreType.DMA((3, CUTS)),
         ],
         compiler_params=params(10),
         cost_estimate=cost(2 * ROWS * D_V * D_LAT),
@@ -347,7 +353,7 @@
 def gather_kernel(p0, p1, p2, p3, *outs):
     for t in range(2):
         for k in range(N_XH):
-            a, b, d, c = (p[t, k].astype(f32) for p in (p0, p1, p2, p3))
+            a, c, b, d = (p[t, k].astype(f32) for p in (p0, p1, p2, p3))
             outs[2 * t + k][...] = ((a + c) + (b + d)).astype(bf16)
 
 
@@ -404,7 +410,7 @@
     s1, s3, s2 = (shift(total, dy=d).astype(f32) for d in (1, 3, 2))
     total = ((total.astype(f32) + s2) + (s1 + s3)).astype(bf16)
 
-    keep, send, give_keep, give_send = gather(cg[0], *(shift(cg[d], dy=d) for d in (1, 3, 2)))
+    keep, send, give_keep, give_send = gather(cg[0], *(shift(cg[d], dy=d) for d in (2, 1, 3)))
     got = shift(send, dx=2), shift(give_keep, dcore=1), shift(give_send, dx=2, dcore=1)
     return add(keep, *got).T, total.T
 

time: 70.6 us -> 70.1 us (level)
  transfers between devices with their start and end apart: 25 -> 25, of which waited for: 5 -> 7; matrix products, arithmetic and copies ran while one was open for 1% -> 2% of each run, Pallas kernels for 24% -> 25%
where the time goes in v5:
time: 70.1 us; the launch traced here: 69.3 us
  starting transfers between devices  36.3 us (52%)
  Pallas kernels  22 us (31%)
  waiting for transfers between devices  8.36 us (12%)
  other arithmetic  1.63 us (2%)
  between operations  0.8 us (1%)
    ppermute x25, starting transfers between devices, shift(): return lax.ppermute(x, AXES, pairs)  36.3 us
    pallas_call x3, Pallas kernels, scores(): pl.pallas_call(functools.partial(scores_kernel, slots), out_shape=(kept(n...  8.53 us
    ppermute x25, waiting for transfers between devices, shift(): return lax.ppermute(x, AXES, pairs)  8.36 us
    pallas_call x2, Pallas kernels, grads(): pl.pallas_call(functools.partial(grads_kernel, picks), out_shape=(like(N_...  5.24 us
    pallas_call x1, Pallas kernels, project(): pl.pallas_call(project_kernel, out_shape=(like(2, N_XH, C_COLS, TOK),) *...  4.92 us
    pallas_call x1, Pallas kernels, prologue(): pl.pallas_call(prologue_kernel, out_shape=(kept(ROW, ROWS), kept(D_LAT, R...  3.22 us
  transfers between devices with their start and end apart: 25, of which 7 were waited for; matrix products, arithmetic and copies ran while one was open for 2% of the time, Pallas kernels for 25%

profile of v5, /device:TPU:0, one launch (start us, length us, event | category | flops | bytes accessed | tf_op | source)
XLA Modules:
  0.0 69.3 jit_solution(1004033135546014454)
XLA Ops:
  1.2 2.0 %collective-permute-start.2 = (bf16[576,128]{1,0:T(8,128)(2,1)}, bf16[576,128]{1,0:T(8,128)(2,1)S(1)}, u32[]{:S(2)}, u32[]{:S(2)}) collective-permute-start(bf16[576,128]{1,0:T(8,128)(2,1)} %bitcast.16), channel_id=1, source_target_pairs={{0,4},{1,5},{2,6},{3,7},{4,8},{5,9},{6,10},{7,11},{8,12},{9,13},{1... | collective-permute-start | bytes 442376 | tf_op jit(solution)/shard_map/ppermute | solution.py:62
  3.2 2.1 %collective-permute-start.3 = (bf16[576,128]{1,0:T(8,128)(2,1)}, bf16[576,128]{1,0:T(8,128)(2,1)S(1)}, u32[]{:S(2)}, u32[]{:S(2)}) collective-permute-start(bf16[576,128]{1,0:T(8,128)(2,1)} %bitcast.17), channel_id=1, source_target_pairs={{0,12},{1,13},{2,14},{3,15},{4,0},{5,1},{6,2},{7,3},{8,4},{9,5},{1... | collective-permute-start | bytes 442376 | tf_op jit(solution)/shard_map/ppermute | solution.py:62
  5.4 1.9 %collective-permute-start.4 = (bf16[576,128]{1,0:T(8,128)(2,1)}, bf16[576,128]{1,0:T(8,128)(2,1)S(1)}, u32[]{:S(2)}, u32[]{:S(2)}) collective-permute-start(bf16[576,128]{1,0:T(8,128)(2,1)} %bitcast.18), channel_id=1, source_target_pairs={{0,8},{1,9},{2,10},{3,11},{4,12},{5,13},{6,14},{7,15},{8,0},{9,1},... | collective-permute-start | bytes 442376 | tf_op jit(solution)/shard_map/ppermute | solution.py:62
  7.3 1.5 %collective-permute-start.7 = (bf16[576,128]{1,0:T(8,128)(2,1)}, bf16[576,128]{1,0:T(8,128)(2,1)S(1)}, u32[]{:S(2)}, u32[]{:S(2)}) collective-permute-start(bf16[576,128]{1,0:T(8,128)(2,1)} %bitcast.19), channel_id=1, source_target_pairs={{0,2},{1,3},{2,16},{3,17},{4,6},{5,7},{6,20},{7,21},{8,10},{9,11},... | collective-permute-start | bytes 442376 | tf_op jit(solution)/shard_map/ppermute | solution.py:62
  8.8 3.2 %prologue.1 = (bf16[576,2048]{1,0:T(8,128)(2,1)S(1)}, bf16[512,2048]{1,0:T(8,128)(2,1)S(1)}, f32[8,128]{1,0:T(8,128)}) custom-call(bf16[128,4608]{1,0:T(8,128)(2,1)} %q0.1, bf16[128,4608]{1,0:T(8,128)(2,1)S(1)} %collective-permute-done.q1, bf16[128,1024]{1,0:T(8,128)(2,1)} %do0.1, bf16[128,1024]{1,0:T(8,128)(2,1)S(1)} %collective-permute-done.1.do1, ...), custom_call_target="tpu_custom_call" | custom-call | flops 268435456 | bytes 1048576 | tf_op jit(solution)/shard_map/prologue/pallas_call | solution.py:140
  12.1 1.6 %collective-permute-start.5 = (bf16[576,128]{1,0:T(8,128)(2,1)S(1)}, bf16[576,128]{1,0:T(8,128)(2,1)S(1)}, u32[]{:S(2)}, u32[]{:S(2)}) collective-permute-start(bf16[576,128]{1,0:T(8,128)(2,1)S(1)} %collective-permute-done.2.refs_0_), channel_id=1, source_target_pairs={{0,2},{1,3},{2,16},{3,17},{4,6},{5,7},{6,20},{7,21},{8,10},{9,11},... | collective-permute-start | bytes 442376 | tf_op jit(solution)/shard_map/ppermute | solution.py:62
  13.6 1.7 %collective-permute-start.6 = (bf16[576,128]{1,0:T(8,128)(2,1)S(1)}, bf16[576,128]{1,0:T(8,128)(2,1)S(1)}, u32[]{:S(2)}, u32[]{:S(2)}) collective-permute-start(bf16[576,128]{1,0:T(8,128)(2,1)S(1)} %collective-permute-done.3.refs_1_), channel_id=1, source_target_pairs={{0,18},{1,19},{2,0},{3,1},{4,22},{5,23},{6,4},{7,5},{8,26},{9,27},... | collective-permute-start | bytes 442376 | tf_op jit(solution)/shard_map/ppermute | solution.py:62
  15.4 1.4 %collective-permute-start.8 = (bf16[576,128]{1,0:T(8,128)(2,1)S(1)}, bf16[576,128]{1,0:T(8,128)(2,1)S(1)}, u32[]{:S(2)}, u32[]{:S(2)}) collective-permute-start(bf16[576,128]{1,0:T(8,128)(2,1)S(1)} %collective-permute-done.4.refs_3_), channel_id=1, source_target_pairs={{0,18},{1,19},{2,0},{3,1},{4,22},{5,23},{6,4},{7,5},{8,26},{9,27},... | collective-permute-start | bytes 442376 | tf_op jit(solution)/shard_map/ppermute | solution.py:62
  16.8 3.9 %scores.3 = (bf16[512,2048]{1,0:T(8,128)(2,1)S(1)}, bf16[512,2048]{1,0:T(8,128)(2,1)S(1)}, bf16[576,512]{1,0:T(8,128)(2,1)S(1)}, f32[8,2048]{1,0:T(8,128)S(1)}, f32[8,2048]{1,0:T(8,128)S(1)}) custom-call(s32[32]{0:T(128)S(1)} %copy-done.1, s32[5]{0:T(128)S(1)} %stack.23.place, bf16[576,2048]{1,0:T(8,128)(2,1)S(1)} %get-tuple-element.39.qt.refs_8_, ...), custom_call_target="tpu_custom_call" | custom-call | flops 2281701376 | bytes 1048576 | tf_op jit(solution)/shard_map/scores/pallas_call | solution.py:226
  20.7 2.3 %scores.4 = (bf16[256,2048]{1,0:T(8,128)(2,1)S(1)}, bf16[256,2048]{1,0:T(8,128)(2,1)S(1)}, bf16[576,256]{1,0:T(8,128)(2,1)S(1)}, f32[8,2048]{1,0:T(8,128)S(1)}, f32[8,2048]{1,0:T(8,128)S(1)}) custom-call(s32[32]{0:T(128)S(1)} %copy-done.1, s32[5]{0:T(128)S(1)} %stack.23.place, bf16[576,2048]{1,0:T(8,128)(2,1)S(1)} %get-tuple-element.39.qt.refs_8_, ...), custom_call_target="tpu_custom_call" | custom-call | flops 1140850688 | bytes 1048576 | tf_op jit(solution)/shard_map/scores/pallas_call | solution.py:226
  23.0 2.3 %scores.5 = (bf16[256,2048]{1,0:T(8,128)(2,1)S(1)}, bf16[256,2048]{1,0:T(8,128)(2,1)S(1)}, bf16[576,256]{1,0:T(8,128)(2,1)S(1)}, f32[8,2048]{1,0:T(8,128)S(1)}, f32[8,2048]{1,0:T(8,128)S(1)}) custom-call(s32[32]{0:T(128)S(1)} %copy-done.1, s32[5]{0:T(128)S(1)} %stack.23.place, bf16[576,2048]{1,0:T(8,128)(2,1)S(1)} %get-tuple-element.39.qt.refs_8_, ...), custom_call_target="tpu_custom_call" | custom-call | flops 1140850688 | bytes 1048576 | tf_op jit(solution)/shard_map/scores/pallas_call | solution.py:226
  25.6 1.2 %collective-permute-done.9.refs_7_ = f32[8,2048]{1,0:T(8,128)S(1)} collective-permute-done((f32[8,2048]{1,0:T(8,128)S(1)}, f32[8,2048]{1,0:T(8,128)S(1)}, u32[]{:S(2)}, u32[]{:S(2)}) %collective-permute-start.9) | collective-permute-done | bytes 65568 | tf_op jit(solution)/shard_map/ppermute | solution.py:62
  26.9 2.6 %grads.3 = (bf16[2,576,128]{2,1,0:T(8,128)(2,1)S(1)}, bf16[2,576,128]{2,1,0:T(8,128)(2,1)S(1)}, bf16[256,2048]{1,0:T(8,128)(2,1)S(1)}, bf16[256,2048]{1,0:T(8,128)(2,1)S(1)}) custom-call(bf16[512,2048]{1,0:T(8,128)(2,1)S(1)} %get-tuple-element.41.refs_0_, bf16[256,2048]{1,0:T(8,128)(2,1)S(1)} %get-tuple-element.56.refs_1_, ...), custom_call_target="tpu_custom_call" | custom-call | flops 2281701376 | bytes 1048576 | tf_op jit(solution)/shard_map/grads/pallas_call | solution.py:284
  29.5 2.5 %collective-permute-start.18 = (bf16[2,576,128]{2,1,0:T(8,128)(2,1)S(1)}, bf16[2,576,128]{2,1,0:T(8,128)(2,1)S(1)}, u32[]{:S(2)}, u32[]{:S(2)}) collective-permute-start(bf16[2,576,128]{2,1,0:T(8,128)(2,1)S(1)} %get-tuple-element.75), channel_id=1, source_target_pairs={{0,8},{1,9},{2,10},{3,11},{4,12},{5,13},{6,14},{7,15},{8,0},{9,1},... | collective-permute-start | bytes 884744 | tf_op jit(solution)/shard_map/ppermute | solution.py:62
  32.1 2.6 %grads.2 = (bf16[2,576,128]{2,1,0:T(8,128)(2,1)S(1)}, bf16[2,576,128]{2,1,0:T(8,128)(2,1)S(1)}, bf16[256,2048]{1,0:T(8,128)(2,1)S(1)}, bf16[256,2048]{1,0:T(8,128)(2,1)S(1)}) custom-call(bf16[512,2048]{1,0:T(8,128)(2,1)S(1)} %get-tuple-element.41.refs_0_, bf16[256,2048]{1,0:T(8,128)(2,1)S(1)} %get-tuple-element.46.refs_1_, ...), custom_call_target="tpu_custom_call" | custom-call | flops 2281701376 | bytes 1048576 | tf_op jit(solution)/shard_map/grads/pallas_call | solution.py:284
  34.7 1.5 %collective-permute-start.16 = (bf16[2,576,128]{2,1,0:T(8,128)(2,1)S(1)}, bf16[2,576,128]{2,1,0:T(8,128)(2,1)S(1)}, u32[]{:S(2)}, u32[]{:S(2)}) collective-permute-start(bf16[2,576,128]{2,1,0:T(8,128)(2,1)S(1)} %get-tuple-element.73), channel_id=1, source_target_pairs={{0,12},{1,13},{2,14},{3,15},{4,0},{5,1},{6,2},{7,3},{8,4},{9,5},{1... | collective-permute-start | bytes 884744 | tf_op jit(solution)/shard_map/ppermute | solution.py:62
  36.9 4.9 %project.1 = (bf16[2,2,192,128]{3,2,1,0:T(8,128)(2,1)S(1)}, bf16[2,2,192,128]{3,2,1,0:T(8,128)(2,1)S(1)}, bf16[2,2,192,128]{3,2,1,0:T(8,128)(2,1)S(1)}, bf16[2,2,192,128]{3,2,1,0:T(8,128)(2,1)S(1)}) custom-call(s32[32]{0:T(128)S(1)} %copy-done.1, s32[5]{0:T(128)S(1)} %stack.23.place, bf16[8,128,512]{2,1,0:T(8,128)(2,1)S(1)} %copy-done, ...), custom_call_target="tpu_custom_call" | custom-call | flops 2415919104 | bytes 1048576 | tf_op jit(solution)/shard_map/project/pallas_call | solution.py:341
  41.8 3.3 %collective-permute-start.10 = (bf16[2,2,192,128]{3,2,1,0:T(8,128)(2,1)S(1)}, bf16[2,2,192,128]{3,2,1,0:T(8,128)(2,1)S(1)}, u32[]{:S(2)}, u32[]{:S(2)}) collective-permute-start(bf16[2,2,192,128]{3,2,1,0:T(8,128)(2,1)S(1)} %get-tuple-element.65), channel_id=1, source_target_pairs={{0,64},{1,65},{2,66},{3,67},{4,68},{5,69},{6,70},{7,71},{8,72},{9,... | collective-permute-start | bytes 589832 | tf_op jit(solution)/shard_map/ppermute | solution.py:62
  45.7 2.6 %collective-permute-start.12 = (bf16[2,2,192,128]{3,2,1,0:T(8,128)(2,1)S(1)}, bf16[2,2,192,128]{3,2,1,0:T(8,128)(2,1)S(1)}, u32[]{:S(2)}, u32[]{:S(2)}) collective-permute-start(bf16[2,2,192,128]{3,2,1,0:T(8,128)(2,1)S(1)} %get-tuple-element.67), channel_id=1, source_target_pairs={{0,96},{1,97},{2,98},{3,99},{4,100},{5,101},{6,102},{7,103},{8,104... | collective-permute-start | bytes 589832 | tf_op jit(solution)/shard_map/ppermute | solution.py:62
  48.5 0.9 %collective-permute-start.19 = (bf16[576,128]{1,0:T(8,128)(2,1)S(1)}, bf16[576,128]{1,0:T(8,128)(2,1)S(1)}, u32[]{:S(2)}, u32[]{:S(2)}) collective-permute-start(bf16[576,128]{1,0:T(8,128)(2,1)S(1)} %get-tuple-element.76), channel_id=1, source_target_pairs={{0,16},{1,17},{2,18},{3,19},{4,20},{5,21},{6,22},{7,23},{8,24},{9,... | collective-permute-start | bytes 442376 | tf_op jit(solution)/shard_map/ppermute | solution.py:62
  49.4 1.4 %collective-permute-start.20 = (bf16[576,128]{1,0:T(8,128)(2,1)S(1)}, bf16[576,128]{1,0:T(8,128)(2,1)S(1)}, u32[]{:S(2)}, u32[]{:S(2)}) collective-permute-start(bf16[576,128]{1,0:T(8,128)(2,1)S(1)} %get-tuple-element.77), channel_id=1, source_target_pairs={{0,2},{1,3},{2,16},{3,17},{4,6},{5,7},{6,20},{7,21},{8,10},{9,11},... | collective-permute-start | bytes 442376 | tf_op jit(solution)/shard_map/ppermute | solution.py:62
  51.2 1.4 %collective-permute-start.21 = (bf16[576,128]{1,0:T(8,128)(2,1)S(1)}, bf16[576,128]{1,0:T(8,128)(2,1)S(1)}, u32[]{:S(2)}, u32[]{:S(2)}) collective-permute-start(bf16[576,128]{1,0:T(8,128)(2,1)S(1)} %get-tuple-element.77), channel_id=1, source_target_pairs={{0,18},{1,19},{2,0},{3,1},{4,22},{5,23},{6,4},{7,5},{8,26},{9,27},... | collective-permute-start | bytes 442376 | tf_op jit(solution)/shard_map/ppermute | solution.py:62
  52.6 1.2 %collective-permute-done.11.p2 = bf16[2,2,192,128]{3,2,1,0:T(8,128)(2,1)S(1)} collective-permute-done((bf16[2,2,192,128]{3,2,1,0:T(8,128)(2,1)S(1)}, bf16[2,2,192,128]{3,2,1,0:T(8,128)(2,1)S(1)}, u32[]{:S(2)}, u32[]{:S(2)}) %collective-permute-start.11) | collective-permute-done | bytes 196640 | tf_op jit(solution)/shard_map/ppermute | solution.py:62
  54.2 0.9 %collective-permute-start.13 = (bf16[192,128]{1,0:T(8,128)(2,1)S(1)}, bf16[192,128]{1,0:T(8,128)(2,1)S(1)}, u32[]{:S(2)}, u32[]{:S(2)}) collective-permute-start(bf16[192,128]{1,0:T(8,128)(2,1)S(1)} %get-tuple-element.69), channel_id=1, source_target_pairs={{0,16},{1,17},{2,18},{3,19},{4,20},{5,21},{6,22},{7,23},{8,24},{9,... | collective-permute-start | bytes 147464 | tf_op jit(solution)/shard_map/ppermute | solution.py:62
  55.1 0.9 %collective-permute-done.19 = bf16[576,128]{1,0:T(8,128)(2,1)S(1)} collective-permute-done((bf16[576,128]{1,0:T(8,128)(2,1)S(1)}, bf16[576,128]{1,0:T(8,128)(2,1)S(1)}, u32[]{:S(2)}, u32[]{:S(2)}) %collective-permute-start.19) | collective-permute-done | bytes 147488 | tf_op jit(solution)/shard_map/ppermute | solution.py:62
  55.9 2.0 %collective-permute-start.15 = (bf16[192,128]{1,0:T(8,128)(2,1)S(1)}, bf16[192,128]{1,0:T(8,128)(2,1)S(1)}, u32[]{:S(2)}, u32[]{:S(2)}) collective-permute-start(bf16[192,128]{1,0:T(8,128)(2,1)S(1)} %get-tuple-element.71), channel_id=1, source_target_pairs={{0,17},{1,16},{2,19},{3,18},{4,21},{5,20},{6,23},{7,22},{8,25},{9,... | collective-permute-start | bytes 147464 | tf_op jit(solution)/shard_map/ppermute | solution.py:62
  58.0 2.3 %collective-permute-start.22 = (bf16[576,128]{1,0:T(8,128)(2,1)S(1)}, bf16[576,128]{1,0:T(8,128)(2,1)S(1)}, u32[]{:S(2)}, u32[]{:S(2)}) collective-permute-start(bf16[576,128]{1,0:T(8,128)(2,1)S(1)} %add_convert_fusion.1), channel_id=1, source_target_pairs={{0,64},{1,65},{2,66},{3,67},{4,68},{5,69},{6,70},{7,71},{8,72},{9,... | collective-permute-start | bytes 442376 | tf_op jit(solution)/shard_map/ppermute | solution.py:62
  60.2 1.4 %collective-permute-start.23 = (bf16[576,128]{1,0:T(8,128)(2,1)S(1)}, bf16[576,128]{1,0:T(8,128)(2,1)S(1)}, u32[]{:S(2)}, u32[]{:S(2)}) collective-permute-start(bf16[576,128]{1,0:T(8,128)(2,1)S(1)} %add_convert_fusion.1), channel_id=1, source_target_pairs={{0,32},{1,33},{2,34},{3,35},{4,36},{5,37},{6,38},{7,39},{8,40},{9,... | collective-permute-start | bytes 442376 | tf_op jit(solution)/shard_map/ppermute | solution.py:62
  61.6 1.9 %collective-permute-start.24 = (bf16[576,128]{1,0:T(8,128)(2,1)S(1)}, bf16[576,128]{1,0:T(8,128)(2,1)S(1)}, u32[]{:S(2)}, u32[]{:S(2)}) collective-permute-start(bf16[576,128]{1,0:T(8,128)(2,1)S(1)} %add_convert_fusion.1), channel_id=1, source_target_pairs={{0,96},{1,97},{2,98},{3,99},{4,100},{5,101},{6,102},{7,103},{8,104... | collective-permute-start | bytes 442376 | tf_op jit(solution)/shard_map/ppermute | solution.py:62
  64.1 2.1 %collective-permute-done.22 = bf16[576,128]{1,0:T(8,128)(2,1)S(1)} collective-permute-done((bf16[576,128]{1,0:T(8,128)(2,1)S(1)}, bf16[576,128]{1,0:T(8,128)(2,1)S(1)}, u32[]{:S(2)}, u32[]{:S(2)}) %collective-permute-start.22) | collective-permute-done | bytes 147488 | tf_op jit(solution)/shard_map/ppermute | solution.py:62
  66.3 2.2 %collective-permute-done.23 = bf16[576,128]{1,0:T(8,128)(2,1)S(1)} collective-permute-done((bf16[576,128]{1,0:T(8,128)(2,1)S(1)}, bf16[576,128]{1,0:T(8,128)(2,1)S(1)}, u32[]{:S(2)}, u32[]{:S(2)}) %collective-permute-start.23) | collective-permute-done | bytes 147488 | tf_op jit(solution)/shard_map/ppermute | solution.py:62
  68.5 0.7 %fusion.2 = bf16[128,576]{0,1:T(8,128)(2,1)} fusion(bf16[576,128]{1,0:T(8,128)(2,1)S(1)} %collective-permute-done.24, bf16[576,128]{1,0:T(8,128)(2,1)S(1)} %collective-permute-done.23, bf16[576,128]{1,0:T(8,128)(2,1)S(1)} %collective-permute-done.22, bf16[576,128]{1,0:T(8,128)(2,1)S(1)} %add_convert_fusion.1), kind=kLoop, calls=%fused_computation.6 | loop fusion | flops 589824 | bytes 737280 | tf_op jit(solution)/shard_map/transpose | solution.py:415
  (45 shorter events, 4.1 us)
Async XLA Ops:
  0.6 16.1 %copy-start.2 = (bf16[128,576]{0,1:T(8,128)(2,1)S(1)}, bf16[128,576]{0,1:T(8,128)(2,1)}, u32[]{:S(2)}) copy-start(bf16[128,576]{0,1:T(8,128)(2,1)} %param.9) | copy-start | bytes 442372
  0.6 16.1 %copy-start.1 = (s32[32]{0:T(128)S(1)}, s32[32]{0:T(128)}, u32[]{:S(2)}) copy-start(s32[32]{0:T(128)} %order.7) | copy-start | bytes 388
  0.7 8.2 %collective-permute-start = (bf16[128,4608]{1,0:T(8,128)(2,1)}, bf16[128,4608]{1,0:T(8,128)(2,1)S(1)}, u32[]{:S(2)}, u32[]{:S(2)}) collective-permute-start(bf16[128,4608]{1,0:T(8,128)(2,1)} %q0.1), channel_id=1, source_target_pairs={{0,1},{1,0},{2,3},{3,2},{4,5},{5,4},{6,7},{7,6},{8,9},{9,8},{10,11... | collective-permute-start | bytes 3538952 | tf_op jit(solution)/shard_map/ppermute | solution.py:62
  0.7 6.6 %collective-permute-start.1 = (bf16[128,1024]{1,0:T(8,128)(2,1)}, bf16[128,1024]{1,0:T(8,128)(2,1)S(1)}, u32[]{:S(2)}, u32[]{:S(2)}) collective-permute-start(bf16[128,1024]{1,0:T(8,128)(2,1)} %do0.1), channel_id=1, source_target_pairs={{0,1},{1,0},{2,3},{3,2},{4,5},{5,4},{6,7},{7,6},{8,9},{9,8},{10,11... | collective-permute-start | bytes 786440 | tf_op jit(solution)/shard_map/ppermute | solution.py:62
  1.2 10.8 %collective-permute-start.2 = (bf16[576,128]{1,0:T(8,128)(2,1)}, bf16[576,128]{1,0:T(8,128)(2,1)S(1)}, u32[]{:S(2)}, u32[]{:S(2)}) collective-permute-start(bf16[576,128]{1,0:T(8,128)(2,1)} %bitcast.16), channel_id=1, source_target_pairs={{0,4},{1,5},{2,6},{3,7},{4,8},{5,9},{6,10},{7,11},{8,12},{9,13},{1... | collective-permute-start | bytes 442376 | tf_op jit(solution)/shard_map/ppermute | solution.py:62
  3.2 10.4 %collective-permute-start.3 = (bf16[576,128]{1,0:T(8,128)(2,1)}, bf16[576,128]{1,0:T(8,128)(2,1)S(1)}, u32[]{:S(2)}, u32[]{:S(2)}) collective-permute-start(bf16[576,128]{1,0:T(8,128)(2,1)} %bitcast.17), channel_id=1, source_target_pairs={{0,12},{1,13},{2,14},{3,15},{4,0},{5,1},{6,2},{7,3},{8,4},{9,5},{1... | collective-permute-start | bytes 442376 | tf_op jit(solution)/shard_map/ppermute | solution.py:62
  5.4 10.0 %collective-permute-start.4 = (bf16[576,128]{1,0:T(8,128)(2,1)}, bf16[576,128]{1,0:T(8,128)(2,1)S(1)}, u32[]{:S(2)}, u32[]{:S(2)}) collective-permute-start(bf16[576,128]{1,0:T(8,128)(2,1)} %bitcast.18), channel_id=1, source_target_pairs={{0,8},{1,9},{2,10},{3,11},{4,12},{5,13},{6,14},{7,15},{8,0},{9,1},... | collective-permute-start | bytes 442376 | tf_op jit(solution)/shard_map/ppermute | solution.py:62
  7.3 15.7 %collective-permute-start.7 = (bf16[576,128]{1,0:T(8,128)(2,1)}, bf16[576,128]{1,0:T(8,128)(2,1)S(1)}, u32[]{:S(2)}, u32[]{:S(2)}) collective-permute-start(bf16[576,128]{1,0:T(8,128)(2,1)} %bitcast.19), channel_id=1, source_target_pairs={{0,2},{1,3},{2,16},{3,17},{4,6},{5,7},{6,20},{7,21},{8,10},{9,11},... | collective-permute-start | bytes 442376 | tf_op jit(solution)/shard_map/ppermute | solution.py:62
  12.1 8.6 %collective-permute-start.5 = (bf16[576,128]{1,0:T(8,128)(2,1)S(1)}, bf16[576,128]{1,0:T(8,128)(2,1)S(1)}, u32[]{:S(2)}, u32[]{:S(2)}) collective-permute-start(bf16[576,128]{1,0:T(8,128)(2,1)S(1)} %collective-permute-done.2.refs_0_), channel_id=1, source_target_pairs={{0,2},{1,3},{2,16},{3,17},{4,6},{5,7},{6,20},{7,21},{8,10},{9,11},... | collective-permute-start | bytes 442376 | tf_op jit(solution)/shard_map/ppermute | solution.py:62
  13.6 7.1 %collective-permute-start.6 = (bf16[576,128]{1,0:T(8,128)(2,1)S(1)}, bf16[576,128]{1,0:T(8,128)(2,1)S(1)}, u32[]{:S(2)}, u32[]{:S(2)}) collective-permute-start(bf16[576,128]{1,0:T(8,128)(2,1)S(1)} %collective-permute-done.3.refs_1_), channel_id=1, source_target_pairs={{0,18},{1,19},{2,0},{3,1},{4,22},{5,23},{6,4},{7,5},{8,26},{9,27},... | collective-permute-start | bytes 442376 | tf_op jit(solution)/shard_map/ppermute | solution.py:62
  15.4 7.7 %collective-permute-start.8 = (bf16[576,128]{1,0:T(8,128)(2,1)S(1)}, bf16[576,128]{1,0:T(8,128)(2,1)S(1)}, u32[]{:S(2)}, u32[]{:S(2)}) collective-permute-start(bf16[576,128]{1,0:T(8,128)(2,1)S(1)} %collective-permute-done.4.refs_3_), channel_id=1, source_target_pairs={{0,18},{1,19},{2,0},{3,1},{4,22},{5,23},{6,4},{7,5},{8,26},{9,27},... | collective-permute-start | bytes 442376 | tf_op jit(solution)/shard_map/ppermute | solution.py:62
  25.4 1.5 %collective-permute-start.9 = (f32[8,2048]{1,0:T(8,128)S(1)}, f32[8,2048]{1,0:T(8,128)S(1)}, u32[]{:S(2)}, u32[]{:S(2)}) collective-permute-start(f32[8,2048]{1,0:T(8,128)S(1)} %get-tuple-element.53.refs_6_), channel_id=1, source_target_pairs={{0,1},{1,0},{2,3},{3,2},{4,5},{5,4},{6,7},{7,6},{8,9},{9,8},{10,11... | collective-permute-start | bytes 196616 | tf_op jit(solution)/shard_map/ppermute | solution.py:62
  29.5 16.2 %collective-permute-start.18 = (bf16[2,576,128]{2,1,0:T(8,128)(2,1)S(1)}, bf16[2,576,128]{2,1,0:T(8,128)(2,1)S(1)}, u32[]{:S(2)}, u32[]{:S(2)}) collective-permute-start(bf16[2,576,128]{2,1,0:T(8,128)(2,1)S(1)} %get-tuple-element.75), channel_id=1, source_target_pairs={{0,8},{1,9},{2,10},{3,11},{4,12},{5,13},{6,14},{7,15},{8,0},{9,1},... | collective-permute-start | bytes 884744 | tf_op jit(solution)/shard_map/ppermute | solution.py:62
  32.0 4.8 %slice-start = ((s8[4718592]{0:T(1024)(128)(4,1)}), s8[4194304]{0:T(1024)(128)(4,1)S(1)}, s32[]{:S(2)}) async-start(s8[4718592]{0:T(1024)(128)(4,1)} %bitcast.14), calls=%async_computation | async-start | bytes 8388608
  32.1 4.7 %copy-start.3 = (f32[32]{0:T(128)S(1)}, f32[32]{0:T(128)}, u32[]{:S(2)}) copy-start(f32[32]{0:T(128)} %constant.21.clone) | copy-start | bytes 388
  32.1 4.8 %slice-start.1 = ((s8[4718592]{0:T(1024)(128)(4,1)}), s8[524288]{0:T(1024)(128)(4,1)S(1)}, s32[]{:S(2)}) async-start(s8[4718592]{0:T(1024)(128)(4,1)} %bitcast.14), calls=%async_computation.1 | async-start | bytes 1048576
  32.1 4.8 %copy-start = (bf16[8,128,512]{2,1,0:T(8,128)(2,1)S(1)}, bf16[8,128,512]{2,1,0:T(8,128)(2,1)}, u32[]{:S(2)}) copy-start(bf16[8,128,512]{2,1,0:T(8,128)(2,1)} %uk.1) | copy-start | bytes 3145732
  34.7 13.6 %collective-permute-start.16 = (bf16[2,576,128]{2,1,0:T(8,128)(2,1)S(1)}, bf16[2,576,128]{2,1,0:T(8,128)(2,1)S(1)}, u32[]{:S(2)}, u32[]{:S(2)}) collective-permute-start(bf16[2,576,128]{2,1,0:T(8,128)(2,1)S(1)} %get-tuple-element.73), channel_id=1, source_target_pairs={{0,12},{1,13},{2,14},{3,15},{4,0},{5,1},{6,2},{7,3},{8,4},{9,5},{1... | collective-permute-start | bytes 884744 | tf_op jit(solution)/shard_map/ppermute | solution.py:62
  36.1 12.2 %collective-permute-start.17 = (bf16[2,576,128]{2,1,0:T(8,128)(2,1)S(1)}, bf16[2,576,128]{2,1,0:T(8,128)(2,1)S(1)}, u32[]{:S(2)}, u32[]{:S(2)}) collective-permute-start(bf16[2,576,128]{2,1,0:T(8,128)(2,1)S(1)} %get-tuple-element.74), channel_id=1, source_target_pairs={{0,4},{1,5},{2,6},{3,7},{4,8},{5,9},{6,10},{7,11},{8,12},{9,13},{1... | collective-permute-start | bytes 884744 | tf_op jit(solution)/shard_map/ppermute | solution.py:62
  41.8 9.4 %collective-permute-start.10 = (bf16[2,2,192,128]{3,2,1,0:T(8,128)(2,1)S(1)}, bf16[2,2,192,128]{3,2,1,0:T(8,128)(2,1)S(1)}, u32[]{:S(2)}, u32[]{:S(2)}) collective-permute-start(bf16[2,2,192,128]{3,2,1,0:T(8,128)(2,1)S(1)} %get-tuple-element.65), channel_id=1, source_target_pairs={{0,64},{1,65},{2,66},{3,67},{4,68},{5,69},{6,70},{7,71},{8,72},{9,... | collective-permute-start | bytes 589832 | tf_op jit(solution)/shard_map/ppermute | solution.py:62
  45.1 8.7 %collective-permute-start.11 = (bf16[2,2,192,128]{3,2,1,0:T(8,128)(2,1)S(1)}, bf16[2,2,192,128]{3,2,1,0:T(8,128)(2,1)S(1)}, u32[]{:S(2)}, u32[]{:S(2)}) collective-permute-start(bf16[2,2,192,128]{3,2,1,0:T(8,128)(2,1)S(1)} %get-tuple-element.66), channel_id=1, source_target_pairs={{0,32},{1,33},{2,34},{3,35},{4,36},{5,37},{6,38},{7,39},{8,40},{9,... | collective-permute-start | bytes 589832 | tf_op jit(solution)/shard_map/ppermute | solution.py:62
  45.7 8.3 %collective-permute-start.12 = (bf16[2,2,192,128]{3,2,1,0:T(8,128)(2,1)S(1)}, bf16[2,2,192,128]{3,2,1,0:T(8,128)(2,1)S(1)}, u32[]{:S(2)}, u32[]{:S(2)}) collective-permute-start(bf16[2,2,192,128]{3,2,1,0:T(8,128)(2,1)S(1)} %get-tuple-element.67), channel_id=1, source_target_pairs={{0,96},{1,97},{2,98},{3,99},{4,100},{5,101},{6,102},{7,103},{8,104... | collective-permute-start | bytes 589832 | tf_op jit(solution)/shard_map/ppermute | solution.py:62
  48.5 7.5 %collective-permute-start.19 = (bf16[576,128]{1,0:T(8,128)(2,1)S(1)}, bf16[576,128]{1,0:T(8,128)(2,1)S(1)}, u32[]{:S(2)}, u32[]{:S(2)}) collective-permute-start(bf16[576,128]{1,0:T(8,128)(2,1)S(1)} %get-tuple-element.76), channel_id=1, source_target_pairs={{0,16},{1,17},{2,18},{3,19},{4,20},{5,21},{6,22},{7,23},{8,24},{9,... | collective-permute-start | bytes 442376 | tf_op jit(solution)/shard_map/ppermute | solution.py:62
  49.4 8.5 %collective-permute-start.20 = (bf16[576,128]{1,0:T(8,128)(2,1)S(1)}, bf16[576,128]{1,0:T(8,128)(2,1)S(1)}, u32[]{:S(2)}, u32[]{:S(2)}) collective-permute-start(bf16[576,128]{1,0:T(8,128)(2,1)S(1)} %get-tuple-element.77), channel_id=1, source_target_pairs={{0,2},{1,3},{2,16},{3,17},{4,6},{5,7},{6,20},{7,21},{8,10},{9,11},... | collective-permute-start | bytes 442376 | tf_op jit(solution)/shard_map/ppermute | solution.py:62
  51.2 6.7 %collective-permute-start.21 = (bf16[576,128]{1,0:T(8,128)(2,1)S(1)}, bf16[576,128]{1,0:T(8,128)(2,1)S(1)}, u32[]{:S(2)}, u32[]{:S(2)}) collective-permute-start(bf16[576,128]{1,0:T(8,128)(2,1)S(1)} %get-tuple-element.77), channel_id=1, source_target_pairs={{0,18},{1,19},{2,0},{3,1},{4,22},{5,23},{6,4},{7,5},{8,26},{9,27},... | collective-permute-start | bytes 442376 | tf_op jit(solution)/shard_map/ppermute | solution.py:62
  54.2 7.5 %collective-permute-start.13 = (bf16[192,128]{1,0:T(8,128)(2,1)S(1)}, bf16[192,128]{1,0:T(8,128)(2,1)S(1)}, u32[]{:S(2)}, u32[]{:S(2)}) collective-permute-start(bf16[192,128]{1,0:T(8,128)(2,1)S(1)} %get-tuple-element.69), channel_id=1, source_target_pairs={{0,16},{1,17},{2,18},{3,19},{4,20},{5,21},{6,22},{7,23},{8,24},{9,... | collective-permute-start | bytes 147464 | tf_op jit(solution)/shard_map/ppermute | solution.py:62
  55.1 8.4 %collective-permute-start.14 = (bf16[192,128]{1,0:T(8,128)(2,1)S(1)}, bf16[192,128]{1,0:T(8,128)(2,1)S(1)}, u32[]{:S(2)}, u32[]{:S(2)}) collective-permute-start(bf16[192,128]{1,0:T(8,128)(2,1)S(1)} %get-tuple-element.70), channel_id=1, source_target_pairs={{0,1},{1,0},{2,3},{3,2},{4,5},{5,4},{6,7},{7,6},{8,9},{9,8},{10,11... | collective-permute-start | bytes 147464 | tf_op jit(solution)/shard_map/ppermute | solution.py:62
  55.9 7.5 %collective-permute-start.15 = (bf16[192,128]{1,0:T(8,128)(2,1)S(1)}, bf16[192,128]{1,0:T(8,128)(2,1)S(1)}, u32[]{:S(2)}, u32[]{:S(2)}) collective-permute-start(bf16[192,128]{1,0:T(8,128)(2,1)S(1)} %get-tuple-element.71), channel_id=1, source_target_pairs={{0,17},{1,16},{2,19},{3,18},{4,21},{5,20},{6,23},{7,22},{8,25},{9,... | collective-permute-start | bytes 147464 | tf_op jit(solution)/shard_map/ppermute | solution.py:62
  58.0 8.3 %collective-permute-start.22 = (bf16[576,128]{1,0:T(8,128)(2,1)S(1)}, bf16[576,128]{1,0:T(8,128)(2,1)S(1)}, u32[]{:S(2)}, u32[]{:S(2)}) collective-permute-start(bf16[576,128]{1,0:T(8,128)(2,1)S(1)} %add_convert_fusion.1), channel_id=1, source_target_pairs={{0,64},{1,65},{2,66},{3,67},{4,68},{5,69},{6,70},{7,71},{8,72},{9,... | collective-permute-start | bytes 442376 | tf_op jit(solution)/shard_map/ppermute | solution.py:62
  60.2 8.2 %collective-permute-start.23 = (bf16[576,128]{1,0:T(8,128)(2,1)S(1)}, bf16[576,128]{1,0:T(8,128)(2,1)S(1)}, u32[]{:S(2)}, u32[]{:S(2)}) collective-permute-start(bf16[576,128]{1,0:T(8,128)(2,1)S(1)} %add_convert_fusion.1), channel_id=1, source_target_pairs={{0,32},{1,33},{2,34},{3,35},{4,36},{5,37},{6,38},{7,39},{8,40},{9,... | collective-permute-start | bytes 442376 | tf_op jit(solution)/shard_map/ppermute | solution.py:62
  61.6 6.9 %collective-permute-start.24 = (bf16[576,128]{1,0:T(8,128)(2,1)S(1)}, bf16[576,128]{1,0:T(8,128)(2,1)S(1)}, u32[]{:S(2)}, u32[]{:S(2)}) collective-permute-start(bf16[576,128]{1,0:T(8,128)(2,1)S(1)} %add_convert_fusion.1), channel_id=1, source_target_pairs={{0,96},{1,97},{2,98},{3,99},{4,100},{5,101},{6,102},{7,103},{8,104... | collective-permute-start | bytes 442376 | tf_op jit(solution)/shard_map/ppermute | solution.py:62
